TPU v7x, 32 devices: a whole 2x2x4 slice. The times are simulated.
32 devices in a mesh: tower: 4 (over y, core), dev: 8 (over z, x).
Axes of the slice: x: 2, y: 2, z: 4, core: 2. Of those that a mesh axis runs over, the one named last changes fastest.
Arguments:
- bag_ids: int32 [4, 1024, 32, 4], P('tower', None, 'dev'), may hold values from 0 to 1023
- bag_lengths: int32 [4, 1024, 32], P('tower', None, 'dev'), may hold values from 1 to 4
- tables: bfloat16 [4, 32, 1024, 128], P('tower', 'dev'), may hold values from -3 to 3
- cross_down: bfloat16 [4, 1, 4096, 512], P('tower'), may hold values from -0.09375 to 0.09375
- cross_up: bfloat16 [4, 1, 512, 4096], P('tower'), may hold values from -0.25 to 0.25
- cross_bias: float32 [4, 1, 4096], P('tower'), may hold values from -4 to 4
- proj_weight: bfloat16 [4, 4096, 512], P('tower'), may hold values from -0.09375 to 0.09375
- proj_bias: float32 [4, 512], P('tower'), may hold values from -3 to 3
Outputs:
- interactions: float32 [1024, 6], P(('tower', 'dev'))
Inputs may be any that keep to these rules, and one draw needn't show every extreme that they name: `bag_ids`: where table rows travel between devices, each is sent as a whole 32-bit integer, one to a slot; a program may not pack several table rows into one word. `bag_lengths`: where bag lengths travel between devices, a program may pack several of them into one word.
All inputs are finite; a program needn't handle non-finite values.
Results may differ from a plain program's by a relative error of at most 0.0071.
Values may be sent and summed in bfloat16 or wider, within the bound.
No kernel may reach another device: no remote copies, remote signals or barrier semaphores. Data moves between devices by JAX's collectives and lax.ppermute only.
A program may use at most 128 MiB of HBM per device.

v0:
```python
import jax
import jax.numpy as jnp
import numpy as np
from jax import lax
from jax.sharding import PartitionSpec as P

EMB = 128
OUT = 512


def pool_rows(tables_one, ids_one, lengths_one):
    table_rows = tables_one.shape[1]
    positions = lax.iota(jnp.int32, table_rows)
    counts = jnp.zeros(ids_one.shape[:2] + (table_rows,), jnp.bfloat16)
    for slot_index in range(ids_one.shape[2]):
        matched = (ids_one[:, :, slot_index, None] == positions) & (slot_index < lengths_one)[
            :, :, None
        ]
        counts = counts + matched.astype(jnp.bfloat16)
    summed = jnp.einsum("sft,ftd->sfd", counts, tables_one, preferred_element_type=jnp.float32)
    return summed.astype(jnp.bfloat16)


def tower_forward(base, down, up, bias, proj, proj_b):
    base_f = base.astype(jnp.float32)
    cross = base
    low = jnp.dot(cross, down[0], preferred_element_type=jnp.float32).astype(jnp.bfloat16)
    high = jnp.dot(low, up[0], preferred_element_type=jnp.float32) + bias[0]
    cross = (base_f * high + cross.astype(jnp.float32)).astype(jnp.bfloat16)
    return (jnp.dot(cross, proj, preferred_element_type=jnp.float32) + proj_b).astype(jnp.bfloat16)


def local(bag_ids, bag_lengths, tables, cross_down, cross_up, cross_bias, proj_weight, proj_bias):
    towers = lax.axis_size("tower")
    members = lax.axis_size("dev")
    samples = bag_ids.shape[1]
    block = samples // (towers * members)
    feat_dev = bag_ids.shape[2]
    weights = (cross_down[0], cross_up[0], cross_bias[0], proj_weight[0], proj_bias[0])
    pooled = pool_rows(tables[0], bag_ids[0], bag_lengths[0])
    pooled = pooled.reshape(towers, members, block, feat_dev, EMB)
    pooled_block = lax.all_to_all(pooled, "dev", split_axis=1, concat_axis=3, tiled=True)
    count = pooled_block.shape[2]
    rows = pooled_block.reshape(towers * count, -1)
    outputs = tower_forward(rows, *weights).reshape(towers, count, -1)
    gathered = lax.all_to_all(outputs, "tower", split_axis=0, concat_axis=0, tiled=True)
    gram = jnp.einsum(
        "isk,jsk->sij", gathered, gathered, preferred_element_type=jnp.float32
    ) / jnp.sqrt(jnp.float32(OUT))
    upper, lower = np.triu_indices(towers, 1)
    return gram[:, upper, lower]


def solution(mesh):
    placed = (
        P("tower", None, "dev", None),
        P("tower", None, "dev"),
        P("tower", "dev", None, None),
        P("tower", None, None, None),
        P("tower", None, None, None),
        P("tower", None, None),
        P("tower", None, None),
        P("tower", None),
    )
    return jax.shard_map(
        local, mesh=mesh, in_specs=placed, out_specs=P(("tower", "dev"), None), check_vma=False
    )
```

profile of v0, /device:TPU:0, one launch (start us, length us, event | category | flops | bytes accessed | tf_op | source)
XLA Modules:
  0.0 72.1 jit_solution(12589742832766468581)
XLA Ops:
  0.0 0.0 copy-start
  0.0 0.8 %compare_bitcast_fusion.3 = (pred[1024,4]{0,1:T(4,128)(4,1)S(1)}, pred[1024,4]{0,1:T(4,128)(4,1)S(1)}, pred[1024,4]{0,1:T(4,128)(4,1)S(1)}, pred[1024,4]{0,1:T(4,128)(4,1)S(1)}) fusion(s32[1,1024,4]{1,2,0:T(4,128)} %param.13), kind=kLoop, calls=%fused_computation.48 | loop fusion | flops 16384 | bytes 32768 | tf_op jit(solution)/shard_map/gt | solution.py:16
  0.8 1.1 %fusion.48 = (s32[1024,4,1]{0,2,1:T(1,128)S(1)}, s32[1024,4,1]{0,2,1:T(1,128)S(1)}, s32[1024,4,1]{0,2,1:T(1,128)S(1)}, s32[1024,4,1]{0,2,1:T(1,128)S(1)}) fusion(s32[1024,4,4]{0,2,1:T(4,128)} %bitcast.54), kind=kLoop, calls=%fused_computation.49 | loop fusion | bytes 131072 | tf_op jit(solution)/shard_map/slice | solution.py:16
  1.9 0.0 copy-done
  1.9 18.4 %fusion.32 = bf16[4,1024,128]{2,1,0:T(8,128)(2,1)S(1)} fusion(s32[1024,4]{0,1:T(4,128)S(1)} %get-tuple-element.13, s32[1024,4]{0,1:T(4,128)S(1)} %get-tuple-element.14, s32[1024,4]{0,1:T(4,128)S(1)} %get-tuple-element.15, s32[1024,4]{0,1:T(4,128)S(1)} %get-tuple-element.16, pred[1024,4]{0,1:T(4,128)(4,1)S(1)} %get-tuple-element.11, ...), kind=kOutput, calls=%fused_computation.34 | convolution fusion | flops 1158152192 | bytes 2179072 | tf_op jit(solution)/shard_map/sft,ftd->sfd/dot_general | solution.py:20
  20.4 0.0 copy-start.2
  20.4 0.8 %copy.18 = bf16[4,8,32,4,128]{4,3,2,0,1:T(4,128)(2,1)S(1)} copy(bf16[4,8,32,4,128]{4,2,1,0,3:T(8,128)(2,1)S(1)} %bitcast.52) | data formatting | bytes 2097152 | tf_op jit(solution)/shard_map/reshape | solution.py:41
  21.2 32.8 %all_to_all.20 = bf16[4,8,32,4,128]{4,3,2,0,1:T(4,128)(2,1)S(1)} all-to-all(bf16[4,8,32,4,128]{4,3,2,0,1:T(4,128)(2,1)S(1)} %copy.18), channel_id=1, replica_groups=mesh['tower'=4,'dev'=8] {'dev'}, dimensions={1} | all-to-all | bytes 2097152 | tf_op jit(solution)/shard_map/all_to_all | solution.py:42
  54.0 0.4 copy.19
  54.4 0.8 %reshape.40 = bf16[128,4096]{1,0:T(8,128)(2,1)S(1)} reshape(bf16[4,1,32,8,4,128]{5,4,3,2,0,1:T(4,128)(2,1)S(1)} %copy.19) | data formatting | bytes 2097152 | tf_op jit(solution)/shard_map/reshape | solution.py:44
  55.3 0.0 copy-done.2
  55.3 0.0 copy-start.3
  55.3 5.1 %fusion.26 = bf16[128,4096]{1,0:T(8,128)(2,1)S(1)} fusion(bf16[1,1,512,4096]{3,2,1,0:T(8,128)(2,1)} %param.16, bf16[128,4096]{1,0:T(8,128)(2,1)S(1)} %reshape.40, f32[4096]{0:T(1024)S(1)} %bitcast.55, bf16[1,1,4096,512]{3,2,1,0:T(8,128)(2,1)} %param.15), kind=kOutput, calls=%fused_computation.28 | convolution fusion | flops 1076428800 | bytes 10502144 | tf_op jit(solution)/shard_map/dot_general | solution.py:28
  60.4 0.0 copy-start.1
  60.4 0.0 copy-done.3
  60.4 2.9 %fusion.41 = bf16[128,512]{1,0:T(8,128)(2,1)S(1)} fusion(bf16[128,4096]{1,0:T(8,128)(2,1)S(1)} %fusion.26, bf16[1,4096,512]{2,1,0:T(8,128)(2,1)} %param.18, f32[512]{0:T(512)S(1)} %bitcast.56), kind=kOutput, calls=%fused_computation.37 | convolution fusion | flops 537001984 | bytes 5376000 | tf_op jit(solution)/shard_map/dot_general | solution.py:30
  63.4 7.2 %all_to_all.21 = bf16[4,32,512]{2,1,0:T(8,128)(2,1)S(1)} all-to-all(bf16[4,32,512]{2,1,0:T(8,128)(2,1)S(1)} %bitcast.53), channel_id=1, replica_groups=mesh['tower'=4,'dev'=8] {'tower'}, dimensions={0} | all-to-all | bytes 262144 | tf_op jit(solution)/shard_map/all_to_all | solution.py:46
  70.6 0.2 convolution_multiply_fusion
  70.8 0.1 copy.22
  70.9 0.0 copy-done.1
  70.9 1.2 %gather_fusion = f32[6,32]{1,0:T(8,128)} fusion(f32[32,4,4]{0,2,1:T(4,128)S(1)} %copy.22, s32[6]{0:T(128)S(1)} %copy-done.1), kind=kCustom, calls=%fused_computation | custom fusion | bytes 1584 | tf_op jit(solution)/shard_map/gather | solution.py:51
  (2 shorter events, 0.0 us)
Async XLA Ops:
  0.0 1.9 %copy-start = (bf16[1,4,1024,128]{3,2,1,0:T(8,128)(2,1)S(1)}, bf16[1,4,1024,128]{3,2,1,0:T(8,128)(2,1)}, u32[]{:S(2)}) copy-start(bf16[1,4,1024,128]{3,2,1,0:T(8,128)(2,1)} %param.14) | copy-start | bytes 3145732
  20.4 34.9 %copy-start.2 = (f32[1,1,4096]{2,1,0:T(1,128)S(1)}, f32[1,1,4096]{2,1,0:T(1,128)}, u32[]{:S(2)}) copy-start(f32[1,1,4096]{2,1,0:T(1,128)} %param.17) | copy-start | bytes 49156
  55.3 5.2 %copy-start.3 = (f32[1,512]{1,0:T(1,128)S(1)}, f32[1,512]{1,0:T(1,128)}, u32[]{:S(2)}) copy-start(f32[1,512]{1,0:T(1,128)} %param.19) | copy-start | bytes 6148
  60.4 10.5 %copy-start.1 = (s32[6]{0:T(128)S(1)}, s32[6]{0:T(128)}, u32[]{:S(2)}) copy-start(s32[6]{0:T(128)} %constant.53) | copy-start | bytes 76
where the time goes:
time: 72.4 us; the launch traced here: 72.1 us
  blocking collectives  40 us (55%)
  matrix products  26.7 us (37%)
  local copies, waits for them, and re-layouts  4.44 us (6%)
  other arithmetic  0.83 us (1%)
    all_to_all x1, blocking collectives, local(): lax.all_to_all(pooled, 'dev', split_axis=1, concat_axis=3, tiled=True)  32.8 us
    dot_general x1, matrix products, pool_rows(): jnp.einsum('sft,ftd->sfd', counts, tables_one, preferred_element_type=jnp...  18.4 us
    all_to_all x1, blocking collectives, local(): lax.all_to_all(outputs, 'tower', split_axis=0, concat_axis=0, tiled=True)  7.23 us
    dot_general x1, matrix products, tower_forward(): high = jnp.dot(low, up[0], preferred_element_type=jnp.float32) + bias[0]  5.12 us
    dot_general x1, matrix products, tower_forward(): jnp.dot(cross, proj, preferred_element_type=jnp.float32) + proj_b  2.91 us

commit v1 on v0

v1 whole, which is shorter than its diff:
```python
import functools

import jax
import jax.numpy as jnp
import numpy as np
from jax import lax
from jax.experimental import pallas as pl
from jax.experimental.pallas import tpu as pltpu
from jax.sharding import PartitionSpec as P

LANES = 128
MIB = 1 << 20


def pool_kernel(block, feats, slots, me_ref, ids_ref, len_ref, tab_ref, after_ref, *rest):
    outs, scratch = rest[:-1], rest[-1]
    per = len(outs)
    rows = tab_ref.shape[1]
    lens = len_ref[...]
    stack = []
    for f in range(feats):
        ids = ids_ref[f]
        slot = lax.broadcasted_iota(jnp.int32, ids.shape, 0)
        ids = jnp.where(slot < lens[f : f + 1], ids, -1)
        times = jnp.zeros(ids.shape, jnp.float32)
        for p in range(slots):
            times += jnp.where(ids == ids[p : p + 1], 1.0, 0.0)
        stack += [ids.astype(jnp.float32), times]
    stack = jnp.concatenate(stack, axis=0)
    pad = -stack.shape[0] % LANES
    if pad:
        stack = jnp.concatenate([stack, jnp.zeros((pad, LANES), jnp.float32)], axis=0)
    cols = stack.T
    place = lax.broadcasted_iota(jnp.int16, (LANES, rows), 1)
    for f in range(feats):
        counts = jnp.zeros((LANES, rows), jnp.bfloat16)
        for p in range(slots):
            c = 2 * slots * f + p
            own = cols[:, c : c + 1].astype(jnp.int32).astype(jnp.int16)
            times = cols[:, c + slots : c + slots + 1].astype(jnp.bfloat16)
            counts = jnp.where(place == own, times, counts)
        total = jnp.dot(counts, tab_ref[f], preferred_element_type=jnp.float32)
        scratch[:, f * LANES : (f + 1) * LANES] = total.astype(jnp.bfloat16)
    low = lax.rem(me_ref[0], per)
    for k in range(per):
        start = pl.multiple_of((low ^ k) * block, block)
        outs[k][...] = scratch[pl.ds(start, block), :]


def pool_group(me, ids, lens, tables, after, group, towers, members, block):
    feats, slots, samples = ids.shape
    width = tables.shape[2]
    per = LANES // block
    groups = members // per

    def tile(t, me_ref):
        return t * groups + (me_ref[0] // per ^ group)

    shape = jax.ShapeDtypeStruct((towers * block, feats * width), jnp.bfloat16)
    return pl.pallas_call(
        functools.partial(pool_kernel, block, feats, slots),
        grid_spec=pltpu.PrefetchScalarGridSpec(
            num_scalar_prefetch=1,
            grid=(towers,),
            in_specs=[
                pl.BlockSpec((feats, slots, LANES), lambda t, m: (0, 0, tile(t, m))),
                pl.BlockSpec((feats, LANES), lambda t, m: (0, tile(t, m))),
                pl.BlockSpec(tables.shape, lambda t, m: (0, 0, 0)),
                pl.BlockSpec(memory_space=pl.ANY),
            ],
            out_specs=[pl.BlockSpec((block, feats * width), lambda t, m: (t, 0))] * per,
            scratch_shapes=[pltpu.VMEM((LANES, feats * width), jnp.bfloat16)],
        ),
        out_shape=[shape] * per,
        compiler_params=pltpu.CompilerParams(vmem_limit_bytes=24 * MIB),
        cost_estimate=pl.CostEstimate(
            flops=2 * towers * LANES * feats * tables.shape[1] * width * 8,
            bytes_accessed=tables.size * 2,
            transcendentals=0,
        ),
        name="pool_group",
    )(me, ids, lens, tables, after)


def low_kernel(order, me_ref, down_ref, *rest):
    chunks, out_ref = rest[:-1], rest[-1]
    depth = chunks[0].shape[1]
    total = None
    for k, chunk in zip(order, chunks, strict=True):
        start = pl.multiple_of((me_ref[0] ^ k) * depth, depth)
        part = jnp.dot(
            chunk[...], down_ref[pl.ds(start, depth), :], preferred_element_type=jnp.float32
        )
        total = part if total is None else total + part
    out_ref[...] = total


def low_part(me, down, chunks, order):
    rows = chunks[0].shape[0]
    return pl.pallas_call(
        functools.partial(low_kernel, order),
        in_specs=[pl.BlockSpec(memory_space=pltpu.SMEM)]
        + [pl.BlockSpec(memory_space=pltpu.VMEM)] * (1 + len(chunks)),
        out_specs=pl.BlockSpec(memory_space=pltpu.VMEM),
        out_shape=jax.ShapeDtypeStruct((rows, down.shape[1]), jnp.float32),
        compiler_params=pltpu.CompilerParams(vmem_limit_bytes=24 * MIB),
        cost_estimate=pl.CostEstimate(
            flops=2 * rows * chunks[0].shape[1] * len(chunks) * down.shape[1],
            bytes_accessed=down.size * 2,
            transcendentals=0,
        ),
        name="low_part",
    )(me, down, *chunks)


def tower_kernel(near, far, me_ref, low_ref, down_ref, up_ref, bias_ref, proj_ref, pb_ref, *rest):
    chunks, outs, scratch = rest[: len(near) + len(far)], rest[len(near) + len(far) : -1], rest[-1]
    depth = chunks[0].shape[1]
    block = outs[0].shape[0]
    order = near + far

    def place(k):
        return pl.ds(pl.multiple_of((me_ref[0] ^ k) * depth, depth), depth)

    low = low_ref[...]
    for k, chunk in list(zip(order, chunks, strict=True))[len(near) :]:
        low += jnp.dot(chunk[...], down_ref[place(k), :], preferred_element_type=jnp.float32)
    low = low.astype(jnp.bfloat16)
    total = pb_ref[...]
    for k, chunk in zip(order, chunks, strict=True):
        high = jnp.dot(low, up_ref[:, place(k)], preferred_element_type=jnp.float32)
        high = high + bias_ref[:, place(k)]
        base = chunk[...].astype(jnp.float32)
        cross = (base * high + base).astype(jnp.bfloat16)
        total = total + jnp.dot(cross, proj_ref[place(k), :], preferred_element_type=jnp.float32)
    scratch[...] = total.astype(jnp.bfloat16)
    for k, out in enumerate(outs):
        out[...] = scratch[pl.ds(pl.multiple_of((me_ref[1] ^ k) * block, block), block), :]


def tower_out(me, low, down, up, bias, proj, pb, chunks, near, far, towers):
    rows = chunks[0].shape[0]
    shape = jax.ShapeDtypeStruct((rows // towers, proj.shape[1]), jnp.bfloat16)
    return pl.pallas_call(
        functools.partial(tower_kernel, near, far),
        in_specs=[pl.BlockSpec(memory_space=pltpu.SMEM)]
        + [pl.BlockSpec(memory_space=pltpu.VMEM)] * (6 + len(chunks)),
        out_specs=[pl.BlockSpec(memory_space=pltpu.VMEM)] * towers,
        out_shape=[shape] * towers,
        scratch_shapes=[pltpu.VMEM((rows, proj.shape[1]), jnp.bfloat16)],
        compiler_params=pltpu.CompilerParams(vmem_limit_bytes=32 * MIB),
        cost_estimate=pl.CostEstimate(
            flops=4 * rows * proj.size, bytes_accessed=proj.size * 4, transcendentals=0
        ),
        name="tower_out",
    )(me, low, down, up, bias, proj, pb, *chunks)


def gram_kernel(me_ref, *rest):
    chunks, out_ref, rows_ref = rest[:-2], rest[-2], rest[-1]
    towers, (block, width) = len(chunks), chunks[0].shape
    for k, chunk in enumerate(chunks):
        rows_ref[me_ref[1] ^ k] = chunk[...]
    rows = rows_ref[...].reshape(towers * block, width)
    gram = lax.dot_general(
        rows, rows, (((1,), (1,)), ((), ())), preferred_element_type=jnp.float32
    ) * (1.0 / np.sqrt(np.float32(width)))
    n = towers * block
    at = lax.broadcasted_iota(jnp.int32, (block, n), 0)
    to = lax.broadcasted_iota(jnp.int32, (block, n), 1)
    own = at == lax.rem(to, block)
    place = 0
    for i in range(towers):
        picked = jnp.where(own, gram[i * block : (i + 1) * block], 0.0)
        line = jnp.sum(picked, axis=0, keepdims=True)
        for j in range(i + 1, towers):
            out_ref[place : place + 1, :] = line[:, j * block : (j + 1) * block]
            place += 1


def gram_pairs(me, chunks):
    towers, (block, width) = len(chunks), chunks[0].shape
    pairs = towers * (towers - 1) // 2
    return pl.pallas_call(
        gram_kernel,
        in_specs=[pl.BlockSpec(memory_space=pltpu.SMEM)]
        + [pl.BlockSpec(memory_space=pltpu.VMEM)] * towers,
        out_specs=pl.BlockSpec(memory_space=pltpu.VMEM),
        out_shape=jax.ShapeDtypeStruct((pairs, block), jnp.float32),
        scratch_shapes=[pltpu.VMEM((towers, block, width), jnp.bfloat16)],
        compiler_params=pltpu.CompilerParams(vmem_limit_bytes=16 * MIB),
        name="gram_pairs",
    )(me, *chunks)


def swap(x, axis, k):
    size = lax.axis_size(axis)
    return lax.ppermute(x, axis, [(i, i ^ k) for i in range(size)])


def local(bag_ids, bag_lengths, tables, cross_down, cross_up, cross_bias, proj_weight, proj_bias):
    towers = lax.axis_size("tower")
    members = lax.axis_size("dev")
    samples = bag_ids.shape[1]
    block = samples // (towers * members)
    per = LANES // block
    groups = members // per
    me = jnp.stack([lax.axis_index("dev"), lax.axis_index("tower")])
    ids = bag_ids[0].transpose(1, 2, 0)
    lens = bag_lengths[0].transpose(1, 0)
    after = lens
    pooled = {}
    for g in range(groups - 1, -1, -1):
        parts = pool_group(me, ids, lens, tables[0], after, g, towers, members, block)
        after = parts[0]
        for k, part in enumerate(parts):
            pooled[g * per + k] = part
    near = tuple(range(per))
    far = tuple(range(per, members))
    arrived = {0: pooled[0]}
    for k in range(members - 1, 0, -1):
        arrived[k] = swap(pooled[k], "dev", k)
    down, up, bias = cross_down[0, 0], cross_up[0, 0], cross_bias[0]
    low = low_part(me, down, [arrived[k] for k in near], near)
    outs = tower_out(
        me, low, down, up, bias, proj_weight[0], proj_bias,
        [arrived[k] for k in near + far], near, far, towers,
    )
    met = {0: outs[0]}
    for k in range(towers - 1, 0, -1):
        met[k] = swap(outs[k], "tower", k)
    return gram_pairs(me, [met[k] for k in range(towers)]).T


def solution(mesh):
    placed = (
        P("tower", None, "dev", None),
        P("tower", None, "dev"),
        P("tower", "dev", None, None),
        P("tower", None, None, None),
        P("tower", None, None, None),
        P("tower", None, None),
        P("tower", None, None),
        P("tower", None),
    )
    return jax.shard_map(
        local, mesh=mesh, in_specs=placed, out_specs=P(("tower", "dev"), None), check_vma=False
    )
```

time: 72.4 us -> 52.5 us (0.73)
  blocking collectives: 40 us -> 0 us
  matrix products: 26.7 us -> 0 us
  waiting for transfers between devices: 0 us -> 21 us
  starting transfers between devices: 0 us -> 14.4 us
  Pallas kernels: 0 us -> 13.8 us
  local copies, waits for them, and re-layouts: 4.44 us -> 2.81 us
  other arithmetic: 0.83 us -> 0.07 us
    all_to_all x2 -> x0, blocking collectives: 40 us -> none  [the longest x1 32.8 us: local(): lax.all_to_all(pooled, 'dev', split_axis=1, concat_axis=3, tiled=True)]
    dot_general x4 -> x0, matrix products: 26.7 us -> none  [the longest x1 18.4 us: pool_rows(): jnp.einsum('sft,ftd->sfd', counts, tables_one, preferred_element_type=jnp...]
    ppermute x0 -> x10, waiting for transfers between devices: none -> 21 us  [swap(): return lax.ppermute(x, axis, [(i, i ^ k) for i in range(size)])]
    ppermute x0 -> x10, starting transfers between devices: none -> 14.4 us  [swap(): return lax.ppermute(x, axis, [(i, i ^ k) for i in range(size)])]
    pallas_call x0 -> x5, Pallas kernels: none -> 13.8 us  [the longest x2 8.15 us: pool_group(): pl.pallas_call(functools.partial(pool_kernel, block, feats, slots), grid_...]
    unnamed x10 -> x16, local copies, waits for them, and re-layouts: 0.04 us -> 2.81 us
    reshape x2 -> x0, local copies, waits for them, and re-layouts: 1.64 us -> none  [the longest x1 0.82 us: local(): rows = pooled_block.reshape(towers * count, -1)]
    gather x1 -> x0, local copies, waits for them, and re-layouts: 1.21 us -> none  [local(): return gram[:, upper, lower]]
  transfers between devices with their start and end apart: 0 -> 10, of which waited for: 0 -> 6; matrix products, arithmetic and copies ran while one was open for 0% -> 0% of each run, Pallas kernels for 0% -> 2%
where the time goes in v1:
time: 52.5 us; the launch traced here: 52.3 us
  waiting for transfers between devices  21 us (40%)
  starting transfers between devices  14.4 us (27%)
  Pallas kernels  13.8 us (26%)
  local copies, waits for them, and re-layouts  2.81 us (5%)
    ppermute x10, waiting for transfers between devices, swap(): return lax.ppermute(x, axis, [(i, i ^ k) for i in range(size)])  21 us
    ppermute x10, starting transfers between devices, swap(): return lax.ppermute(x, axis, [(i, i ^ k) for i in range(size)])  14.4 us
    pallas_call x2, Pallas kernels, pool_group(): pl.pallas_call(functools.partial(pool_kernel, block, feats, slots), grid_...  8.15 us
    pallas_call x1, Pallas kernels, tower_out(): pl.pallas_call(functools.partial(tower_kernel, near, far), in_specs=[pl.B...  3.27 us
    unnamed x16, local copies, waits for them, and re-layouts  2.81 us
    pallas_call x1, Pallas kernels, gram_pairs(): pl.pallas_call(gram_kernel, in_specs=[pl.BlockSpec(memory_space=pltpu.SME...  1.4 us
  transfers between devices with their start and end apart: 10, of which 6 were waited for; matrix products, arithmetic and copies ran while one was open for 0% of the time, Pallas kernels for 2%

profile of v1, /device:TPU:0, one launch (start us, length us, event | category | flops | bytes accessed | tf_op | source)
XLA Modules:
  0.0 52.3 jit_solution(8103144537926178459)
XLA Ops:
  0.0 0.1 pad_add_fusion.me_ref
  0.1 0.0 copy-start.5
  0.1 1.2 %copy-done.5 = bf16[1,4,1024,128]{3,2,1,0:T(8,128)(2,1)S(1)} copy-done((bf16[1,4,1024,128]{3,2,1,0:T(8,128)(2,1)S(1)}, bf16[1,4,1024,128]{3,2,1,0:T(8,128)(2,1)}, u32[]{:S(2)}) %copy-start.5) | copy-done | bytes 1048600
  1.3 0.0 copy-start.6
  1.3 0.8 %copy-done.6 = s32[1,1024,4,4]{1,3,2,0:T(4,128)S(1)} copy-done((s32[1,1024,4,4]{1,3,2,0:T(4,128)S(1)}, s32[1,1024,4,4]{1,3,2,0:T(4,128)}, u32[]{:S(2)}) %copy-start.6) | copy-done | bytes 65560
  2.1 0.0 copy-start.7
  2.1 0.7 %copy-done.7 = s32[1,1024,4]{1,2,0:T(4,128)S(1)} copy-done((s32[1,1024,4]{1,2,0:T(4,128)S(1)}, s32[1,1024,4]{1,2,0:T(4,128)}, u32[]{:S(2)}) %copy-start.7) | copy-done | bytes 16408
  2.9 4.1 %pool_group.2 = (bf16[128,512]{1,0:T(8,128)(2,1)S(1)}, bf16[128,512]{1,0:T(8,128)(2,1)S(1)}, bf16[128,512]{1,0:T(8,128)(2,1)S(1)}, bf16[128,512]{1,0:T(8,128)(2,1)S(1)}) custom-call(s32[2]{0:T(128)S(1)} %pad_add_fusion.me_ref, s32[4,4,1024]{2,1,0:T(4,128)S(1)} %bitcast.21, s32[4,1024]{1,0:T(4,128)S(1)} %bitcast.23, bf16[4,1024,128]{2,1,0:T(8,128)(2,1)S(1)} %bitcast.19, ...), custom_call_target="tpu_custom_call" | custom-call | flops 4294967296 | bytes 1048576 | tf_op jit(solution)/shard_map/pool_group/pallas_call | solution.py:60
  6.9 0.0 copy-start
  7.0 0.0 copy-start.2
  7.0 4.1 %pool_group.3 = (bf16[128,512]{1,0:T(8,128)(2,1)S(1)}, bf16[128,512]{1,0:T(8,128)(2,1)S(1)}, bf16[128,512]{1,0:T(8,128)(2,1)S(1)}, bf16[128,512]{1,0:T(8,128)(2,1)S(1)}) custom-call(s32[2]{0:T(128)S(1)} %pad_add_fusion.me_ref, s32[4,4,1024]{2,1,0:T(4,128)S(1)} %bitcast.22, s32[4,1024]{1,0:T(4,128)S(1)} %bitcast.25, bf16[4,1024,128]{2,1,0:T(8,128)(2,1)S(1)} %bitcast.20, ...), custom_call_target="tpu_custom_call" | custom-call | flops 4294967296 | bytes 1048576 | tf_op jit(solution)/shard_map/pool_group/pallas_call | solution.py:60
  11.0 0.0 copy-start.1
  11.1 0.0 copy-start.3
  11.1 0.0 copy-start.4
  11.1 3.0 %collective-permute-start = (bf16[128,512]{1,0:T(8,128)(2,1)S(1)}, bf16[128,512]{1,0:T(8,128)(2,1)S(1)}, u32[]{:S(2)}, u32[]{:S(2)}) collective-permute-start(bf16[128,512]{1,0:T(8,128)(2,1)S(1)} %get-tuple-element.19), channel_id=1, source_target_pairs={{0,1},{1,0},{2,3},{3,2},{4,5},{5,4},{6,7},{7,6},{8,9},{9,8},{10,11... | collective-permute-start | bytes 393224 | tf_op jit(solution)/shard_map/ppermute | solution.py:198
  14.1 1.6 %collective-permute-start.1 = (bf16[128,512]{1,0:T(8,128)(2,1)S(1)}, bf16[128,512]{1,0:T(8,128)(2,1)S(1)}, u32[]{:S(2)}, u32[]{:S(2)}) collective-permute-start(bf16[128,512]{1,0:T(8,128)(2,1)S(1)} %get-tuple-element.20), channel_id=1, source_target_pairs={{0,2},{1,3},{2,0},{3,1},{4,6},{5,7},{6,4},{7,5},{8,10},{9,11},{10,... | collective-permute-start | bytes 393224 | tf_op jit(solution)/shard_map/ppermute | solution.py:198
  15.7 0.0 collective-permute-start.2
  15.7 3.9 %collective-permute-start.4 = (bf16[128,512]{1,0:T(8,128)(2,1)S(1)}, bf16[128,512]{1,0:T(8,128)(2,1)S(1)}, u32[]{:S(2)}, u32[]{:S(2)}) collective-permute-start(bf16[128,512]{1,0:T(8,128)(2,1)S(1)} %get-tuple-element.22), channel_id=1, source_target_pairs={{0,5},{1,4},{2,7},{3,6},{4,1},{5,0},{6,3},{7,2},{8,13},{9,12},{10,... | collective-permute-start | bytes 393224 | tf_op jit(solution)/shard_map/ppermute | solution.py:198
  19.6 1.4 %collective-permute-start.5 = (bf16[128,512]{1,0:T(8,128)(2,1)S(1)}, bf16[128,512]{1,0:T(8,128)(2,1)S(1)}, u32[]{:S(2)}, u32[]{:S(2)}) collective-permute-start(bf16[128,512]{1,0:T(8,128)(2,1)S(1)} %get-tuple-element.23), channel_id=1, source_target_pairs={{0,6},{1,7},{2,4},{3,5},{4,2},{5,3},{6,0},{7,1},{8,14},{9,15},{10,... | collective-permute-start | bytes 393224 | tf_op jit(solution)/shard_map/ppermute | solution.py:198
  21.0 0.0 collective-permute-done.rest_1_
  21.0 2.4 %collective-permute-start.6 = (bf16[128,512]{1,0:T(8,128)(2,1)S(1)}, bf16[128,512]{1,0:T(8,128)(2,1)S(1)}, u32[]{:S(2)}, u32[]{:S(2)}) collective-permute-start(bf16[128,512]{1,0:T(8,128)(2,1)S(1)} %get-tuple-element.24), channel_id=1, source_target_pairs={{0,7},{1,6},{2,5},{3,4},{4,3},{5,2},{6,1},{7,0},{8,15},{9,14},{10,... | collective-permute-start | bytes 393224 | tf_op jit(solution)/shard_map/ppermute | solution.py:198
  23.4 0.0 collective-permute-done.1.rest_2_
  23.4 0.2 collective-permute-start.3
  23.6 0.9 %collective-permute-done.2.rest_3_ = bf16[128,512]{1,0:T(8,128)(2,1)S(1)} collective-permute-done((bf16[128,512]{1,0:T(8,128)(2,1)S(1)}, bf16[128,512]{1,0:T(8,128)(2,1)S(1)}, u32[]{:S(2)}, u32[]{:S(2)}) %collective-permute-start.2) | collective-permute-done | bytes 131104 | tf_op jit(solution)/shard_map/ppermute | solution.py:198
  24.5 0.0 copy-done
  24.5 1.0 %low_part.1.low_ref = f32[128,512]{1,0:T(8,128)S(1)} custom-call(s32[2]{0:T(128)S(1)} %pad_add_fusion.me_ref, bf16[4096,512]{1,0:T(8,128)(2,1)S(1)} %bitcast.14, bf16[128,512]{1,0:T(8,128)(2,1)S(1)} %get-tuple-element.18.rest_0_, bf16[128,512]{1,0:T(8,128)(2,1)S(1)} %collective-permute-done.rest_1_, bf16[128,512]{1,0:T(8,128)(2,1)S(1)} %collective-permute-done.1.rest_2_, ...), custom_call_target="tpu_custom_call" | custom-call | flops 268435456 | bytes 4194304 | tf_op jit(solution)/shard_map/low_part/pallas_call | solution.py:100
  25.5 0.0 collective-permute-done.4.rest_5_
  25.5 5.6 %collective-permute-done.5.rest_6_ = bf16[128,512]{1,0:T(8,128)(2,1)S(1)} collective-permute-done((bf16[128,512]{1,0:T(8,128)(2,1)S(1)}, bf16[128,512]{1,0:T(8,128)(2,1)S(1)}, u32[]{:S(2)}, u32[]{:S(2)}) %collective-permute-start.5) | collective-permute-done | bytes 131104 | tf_op jit(solution)/shard_map/ppermute | solution.py:198
  31.1 2.5 %collective-permute-done.6.rest_7_ = bf16[128,512]{1,0:T(8,128)(2,1)S(1)} collective-permute-done((bf16[128,512]{1,0:T(8,128)(2,1)S(1)}, bf16[128,512]{1,0:T(8,128)(2,1)S(1)}, u32[]{:S(2)}, u32[]{:S(2)}) %collective-permute-start.6) | collective-permute-done | bytes 131104 | tf_op jit(solution)/shard_map/ppermute | solution.py:198
  33.6 9.0 %collective-permute-done.3.rest_4_ = bf16[128,512]{1,0:T(8,128)(2,1)S(1)} collective-permute-done((bf16[128,512]{1,0:T(8,128)(2,1)S(1)}, bf16[128,512]{1,0:T(8,128)(2,1)S(1)}, u32[]{:S(2)}, u32[]{:S(2)}) %collective-permute-start.3) | collective-permute-done | bytes 131104 | tf_op jit(solution)/shard_map/ppermute | solution.py:198
  42.5 0.0 copy-done.2
  42.5 0.0 copy-done.1
  42.5 0.0 copy-done.3
  42.5 0.0 copy-done.4
  42.6 3.3 %tower_out.1 = (bf16[32,512]{1,0:T(8,128)(2,1)S(1)}, bf16[32,512]{1,0:T(8,128)(2,1)S(1)}, bf16[32,512]{1,0:T(8,128)(2,1)S(1)}, bf16[32,512]{1,0:T(8,128)(2,1)S(1)}) custom-call(s32[2]{0:T(128)S(1)} %pad_add_fusion.me_ref, f32[128,512]{1,0:T(8,128)S(1)} %low_part.1.low_ref, bf16[4096,512]{1,0:T(8,128)(2,1)S(1)} %bitcast.15, bf16[512,4096]{1,0:T(8,128)(2,1)S(1)} %bitcast.16, ...), custom_call_target="tpu_custom_call" | custom-call | flops 1073741824 | bytes 8388608 | tf_op jit(solution)/shard_map/tower_out/pallas_call | solution.py:144
  45.8 0.1 collective-permute-start.7
  45.9 1.6 %collective-permute-start.8 = (bf16[32,512]{1,0:T(8,128)(2,1)S(1)}, bf16[32,512]{1,0:T(8,128)(2,1)S(1)}, u32[]{:S(2)}, u32[]{:S(2)}) collective-permute-start(bf16[32,512]{1,0:T(8,128)(2,1)S(1)} %get-tuple-element.27), channel_id=1, source_target_pairs={{0,16},{8,24},{16,0},{24,8},{1,17},{9,25},{17,1},{25,9},{2,18},{10... | collective-permute-start | bytes 98312 | tf_op jit(solution)/shard_map/ppermute | solution.py:198
  47.5 0.3 collective-permute-start.9
  47.8 0.0 collective-permute-done.7.rest_1_
  47.8 2.1 %collective-permute-done.8.rest_2_ = bf16[32,512]{1,0:T(8,128)(2,1)S(1)} collective-permute-done((bf16[32,512]{1,0:T(8,128)(2,1)S(1)}, bf16[32,512]{1,0:T(8,128)(2,1)S(1)}, u32[]{:S(2)}, u32[]{:S(2)}) %collective-permute-start.8) | collective-permute-done | bytes 32800 | tf_op jit(solution)/shard_map/ppermute | solution.py:198
  49.9 0.9 %collective-permute-done.9.rest_3_ = bf16[32,512]{1,0:T(8,128)(2,1)S(1)} collective-permute-done((bf16[32,512]{1,0:T(8,128)(2,1)S(1)}, bf16[32,512]{1,0:T(8,128)(2,1)S(1)}, u32[]{:S(2)}, u32[]{:S(2)}) %collective-permute-start.9) | collective-permute-done | bytes 32800 | tf_op jit(solution)/shard_map/ppermute | solution.py:198
  50.8 1.4 %gram_pairs.1 = f32[6,32]{1,0:T(8,128)} custom-call(s32[2]{0:T(128)S(1)} %pad_add_fusion.me_ref, bf16[32,512]{1,0:T(8,128)(2,1)S(1)} %get-tuple-element.25.rest_0_, bf16[32,512]{1,0:T(8,128)(2,1)S(1)} %collective-permute-done.7.rest_1_, bf16[32,512]{1,0:T(8,128)(2,1)S(1)} %collective-permute-done.8.rest_2_, bf16[32,512]{1,0:T(8,128)(2,1)S(1)} %collective-permute-done.9.rest_3_), custom_call_target="tpu_custom_call" | custom-call | tf_op jit(solution)/shard_map/gram_pairs/pallas_call | solution.py:184
Async XLA Ops:
  0.1 1.2 %copy-start.5 = (bf16[1,4,1024,128]{3,2,1,0:T(8,128)(2,1)S(1)}, bf16[1,4,1024,128]{3,2,1,0:T(8,128)(2,1)}, u32[]{:S(2)}) copy-start(bf16[1,4,1024,128]{3,2,1,0:T(8,128)(2,1)} %param.10) | copy-start | bytes 3145732
  1.3 0.8 %copy-start.6 = (s32[1,1024,4,4]{1,3,2,0:T(4,128)S(1)}, s32[1,1024,4,4]{1,3,2,0:T(4,128)}, u32[]{:S(2)}) copy-start(s32[1,1024,4,4]{1,3,2,0:T(4,128)} %param.8) | copy-start | bytes 196612
  2.1 0.7 %copy-start.7 = (s32[1,1024,4]{1,2,0:T(4,128)S(1)}, s32[1,1024,4]{1,2,0:T(4,128)}, u32[]{:S(2)}) copy-start(s32[1,1024,4]{1,2,0:T(4,128)} %param.9) | copy-start | bytes 49156
  6.9 17.5 %copy-start = (bf16[1,1,4096,512]{3,2,1,0:T(8,128)(2,1)S(1)}, bf16[1,1,4096,512]{3,2,1,0:T(8,128)(2,1)}, u32[]{:S(2)}) copy-start(bf16[1,1,4096,512]{3,2,1,0:T(8,128)(2,1)} %param.11) | copy-start | bytes 12582916
  7.0 35.6 %copy-start.2 = (bf16[1,4096,512]{2,1,0:T(8,128)(2,1)S(1)}, bf16[1,4096,512]{2,1,0:T(8,128)(2,1)}, u32[]{:S(2)}) copy-start(bf16[1,4096,512]{2,1,0:T(8,128)(2,1)} %param.14) | copy-start | bytes 12582916
  11.0 31.5 %copy-start.1 = (bf16[1,1,512,4096]{3,2,1,0:T(8,128)(2,1)S(1)}, bf16[1,1,512,4096]{3,2,1,0:T(8,128)(2,1)}, u32[]{:S(2)}) copy-start(bf16[1,1,512,4096]{3,2,1,0:T(8,128)(2,1)} %param.12) | copy-start | bytes 12582916
  11.1 31.5 %copy-start.3 = (f32[1,1,4096]{2,1,0:T(1,128)S(1)}, f32[1,1,4096]{2,1,0:T(1,128)}, u32[]{:S(2)}) copy-start(f32[1,1,4096]{2,1,0:T(1,128)} %param.13) | copy-start | bytes 49156
  11.1 31.5 %copy-start.4 = (f32[1,512]{1,0:T(1,128)S(1)}, f32[1,512]{1,0:T(1,128)}, u32[]{:S(2)}) copy-start(f32[1,512]{1,0:T(1,128)} %pb_ref.1) | copy-start | bytes 6148
  11.1 9.9 %collective-permute-start = (bf16[128,512]{1,0:T(8,128)(2,1)S(1)}, bf16[128,512]{1,0:T(8,128)(2,1)S(1)}, u32[]{:S(2)}, u32[]{:S(2)}) collective-permute-start(bf16[128,512]{1,0:T(8,128)(2,1)S(1)} %get-tuple-element.19), channel_id=1, source_target_pairs={{0,1},{1,0},{2,3},{3,2},{4,5},{5,4},{6,7},{7,6},{8,9},{9,8},{10,11... | collective-permute-start | bytes 393224 | tf_op jit(solution)/shard_map/ppermute | solution.py:198
  14.1 9.3 %collective-permute-start.1 = (bf16[128,512]{1,0:T(8,128)(2,1)S(1)}, bf16[128,512]{1,0:T(8,128)(2,1)S(1)}, u32[]{:S(2)}, u32[]{:S(2)}) collective-permute-start(bf16[128,512]{1,0:T(8,128)(2,1)S(1)} %get-tuple-element.20), channel_id=1, source_target_pairs={{0,2},{1,3},{2,0},{3,1},{4,6},{5,7},{6,4},{7,5},{8,10},{9,11},{10,... | collective-permute-start | bytes 393224 | tf_op jit(solution)/shard_map/ppermute | solution.py:198
  15.7 8.8 %collective-permute-start.2 = (bf16[128,512]{1,0:T(8,128)(2,1)S(1)}, bf16[128,512]{1,0:T(8,128)(2,1)S(1)}, u32[]{:S(2)}, u32[]{:S(2)}) collective-permute-start(bf16[128,512]{1,0:T(8,128)(2,1)S(1)} %get-tuple-element.21), channel_id=1, source_target_pairs={{0,3},{1,2},{2,1},{3,0},{4,7},{5,6},{6,5},{7,4},{8,11},{9,10},{10,... | collective-permute-start | bytes 393224 | tf_op jit(solution)/shard_map/ppermute | solution.py:198
  15.7 9.8 %collective-permute-start.4 = (bf16[128,512]{1,0:T(8,128)(2,1)S(1)}, bf16[128,512]{1,0:T(8,128)(2,1)S(1)}, u32[]{:S(2)}, u32[]{:S(2)}) collective-permute-start(bf16[128,512]{1,0:T(8,128)(2,1)S(1)} %get-tuple-element.22), channel_id=1, source_target_pairs={{0,5},{1,4},{2,7},{3,6},{4,1},{5,0},{6,3},{7,2},{8,13},{9,12},{10,... | collective-permute-start | bytes 393224 | tf_op jit(solution)/shard_map/ppermute | solution.py:198
  19.6 11.5 %collective-permute-start.5 = (bf16[128,512]{1,0:T(8,128)(2,1)S(1)}, bf16[128,512]{1,0:T(8,128)(2,1)S(1)}, u32[]{:S(2)}, u32[]{:S(2)}) collective-permute-start(bf16[128,512]{1,0:T(8,128)(2,1)S(1)} %get-tuple-element.23), channel_id=1, source_target_pairs={{0,6},{1,7},{2,4},{3,5},{4,2},{5,3},{6,0},{7,1},{8,14},{9,15},{10,... | collective-permute-start | bytes 393224 | tf_op jit(solution)/shard_map/ppermute | solution.py:198
  21.0 12.6 %collective-permute-start.6 = (bf16[128,512]{1,0:T(8,128)(2,1)S(1)}, bf16[128,512]{1,0:T(8,128)(2,1)S(1)}, u32[]{:S(2)}, u32[]{:S(2)}) collective-permute-start(bf16[128,512]{1,0:T(8,128)(2,1)S(1)} %get-tuple-element.24), channel_id=1, source_target_pairs={{0,7},{1,6},{2,5},{3,4},{4,3},{5,2},{6,1},{7,0},{8,15},{9,14},{10,... | collective-permute-start | bytes 393224 | tf_op jit(solution)/shard_map/ppermute | solution.py:198
  23.4 19.1 %collective-permute-start.3 = (bf16[128,512]{1,0:T(8,128)(2,1)S(1)}, bf16[128,512]{1,0:T(8,128)(2,1)S(1)}, u32[]{:S(2)}, u32[]{:S(2)}) collective-permute-start(bf16[128,512]{1,0:T(8,128)(2,1)S(1)} %get-tuple-element.17.after_ref), channel_id=1, source_target_pairs={{0,4},{1,5},{2,6},{3,7},{4,0},{5,1},{6,2},{7,3},{8,12},{9,13},{10,... | collective-permute-start | bytes 393224 | tf_op jit(solution)/shard_map/ppermute | solution.py:198
  45.8 1.9 %collective-permute-start.7 = (bf16[32,512]{1,0:T(8,128)(2,1)S(1)}, bf16[32,512]{1,0:T(8,128)(2,1)S(1)}, u32[]{:S(2)}, u32[]{:S(2)}) collective-permute-start(bf16[32,512]{1,0:T(8,128)(2,1)S(1)} %get-tuple-element.26), channel_id=1, source_target_pairs={{0,8},{8,0},{16,24},{24,16},{1,9},{9,1},{17,25},{25,17},{2,10},{10... | collective-permute-start | bytes 98312 | tf_op jit(solution)/shard_map/ppermute | solution.py:198
  45.9 4.0 %collective-permute-start.8 = (bf16[32,512]{1,0:T(8,128)(2,1)S(1)}, bf16[32,512]{1,0:T(8,128)(2,1)S(1)}, u32[]{:S(2)}, u32[]{:S(2)}) collective-permute-start(bf16[32,512]{1,0:T(8,128)(2,1)S(1)} %get-tuple-element.27), channel_id=1, source_target_pairs={{0,16},{8,24},{16,0},{24,8},{1,17},{9,25},{17,1},{25,9},{2,18},{10... | collective-permute-start | bytes 98312 | tf_op jit(solution)/shard_map/ppermute | solution.py:198
  47.5 3.3 %collective-permute-start.9 = (bf16[32,512]{1,0:T(8,128)(2,1)S(1)}, bf16[32,512]{1,0:T(8,128)(2,1)S(1)}, u32[]{:S(2)}, u32[]{:S(2)}) collective-permute-start(bf16[32,512]{1,0:T(8,128)(2,1)S(1)} %get-tuple-element.28), channel_id=1, source_target_pairs={{0,24},{8,16},{16,8},{24,0},{1,25},{9,17},{17,9},{25,1},{2,26},{10... | collective-permute-start | bytes 98312 | tf_op jit(solution)/shard_map/ppermute | solution.py:198

commit v2 on v0

v2 whole, which is shorter than its diff:
```python
import functools

import jax
import jax.numpy as jnp
import numpy as np
from jax import lax
from jax.experimental import pallas as pl
from jax.experimental.pallas import tpu as pltpu
from jax.sharding import PartitionSpec as P

LANES = 128
MIB = 1 << 20
BATCH = 512
ANY = pl.BlockSpec(memory_space=pl.ANY)
VMEM = pl.BlockSpec(memory_space=pltpu.VMEM)


def bag_tiles(group, block, towers, ids_ref, len_ref):
    feats, slots, samples = ids_ref.shape
    groups = samples // (towers * LANES)
    tiles = []
    for t in range(towers):
        at = pl.ds(pl.multiple_of((t * groups + group) * LANES, LANES), LANES)
        lens = len_ref[:, at]
        rows = []
        for f in range(feats):
            ids = ids_ref[f, :, at]
            slot = lax.broadcasted_iota(jnp.int32, ids.shape, 0)
            ids = jnp.where(slot < lens[f : f + 1], ids, -1)
            times = jnp.zeros(ids.shape, jnp.float32)
            for p in range(slots):
                times += jnp.where(ids == ids[p : p + 1], 1.0, 0.0)
            rows += [ids.astype(jnp.float32), times]
        tiles.append(jnp.concatenate(rows, axis=0))
    return tiles


def bag_columns(tiles, dest, block):
    per = LANES // block
    lane = lax.broadcasted_iota(jnp.int32, tiles[0].shape, 1) // block
    columns = []
    for first in range(0, len(tiles), per):
        merged = None
        for q in range(per):
            shift = lax.rem(q - dest + per, per) * block
            moved = pltpu.roll(tiles[first + q], shift, 1)
            merged = moved if merged is None else jnp.where(lane == q, moved, merged)
        pad = -merged.shape[0] % LANES
        if pad:
            merged = jnp.concatenate([merged, jnp.zeros((pad, LANES), jnp.float32)], axis=0)
        columns.append(merged.T)
    return columns


def pool_rows(columns, f, slots, table):
    rows, table_rows = columns.shape[0], table.shape[0]
    place = lax.broadcasted_iota(jnp.int16, (rows, table_rows), 1)
    counts = jnp.zeros((rows, table_rows), jnp.bfloat16)
    for p in range(slots):
        c = 2 * slots * f + p
        own = columns[:, c : c + 1].astype(jnp.int32).astype(jnp.int16)
        times = columns[:, c + slots : c + slots + 1].astype(jnp.bfloat16)
        counts = jnp.where(place == own, times, counts)
    return jnp.dot(counts, table, preferred_element_type=jnp.float32).astype(jnp.bfloat16)


def pool_dests(tiles, dests, block, slots, tables, buf, ready=None):
    feats, width = tables.shape[0], tables.shape[2]
    height = buf.shape[1]
    batch = max(1, BATCH // height)
    for first in range(0, len(dests), batch):
        some = dests[first : first + batch]
        columns = [c for d in some for c in bag_columns(tiles, d, block)]
        columns = jnp.concatenate(columns, axis=0) if len(columns) > 1 else columns[0]
        for f in range(feats):
            if ready is not None:
                ready(f)
            rows = pool_rows(columns, f, slots, tables[f])
            for i in range(len(some)):
                buf[first + i, :, f * width : (f + 1) * width] = rows[
                    i * height : (i + 1) * height
                ]


def first_kernel(
    k, block, towers, ids_hbm, len_hbm, tab_hbm, out_hbm, ids_ref, len_ref, tab_ref, buf, sems
):
    per = LANES // block
    feats, slots, _ = ids_ref.shape
    width = tab_ref.shape[2]
    bags = [
        pltpu.make_async_copy(ids_hbm, ids_ref, sems.at[0]),
        pltpu.make_async_copy(len_hbm, len_ref, sems.at[1]),
    ]
    rows = [
        pltpu.make_async_copy(tab_hbm.at[f], tab_ref.at[f], sems.at[2 + f]) for f in range(feats)
    ]
    for copy in bags + rows:
        copy.start()
    for copy in bags:
        copy.wait()
    tiles = bag_tiles(lax.axis_index("dev") // per ^ k // per, block, towers, ids_ref, len_ref)
    dest = lax.rem(lax.axis_index("dev"), per) ^ k % per
    columns = bag_columns(tiles, dest, block)
    columns = jnp.concatenate(columns, axis=0) if len(columns) > 1 else columns[0]
    sent = []
    for f in range(feats):
        rows[f].wait()
        at = pl.ds(f * width, width)
        buf[:, at] = pool_rows(columns, f, slots, tab_ref[f])
        sent.append(pltpu.make_async_copy(buf.at[:, at], out_hbm.at[:, at], sems.at[2 + feats + f]))
        sent[-1].start()
    for copy in sent:
        copy.wait()


def pool_first(ids, lens, tables, k, block, towers):
    feats = ids.shape[0]
    depth = feats * tables.shape[2]
    return pl.pallas_call(
        functools.partial(first_kernel, k, block, towers),
        in_specs=[ANY, ANY, ANY],
        out_specs=[ANY, VMEM, VMEM, VMEM],
        out_shape=[
            pltpu.HBM((towers * block, depth), jnp.bfloat16),
            jax.ShapeDtypeStruct(ids.shape, ids.dtype),
            jax.ShapeDtypeStruct(lens.shape, lens.dtype),
            jax.ShapeDtypeStruct(tables.shape, tables.dtype),
        ],
        scratch_shapes=[
            pltpu.VMEM((towers * block, depth), jnp.bfloat16),
            pltpu.SemaphoreType.DMA((2 + 2 * feats,)),
        ],
        compiler_params=pltpu.CompilerParams(vmem_limit_bytes=16 * MIB),
        name="pool_first",
    )(ids, lens, tables)


def more_kernel(ks, block, towers, ids_ref, len_ref, tab_ref, after_ref, *rest):
    outs, (buf, sems) = rest[:-2], rest[-2:]
    per = LANES // block
    slots = ids_ref.shape[1]
    low = lax.rem(lax.axis_index("dev"), per)
    for g in sorted({k // per for k in ks}):
        some = [i for i, k in enumerate(ks) if k // per == g]
        tiles = bag_tiles(lax.axis_index("dev") // per ^ g, block, towers, ids_ref, len_ref)
        dests = [low ^ ks[i] % per for i in some]
        pool_dests(
            tiles, dests, block, slots, tab_ref, buf.at[some[0] : some[0] + len(some)]
        )
    copies = [pltpu.make_async_copy(buf.at[i], out, sems.at[i]) for i, out in enumerate(outs)]
    for copy in copies:
        copy.start()
    for copy in copies:
        copy.wait()


def pool_more(ids, lens, tables, after, ks, block, towers):
    depth = ids.shape[0] * tables.shape[2]
    shape = (towers * block, depth)
    return pl.pallas_call(
        functools.partial(more_kernel, ks, block, towers),
        in_specs=[VMEM, VMEM, VMEM, ANY],
        out_specs=[ANY] * len(ks),
        out_shape=[pltpu.HBM(shape, jnp.bfloat16)] * len(ks),
        scratch_shapes=[
            pltpu.VMEM((len(ks),) + shape, jnp.bfloat16),
            pltpu.SemaphoreType.DMA((len(ks),)),
        ],
        compiler_params=pltpu.CompilerParams(vmem_limit_bytes=16 * MIB),
        cost_estimate=pl.CostEstimate(flops=10**9, bytes_accessed=0, transcendentals=0),
        name="pool_more",
    )(ids, lens, tables, after)


def low_kernel(ks, held, down_ref, *rest):
    chunks, low, out_ref = rest[: len(ks)], rest[len(ks) : -1 - held], rest[-1]
    depth = chunks[0].shape[1]
    total = low[0][...] if low else None
    for k, chunk in zip(ks, chunks, strict=True):
        at = pl.ds(pl.multiple_of((lax.axis_index("dev") ^ k) * depth, depth), depth)
        part = jnp.dot(chunk[...], down_ref[at, :], preferred_element_type=jnp.float32)
        total = part if total is None else total + part
    out_ref[...] = total


def low_part(down, chunks, ks, low, held=()):
    return pl.pallas_call(
        functools.partial(low_kernel, ks, len(held)),
        in_specs=[VMEM] * (1 + len(ks) + len(low)) + [ANY] * len(held),
        out_specs=VMEM,
        out_shape=jax.ShapeDtypeStruct((chunks[0].shape[0], down.shape[1]), jnp.float32),
        compiler_params=pltpu.CompilerParams(vmem_limit_bytes=16 * MIB),
        cost_estimate=pl.CostEstimate(flops=10**9, bytes_accessed=0, transcendentals=0),
        name="low_part",
    )(down, *chunks, *low, *held)


def tower_kernel(
    ks, late, towers, low_ref, down_ref, up_ref, bias_ref, proj_ref, pb_ref, *rest
):
    chunks, outs, scratch = rest[: -towers - 1], rest[-towers - 1 : -1], rest[-1]
    depth = chunks[0].shape[1]
    block = outs[0].shape[0]
    chunks = [
        (pl.ds(pl.multiple_of((lax.axis_index("dev") ^ k) * depth, depth), depth), chunk)
        for k, chunk in zip(ks, chunks, strict=True)
    ]
    low = low_ref[...]
    for at, chunk in chunks[-late:]:
        low += jnp.dot(chunk[...], down_ref[at, :], preferred_element_type=jnp.float32)
    low = low.astype(jnp.bfloat16)
    total = pb_ref[...]
    for at, chunk in chunks:
        high = jnp.dot(low, up_ref[:, at], preferred_element_type=jnp.float32)
        high = high + bias_ref[:, at]
        base = chunk[...].astype(jnp.float32)
        cross = (base * high + base).astype(jnp.bfloat16)
        total = total + jnp.dot(cross, proj_ref[at, :], preferred_element_type=jnp.float32)
    scratch[...] = total.astype(jnp.bfloat16)
    for k, out in enumerate(outs):
        out[...] = scratch[pl.ds(pl.multiple_of((lax.axis_index("tower") ^ k) * block, block), block), :]


def tower_out(low, down, up, bias, proj, pb, chunks, ks, late, towers):
    rows = chunks[0].shape[0]
    shape = jax.ShapeDtypeStruct((rows // towers, proj.shape[1]), jnp.bfloat16)
    return pl.pallas_call(
        functools.partial(tower_kernel, ks, late, towers),
        in_specs=[VMEM] * (6 + len(chunks)),
        out_specs=[VMEM] * towers,
        out_shape=[shape] * towers,
        scratch_shapes=[pltpu.VMEM((rows, proj.shape[1]), jnp.bfloat16)],
        compiler_params=pltpu.CompilerParams(vmem_limit_bytes=16 * MIB),
        cost_estimate=pl.CostEstimate(
            flops=4 * rows * proj.size, bytes_accessed=0, transcendentals=0
        ),
        name="tower_out",
    )(low, down, up, bias, proj, pb, *chunks)


def gram_kernel(*rest):
    chunks, out_ref, rows_ref = rest[:-2], rest[-2], rest[-1]
    towers, (block, width) = len(chunks), chunks[0].shape
    for k, chunk in enumerate(chunks):
        rows_ref[lax.axis_index("tower") ^ k] = chunk[...]
    rows = rows_ref[...].reshape(towers * block, width)
    gram = lax.dot_general(
        rows, rows, (((1,), (1,)), ((), ())), preferred_element_type=jnp.float32
    ) * (1.0 / np.sqrt(np.float32(width)))
    n = towers * block
    at = lax.broadcasted_iota(jnp.int32, (block, n), 0)
    to = lax.broadcasted_iota(jnp.int32, (block, n), 1)
    own = at == lax.rem(to, block)
    place = 0
    for i in range(towers):
        picked = jnp.where(own, gram[i * block : (i + 1) * block], 0.0)
        line = jnp.sum(picked, axis=0, keepdims=True)
        for j in range(i + 1, towers):
            out_ref[place : place + 1, :] = line[:, j * block : (j + 1) * block]
            place += 1


def gram_pairs(chunks):
    towers, (block, width) = len(chunks), chunks[0].shape
    pairs = towers * (towers - 1) // 2
    return pl.pallas_call(
        gram_kernel,
        in_specs=[VMEM] * towers,
        out_specs=VMEM,
        out_shape=jax.ShapeDtypeStruct((pairs, block), jnp.float32),
        scratch_shapes=[pltpu.VMEM((towers, block, width), jnp.bfloat16)],
        compiler_params=pltpu.CompilerParams(vmem_limit_bytes=16 * MIB),
        name="gram_pairs",
    )(*chunks)


def swap(x, axis, k):
    size = lax.axis_size(axis)
    return lax.ppermute(x, axis, [(i, i ^ k) for i in range(size)])


def local(bag_ids, bag_lengths, tables, cross_down, cross_up, cross_bias, proj_weight, proj_bias):
    towers = lax.axis_size("tower")
    members = lax.axis_size("dev")
    samples = bag_ids.shape[1]
    block = samples // (towers * members)
    per = LANES // block
    groups = members // per
    ids = bag_ids[0].transpose(1, 2, 0)
    lens = bag_lengths[0].transpose(1, 0)
    bias = cross_bias[0]
    fixed = [ids, lens, tables[0], cross_down[0, 0], cross_up[0, 0], proj_weight[0]]
    ids, lens, rows, *weights = (pltpu.with_memory_space_constraint(w, pltpu.HBM) for w in fixed)
    down, up, proj = (pltpu.with_memory_space_constraint(w, pltpu.VMEM) for w in weights)
    far, near = list(range(per, members)), list(range(per - 1, 0, -1))
    order = far[:1] + near[:1] + far[1:-1] + near[1:-1] + far[-1:] + near[-1:]
    pooled, got = {}, {}
    pooled[far[0]], ids, lens, rows = pool_first(ids, lens, rows, far[0], block, towers)

    def pool(ks, after):
        ks = sorted(ks)
        done = pltpu.with_memory_space_constraint(pooled[after], pltpu.HBM)
        parts = pool_more(ids, lens, rows, done, ks, block, towers)
        pooled.update(zip(ks, parts, strict=True))

    pool(order[1 : len(far)], far[0])
    pool([0] + order[len(far) :], far[-2])
    for k in order:
        got[k] = swap(pooled[k], "dev", k)
    got[0] = pooled[0]
    low = []
    for some in [[k] for k in order[: len(far)]] + [[0] + near[1:-1]]:
        held = (up, proj) if some == near[:1] else ()
        low = [low_part(down, [got[k] for k in some], some, low, held)]
    ks = [0] + order
    outs = tower_out(low[0], down, up, bias, proj, proj_bias, [got[k] for k in ks], ks, 2, towers)
    met = [outs[0]] + [swap(outs[k], "tower", k) for k in range(1, towers)]
    return gram_pairs(met).T


def solution(mesh):
    placed = (
        P("tower", None, "dev", None),
        P("tower", None, "dev"),
        P("tower", "dev", None, None),
        P("tower", None, None, None),
        P("tower", None, None, None),
        P("tower", None, None),
        P("tower", None, None),
        P("tower", None),
    )
    return jax.shard_map(
        local, mesh=mesh, in_specs=placed, out_specs=P(("tower", "dev"), None), check_vma=False
    )
```

time: 72.4 us -> 40.6 us (0.56)
  blocking collectives: 40 us -> 0 us
  matrix products: 26.7 us -> 0 us
  starting transfers between devices: 0 us -> 15.6 us
  Pallas kernels: 0 us -> 14 us
  waiting for transfers between devices: 0 us -> 10.6 us
  local copies, waits for them, and re-layouts: 4.44 us -> 0.1 us
  other arithmetic: 0.83 us -> 0 us
    all_to_all x2 -> x0, blocking collectives: 40 us -> none  [the longest x1 32.8 us: local(): lax.all_to_all(pooled, 'dev', split_axis=1, concat_axis=3, tiled=True)]
    dot_general x4 -> x0, matrix products: 26.7 us -> none  [the longest x1 18.4 us: pool_rows(): jnp.einsum('sft,ftd->sfd', counts, tables_one, preferred_element_type=jnp...]
    ppermute x0 -> x10, starting transfers between devices: none -> 15.6 us  [swap(): return lax.ppermute(x, axis, [(i, i ^ k) for i in range(size)])]
    pallas_call x0 -> x10, Pallas kernels: none -> 14 us  [the longest x2 5.98 us: pool_more(): pl.pallas_call(functools.partial(more_kernel, ks, block, towers), in_spec...]
    ppermute x0 -> x10, waiting for transfers between devices: none -> 10.6 us  [swap(): return lax.ppermute(x, axis, [(i, i ^ k) for i in range(size)])]
    reshape x2 -> x0, local copies, waits for them, and re-layouts: 1.64 us -> none  [the longest x1 0.82 us: local(): rows = pooled_block.reshape(towers * count, -1)]
    gather x1 -> x0, local copies, waits for them, and re-layouts: 1.21 us -> none  [local(): return gram[:, upper, lower]]
    slice x1 -> x0, local copies, waits for them, and re-layouts: 1.06 us -> none  [pool_rows(): ids_one[:, :, slot_index, None] == positions]
  transfers between devices with their start and end apart: 0 -> 10, of which waited for: 0 -> 3; matrix products, arithmetic and copies ran while one was open for 0% -> 0% of each run, Pallas kernels for 0% -> 18%
where the time goes in v2:
time: 40.6 us; the launch traced here: 40.5 us
  starting transfers between devices  15.6 us (38%)
  Pallas kernels  14 us (34%)
  waiting for transfers between devices  10.6 us (26%)
    ppermute x10, starting transfers between devices, swap(): return lax.ppermute(x, axis, [(i, i ^ k) for i in range(size)])  15.6 us
    ppermute x10, waiting for transfers between devices, swap(): return lax.ppermute(x, axis, [(i, i ^ k) for i in range(size)])  10.6 us
    pallas_call x2, Pallas kernels, pool_more(): pl.pallas_call(functools.partial(more_kernel, ks, block, towers), in_spec...  5.98 us
    pallas_call x1, Pallas kernels, pool_first(): pl.pallas_call(functools.partial(first_kernel, k, block, towers), in_spec...  3.3 us
    pallas_call x1, Pallas kernels, tower_out(): pl.pallas_call(functools.partial(tower_kernel, ks, late, towers), in_spec...  2.57 us
    pallas_call x5, Pallas kernels, low_part(): pl.pallas_call(functools.partial(low_kernel, ks, len(held)), in_specs=[VM...  1.25 us
    pallas_call x1, Pallas kernels, gram_pairs(): pl.pallas_call(gram_kernel, in_specs=[VMEM] * towers, out_specs=VMEM, out...  0.87 us
  transfers between devices with their start and end apart: 10, of which 3 were waited for; matrix products, arithmetic and copies ran while one was open for 0% of the time, Pallas kernels for 18%

profile of v2, /device:TPU:0, one launch (start us, length us, event | category | flops | bytes accessed | tf_op | source)
XLA Modules:
  0.0 40.5 jit_solution(17180905706131802135)
XLA Ops:
  0.0 0.0 copy-start
  0.0 3.3 %pool_first.1 = (bf16[128,512]{1,0:T(8,128)(2,1)}, s32[4,4,1024]{2,1,0:T(4,128)S(1)}, s32[4,1024]{1,0:T(4,128)S(1)}, bf16[4,1024,128]{2,1,0:T(8,128)(2,1)S(1)}) custom-call(s32[4,4,1024]{2,1,0:T(4,128)} %bitcast.24, s32[4,1024]{1,0:T(4,128)} %bitcast.25, bf16[4,1024,128]{2,1,0:T(8,128)(2,1)} %bitcast.23), custom_call_target="tpu_custom_call" | custom-call | tf_op jit(solution)/shard_map/pool_first/pallas_call | solution.py:120
  3.3 4.1 %collective-permute-start.4 = (bf16[128,512]{1,0:T(8,128)(2,1)}, bf16[128,512]{1,0:T(8,128)(2,1)S(1)}, u32[]{:S(2)}, u32[]{:S(2)}) collective-permute-start(bf16[128,512]{1,0:T(8,128)(2,1)} %get-tuple-element.23.after_ref), channel_id=1, source_target_pairs={{0,4},{1,5},{2,6},{3,7},{4,0},{5,1},{6,2},{7,3},{8,12},{9,13},{10,... | collective-permute-start | bytes 393224 | tf_op jit(solution)/shard_map/ppermute | solution.py:280
  7.4 0.0 copy-start.2
  7.4 2.9 %pool_more.2 = (bf16[128,512]{1,0:T(8,128)(2,1)}, bf16[128,512]{1,0:T(8,128)(2,1)}, bf16[128,512]{1,0:T(8,128)(2,1)}) custom-call(s32[4,4,1024]{2,1,0:T(4,128)S(1)} %get-tuple-element.20.ids_ref, s32[4,1024]{1,0:T(4,128)S(1)} %get-tuple-element.21.len_ref, bf16[4,1024,128]{2,1,0:T(8,128)(2,1)S(1)} %get-tuple-element.22.tab_ref, ...), custom_call_target="tpu_custom_call" | custom-call | flops 1000000000 | tf_op jit(solution)/shard_map/pool_more/pallas_call | solution.py:161
  10.3 0.0 copy-start.1
  10.3 1.4 %collective-permute-start.1 = (bf16[128,512]{1,0:T(8,128)(2,1)}, bf16[128,512]{1,0:T(8,128)(2,1)S(1)}, u32[]{:S(2)}, u32[]{:S(2)}) collective-permute-start(bf16[128,512]{1,0:T(8,128)(2,1)} %get-tuple-element.24.after_ref), channel_id=1, source_target_pairs={{0,6},{1,7},{2,4},{3,5},{4,2},{5,3},{6,0},{7,1},{8,14},{9,15},{10,... | collective-permute-start | bytes 393224 | tf_op jit(solution)/shard_map/ppermute | solution.py:280
  11.7 1.2 %collective-permute-start.3 = (bf16[128,512]{1,0:T(8,128)(2,1)}, bf16[128,512]{1,0:T(8,128)(2,1)S(1)}, u32[]{:S(2)}, u32[]{:S(2)}) collective-permute-start(bf16[128,512]{1,0:T(8,128)(2,1)} %get-tuple-element.28), channel_id=1, source_target_pairs={{0,3},{1,2},{2,1},{3,0},{4,7},{5,6},{6,5},{7,4},{8,11},{9,10},{10,... | collective-permute-start | bytes 393224 | tf_op jit(solution)/shard_map/ppermute | solution.py:280
  12.9 3.1 %pool_more.3 = (bf16[128,512]{1,0:T(8,128)(2,1)}, bf16[128,512]{1,0:T(8,128)(2,1)}, bf16[128,512]{1,0:T(8,128)(2,1)}, bf16[128,512]{1,0:T(8,128)(2,1)}) custom-call(s32[4,4,1024]{2,1,0:T(4,128)S(1)} %get-tuple-element.20.ids_ref, s32[4,1024]{1,0:T(4,128)S(1)} %get-tuple-element.21.len_ref, bf16[4,1024,128]{2,1,0:T(8,128)(2,1)S(1)} %get-tuple-element.22.tab_ref, ...), custom_call_target="tpu_custom_call" | custom-call | flops 1000000000 | tf_op jit(solution)/shard_map/pool_more/pallas_call | solution.py:161
  16.1 0.0 copy-start.6
  16.1 1.8 %collective-permute-start = (bf16[128,512]{1,0:T(8,128)(2,1)}, bf16[128,512]{1,0:T(8,128)(2,1)S(1)}, u32[]{:S(2)}, u32[]{:S(2)}) collective-permute-start(bf16[128,512]{1,0:T(8,128)(2,1)} %get-tuple-element.26), channel_id=1, source_target_pairs={{0,2},{1,3},{2,0},{3,1},{4,6},{5,7},{6,4},{7,5},{8,10},{9,11},{10,... | collective-permute-start | bytes 393224 | tf_op jit(solution)/shard_map/ppermute | solution.py:280
  17.9 1.7 %collective-permute-start.2 = (bf16[128,512]{1,0:T(8,128)(2,1)}, bf16[128,512]{1,0:T(8,128)(2,1)S(1)}, u32[]{:S(2)}, u32[]{:S(2)}) collective-permute-start(bf16[128,512]{1,0:T(8,128)(2,1)} %get-tuple-element.27), channel_id=1, source_target_pairs={{0,5},{1,4},{2,7},{3,6},{4,1},{5,0},{6,3},{7,2},{8,13},{9,12},{10,... | collective-permute-start | bytes 393224 | tf_op jit(solution)/shard_map/ppermute | solution.py:280
  19.5 0.0 collective-permute-done.4.rest_0_.rest_1_
  19.5 1.9 %collective-permute-start.5 = (bf16[128,512]{1,0:T(8,128)(2,1)}, bf16[128,512]{1,0:T(8,128)(2,1)S(1)}, u32[]{:S(2)}, u32[]{:S(2)}) collective-permute-start(bf16[128,512]{1,0:T(8,128)(2,1)} %get-tuple-element.29), channel_id=1, source_target_pairs={{0,7},{1,6},{2,5},{3,4},{4,3},{5,2},{6,1},{7,0},{8,15},{9,14},{10,... | collective-permute-start | bytes 393224 | tf_op jit(solution)/shard_map/ppermute | solution.py:280
  21.4 0.0 copy-done
  21.4 0.2 low_part.5.rest_1_
  21.7 0.0 collective-permute-done.3.rest_0_.rest_2_
  21.7 0.0 copy-done.6
  21.7 1.6 %collective-permute-start.6 = (bf16[128,512]{1,0:T(8,128)(2,1)S(1)}, bf16[128,512]{1,0:T(8,128)(2,1)S(1)}, u32[]{:S(2)}, u32[]{:S(2)}) collective-permute-start(bf16[128,512]{1,0:T(8,128)(2,1)S(1)} %copy-done.6), channel_id=1, source_target_pairs={{0,1},{1,0},{2,3},{3,2},{4,5},{5,4},{6,7},{7,6},{8,9},{9,8},{10,11... | collective-permute-start | bytes 393224 | tf_op jit(solution)/shard_map/ppermute | solution.py:280
  23.3 0.0 copy-done.2
  23.3 0.0 copy-done.1
  23.3 0.2 low_part.6.rest_1_
  23.5 0.0 copy-start.3
  23.5 7.5 %collective-permute-done.2.rest_0_.rest_3_ = bf16[128,512]{1,0:T(8,128)(2,1)S(1)} collective-permute-done((bf16[128,512]{1,0:T(8,128)(2,1)}, bf16[128,512]{1,0:T(8,128)(2,1)S(1)}, u32[]{:S(2)}, u32[]{:S(2)}) %collective-permute-start.2) | collective-permute-done | bytes 131104 | tf_op jit(solution)/shard_map/ppermute | solution.py:280
  31.1 0.2 low_part.7.rest_1_
  31.3 0.0 copy-start.4
  31.3 0.0 copy-start.5
  31.3 0.0 collective-permute-done.1.rest_0_.rest_4_
  31.3 0.2 low_part.8.rest_2_
  31.6 0.0 collective-permute-done.rest_1_.rest_5_
  31.6 0.0 copy-done.3
  31.6 0.3 low_part.9.low_ref
  31.9 0.0 collective-permute-done.5.rest_6_
  31.9 0.0 collective-permute-done.6.rest_7_
  32.0 0.1 copy-done.4
  32.0 0.0 copy-done.5
  32.0 2.6 %tower_out.1 = (bf16[32,512]{1,0:T(8,128)(2,1)S(1)}, bf16[32,512]{1,0:T(8,128)(2,1)S(1)}, bf16[32,512]{1,0:T(8,128)(2,1)S(1)}, bf16[32,512]{1,0:T(8,128)(2,1)S(1)}) custom-call(f32[128,512]{1,0:T(8,128)S(1)} %low_part.9.low_ref, bf16[4096,512]{1,0:T(8,128)(2,1)S(1)} %bitcast.17, bf16[512,4096]{1,0:T(8,128)(2,1)S(1)} %bitcast.19, f32[1,4096]{1,0:T(1,128)S(1)} %bitcast.22, ...), custom_call_target="tpu_custom_call" | custom-call | flops 1073741824 | tf_op jit(solution)/shard_map/tower_out/pallas_call | solution.py:228
  34.6 0.1 collective-permute-start.7
  34.7 1.6 %collective-permute-start.8 = (bf16[32,512]{1,0:T(8,128)(2,1)S(1)}, bf16[32,512]{1,0:T(8,128)(2,1)S(1)}, u32[]{:S(2)}, u32[]{:S(2)}) collective-permute-start(bf16[32,512]{1,0:T(8,128)(2,1)S(1)} %get-tuple-element.33), channel_id=1, source_target_pairs={{0,16},{8,24},{16,0},{24,8},{1,17},{9,25},{17,1},{25,9},{2,18},{10... | collective-permute-start | bytes 98312 | tf_op jit(solution)/shard_map/ppermute | solution.py:280
  36.3 0.3 collective-permute-start.9
  36.5 0.0 collective-permute-done.7.rest_1_
  36.6 2.1 %collective-permute-done.8.rest_2_ = bf16[32,512]{1,0:T(8,128)(2,1)S(1)} collective-permute-done((bf16[32,512]{1,0:T(8,128)(2,1)S(1)}, bf16[32,512]{1,0:T(8,128)(2,1)S(1)}, u32[]{:S(2)}, u32[]{:S(2)}) %collective-permute-start.8) | collective-permute-done | bytes 32800 | tf_op jit(solution)/shard_map/ppermute | solution.py:280
  38.7 0.9 %collective-permute-done.9.rest_3_ = bf16[32,512]{1,0:T(8,128)(2,1)S(1)} collective-permute-done((bf16[32,512]{1,0:T(8,128)(2,1)S(1)}, bf16[32,512]{1,0:T(8,128)(2,1)S(1)}, u32[]{:S(2)}, u32[]{:S(2)}) %collective-permute-start.9) | collective-permute-done | bytes 32800 | tf_op jit(solution)/shard_map/ppermute | solution.py:280
  39.6 0.9 %gram_pairs.1 = f32[6,32]{1,0:T(8,128)} custom-call(bf16[32,512]{1,0:T(8,128)(2,1)S(1)} %get-tuple-element.31.rest_0_, bf16[32,512]{1,0:T(8,128)(2,1)S(1)} %collective-permute-done.7.rest_1_, bf16[32,512]{1,0:T(8,128)(2,1)S(1)} %collective-permute-done.8.rest_2_, bf16[32,512]{1,0:T(8,128)(2,1)S(1)} %collective-permute-done.9.rest_3_), custom_call_target="tpu_custom_call" | custom-call | tf_op jit(solution)/shard_map/gram_pairs/pallas_call | solution.py:267
Async XLA Ops:
  0.0 21.4 %copy-start = (bf16[1,1,4096,512]{3,2,1,0:T(8,128)(2,1)S(1)}, bf16[1,1,4096,512]{3,2,1,0:T(8,128)(2,1)}, u32[]{:S(2)}) copy-start(bf16[1,1,4096,512]{3,2,1,0:T(8,128)(2,1)} %param.11) | copy-start | bytes 12582916
  3.3 16.2 %collective-permute-start.4 = (bf16[128,512]{1,0:T(8,128)(2,1)}, bf16[128,512]{1,0:T(8,128)(2,1)S(1)}, u32[]{:S(2)}, u32[]{:S(2)}) collective-permute-start(bf16[128,512]{1,0:T(8,128)(2,1)} %get-tuple-element.23.after_ref), channel_id=1, source_target_pairs={{0,4},{1,5},{2,6},{3,7},{4,0},{5,1},{6,2},{7,3},{8,12},{9,13},{10,... | collective-permute-start | bytes 393224 | tf_op jit(solution)/shard_map/ppermute | solution.py:280
  7.4 15.9 %copy-start.2 = (bf16[1,4096,512]{2,1,0:T(8,128)(2,1)S(1)}, bf16[1,4096,512]{2,1,0:T(8,128)(2,1)}, u32[]{:S(2)}) copy-start(bf16[1,4096,512]{2,1,0:T(8,128)(2,1)} %param.14) | copy-start | bytes 12582916
  10.3 13.0 %copy-start.1 = (bf16[1,1,512,4096]{3,2,1,0:T(8,128)(2,1)S(1)}, bf16[1,1,512,4096]{3,2,1,0:T(8,128)(2,1)}, u32[]{:S(2)}) copy-start(bf16[1,1,512,4096]{3,2,1,0:T(8,128)(2,1)} %param.12) | copy-start | bytes 12582916
  10.3 21.0 %collective-permute-start.1 = (bf16[128,512]{1,0:T(8,128)(2,1)}, bf16[128,512]{1,0:T(8,128)(2,1)S(1)}, u32[]{:S(2)}, u32[]{:S(2)}) collective-permute-start(bf16[128,512]{1,0:T(8,128)(2,1)} %get-tuple-element.24.after_ref), channel_id=1, source_target_pairs={{0,6},{1,7},{2,4},{3,5},{4,2},{5,3},{6,0},{7,1},{8,14},{9,15},{10,... | collective-permute-start | bytes 393224 | tf_op jit(solution)/shard_map/ppermute | solution.py:280
  11.7 10.0 %collective-permute-start.3 = (bf16[128,512]{1,0:T(8,128)(2,1)}, bf16[128,512]{1,0:T(8,128)(2,1)S(1)}, u32[]{:S(2)}, u32[]{:S(2)}) collective-permute-start(bf16[128,512]{1,0:T(8,128)(2,1)} %get-tuple-element.28), channel_id=1, source_target_pairs={{0,3},{1,2},{2,1},{3,0},{4,7},{5,6},{6,5},{7,4},{8,11},{9,10},{10,... | collective-permute-start | bytes 393224 | tf_op jit(solution)/shard_map/ppermute | solution.py:280
  16.1 5.6 %copy-start.6 = (bf16[128,512]{1,0:T(8,128)(2,1)S(1)}, bf16[128,512]{1,0:T(8,128)(2,1)}, u32[]{:S(2)}) copy-start(bf16[128,512]{1,0:T(8,128)(2,1)} %get-tuple-element.30) | copy-start | bytes 393220
  16.1 15.5 %collective-permute-start = (bf16[128,512]{1,0:T(8,128)(2,1)}, bf16[128,512]{1,0:T(8,128)(2,1)S(1)}, u32[]{:S(2)}, u32[]{:S(2)}) collective-permute-start(bf16[128,512]{1,0:T(8,128)(2,1)} %get-tuple-element.26), channel_id=1, source_target_pairs={{0,2},{1,3},{2,0},{3,1},{4,6},{5,7},{6,4},{7,5},{8,10},{9,11},{10,... | collective-permute-start | bytes 393224 | tf_op jit(solution)/shard_map/ppermute | solution.py:280
  17.9 13.2 %collective-permute-start.2 = (bf16[128,512]{1,0:T(8,128)(2,1)}, bf16[128,512]{1,0:T(8,128)(2,1)S(1)}, u32[]{:S(2)}, u32[]{:S(2)}) collective-permute-start(bf16[128,512]{1,0:T(8,128)(2,1)} %get-tuple-element.27), channel_id=1, source_target_pairs={{0,5},{1,4},{2,7},{3,6},{4,1},{5,0},{6,3},{7,2},{8,13},{9,12},{10,... | collective-permute-start | bytes 393224 | tf_op jit(solution)/shard_map/ppermute | solution.py:280
  19.5 12.4 %collective-permute-start.5 = (bf16[128,512]{1,0:T(8,128)(2,1)}, bf16[128,512]{1,0:T(8,128)(2,1)S(1)}, u32[]{:S(2)}, u32[]{:S(2)}) collective-permute-start(bf16[128,512]{1,0:T(8,128)(2,1)} %get-tuple-element.29), channel_id=1, source_target_pairs={{0,7},{1,6},{2,5},{3,4},{4,3},{5,2},{6,1},{7,0},{8,15},{9,14},{10,... | collective-permute-start | bytes 393224 | tf_op jit(solution)/shard_map/ppermute | solution.py:280
  21.7 10.3 %collective-permute-start.6 = (bf16[128,512]{1,0:T(8,128)(2,1)S(1)}, bf16[128,512]{1,0:T(8,128)(2,1)S(1)}, u32[]{:S(2)}, u32[]{:S(2)}) collective-permute-start(bf16[128,512]{1,0:T(8,128)(2,1)S(1)} %copy-done.6), channel_id=1, source_target_pairs={{0,1},{1,0},{2,3},{3,2},{4,5},{5,4},{6,7},{7,6},{8,9},{9,8},{10,11... | collective-permute-start | bytes 393224 | tf_op jit(solution)/shard_map/ppermute | solution.py:280
  23.5 8.1 %copy-start.3 = (bf16[128,512]{1,0:T(8,128)(2,1)S(1)}, bf16[128,512]{1,0:T(8,128)(2,1)}, u32[]{:S(2)}) copy-start(bf16[128,512]{1,0:T(8,128)(2,1)} %get-tuple-element.25.rest_0_) | copy-start | bytes 393220
  31.3 0.7 %copy-start.4 = (f32[1,1,4096]{2,1,0:T(1,128)S(1)}, f32[1,1,4096]{2,1,0:T(1,128)}, u32[]{:S(2)}) copy-start(f32[1,1,4096]{2,1,0:T(1,128)} %param.13) | copy-start | bytes 49156
  31.3 0.7 %copy-start.5 = (f32[1,512]{1,0:T(1,128)S(1)}, f32[1,512]{1,0:T(1,128)}, u32[]{:S(2)}) copy-start(f32[1,512]{1,0:T(1,128)} %pb_ref.1) | copy-start | bytes 6148
  34.6 1.9 %collective-permute-start.7 = (bf16[32,512]{1,0:T(8,128)(2,1)S(1)}, bf16[32,512]{1,0:T(8,128)(2,1)S(1)}, u32[]{:S(2)}, u32[]{:S(2)}) collective-permute-start(bf16[32,512]{1,0:T(8,128)(2,1)S(1)} %get-tuple-element.32), channel_id=1, source_target_pairs={{0,8},{8,0},{16,24},{24,16},{1,9},{9,1},{17,25},{25,17},{2,10},{10... | collective-permute-start | bytes 98312 | tf_op jit(solution)/shard_map/ppermute | solution.py:280
  34.7 4.0 %collective-permute-start.8 = (bf16[32,512]{1,0:T(8,128)(2,1)S(1)}, bf16[32,512]{1,0:T(8,128)(2,1)S(1)}, u32[]{:S(2)}, u32[]{:S(2)}) collective-permute-start(bf16[32,512]{1,0:T(8,128)(2,1)S(1)} %get-tuple-element.33), channel_id=1, source_target_pairs={{0,16},{8,24},{16,0},{24,8},{1,17},{9,25},{17,1},{25,9},{2,18},{10... | collective-permute-start | bytes 98312 | tf_op jit(solution)/shard_map/ppermute | solution.py:280
  36.3 3.3 %collective-permute-start.9 = (bf16[32,512]{1,0:T(8,128)(2,1)S(1)}, bf16[32,512]{1,0:T(8,128)(2,1)S(1)}, u32[]{:S(2)}, u32[]{:S(2)}) collective-permute-start(bf16[32,512]{1,0:T(8,128)(2,1)S(1)} %get-tuple-element.34), channel_id=1, source_target_pairs={{0,24},{8,16},{16,8},{24,0},{1,25},{9,17},{17,9},{25,1},{2,26},{10... | collective-permute-start | bytes 98312 | tf_op jit(solution)/shard_map/ppermute | solution.py:280

commit v3 on v2

--- a/solution.py
+++ b/solution.py
@@ -11,6 +11,7 @@
 LANES = 128
 MIB = 1 << 20
 BATCH = 512
+SPLIT = 256
 ANY = pl.BlockSpec(memory_space=pl.ANY)
 VMEM = pl.BlockSpec(memory_space=pltpu.VMEM)
 
@@ -83,7 +84,7 @@
 
 
 def first_kernel(
-    k, block, towers, ids_hbm, len_hbm, tab_hbm, out_hbm, ids_ref, len_ref, tab_ref, buf, sems
+    k, block, towers, ids_hbm, len_hbm, tab_hbm, out_ref, ids_ref, len_ref, tab_ref, sems
 ):
     per = LANES // block
     feats, slots, _ = ids_ref.shape
@@ -103,15 +104,9 @@
     dest = lax.rem(lax.axis_index("dev"), per) ^ k % per
     columns = bag_columns(tiles, dest, block)
     columns = jnp.concatenate(columns, axis=0) if len(columns) > 1 else columns[0]
-    sent = []
     for f in range(feats):
         rows[f].wait()
-        at = pl.ds(f * width, width)
-        buf[:, at] = pool_rows(columns, f, slots, tab_ref[f])
-        sent.append(pltpu.make_async_copy(buf.at[:, at], out_hbm.at[:, at], sems.at[2 + feats + f]))
-        sent[-1].start()
-    for copy in sent:
-        copy.wait()
+        out_ref[:, f * width : (f + 1) * width] = pool_rows(columns, f, slots, tab_ref[f])
 
 
 def pool_first(ids, lens, tables, k, block, towers):
@@ -120,17 +115,14 @@
     return pl.pallas_call(
         functools.partial(first_kernel, k, block, towers),
         in_specs=[ANY, ANY, ANY],
-        out_specs=[ANY, VMEM, VMEM, VMEM],
+        out_specs=[VMEM, VMEM, VMEM, VMEM],
         out_shape=[
-            pltpu.HBM((towers * block, depth), jnp.bfloat16),
+            pltpu.VMEM((towers * block, depth), jnp.bfloat16),
             jax.ShapeDtypeStruct(ids.shape, ids.dtype),
             jax.ShapeDtypeStruct(lens.shape, lens.dtype),
             jax.ShapeDtypeStruct(tables.shape, tables.dtype),
         ],
-        scratch_shapes=[
-            pltpu.VMEM((towers * block, depth), jnp.bfloat16),
-            pltpu.SemaphoreType.DMA((2 + 2 * feats,)),
-        ],
+        scratch_shapes=[pltpu.SemaphoreType.DMA((2 + feats,))],
         compiler_params=pltpu.CompilerParams(vmem_limit_bytes=16 * MIB),
         name="pool_first",
     )(ids, lens, tables)
@@ -202,21 +194,21 @@
     chunks, outs, scratch = rest[: -towers - 1], rest[-towers - 1 : -1], rest[-1]
     depth = chunks[0].shape[1]
     block = outs[0].shape[0]
-    chunks = [
-        (pl.ds(pl.multiple_of((lax.axis_index("dev") ^ k) * depth, depth), depth), chunk)
-        for k, chunk in zip(ks, chunks, strict=True)
-    ]
     low = low_ref[...]
-    for at, chunk in chunks[-late:]:
+    for k, chunk in list(zip(ks, chunks, strict=True))[-late:]:
+        at = pl.ds(pl.multiple_of((lax.axis_index("dev") ^ k) * depth, depth), depth)
         low += jnp.dot(chunk[...], down_ref[at, :], preferred_element_type=jnp.float32)
     low = low.astype(jnp.bfloat16)
     total = pb_ref[...]
-    for at, chunk in chunks:
-        high = jnp.dot(low, up_ref[:, at], preferred_element_type=jnp.float32)
-        high = high + bias_ref[:, at]
-        base = chunk[...].astype(jnp.float32)
-        cross = (base * high + base).astype(jnp.bfloat16)
-        total = total + jnp.dot(cross, proj_ref[at, :], preferred_element_type=jnp.float32)
+    for k, chunk in zip(ks, chunks, strict=True):
+        for first in range(0, depth, SPLIT):
+            start = (lax.axis_index("dev") ^ k) * depth + first
+            at = pl.ds(pl.multiple_of(start, SPLIT), SPLIT)
+            high = jnp.dot(low, up_ref[:, at], preferred_element_type=jnp.float32)
+            high = high + bias_ref[:, at]
+            base = chunk[:, first : first + SPLIT].astype(jnp.float32)
+            cross = (base * high + base).astype(jnp.bfloat16)
+            total = total + jnp.dot(cross, proj_ref[at, :], preferred_element_type=jnp.float32)
     scratch[...] = total.astype(jnp.bfloat16)
     for k, out in enumerate(outs):
         out[...] = scratch[pl.ds(pl.multiple_of((lax.axis_index("tower") ^ k) * block, block), block), :]
@@ -229,7 +221,7 @@
         functools.partial(tower_kernel, ks, late, towers),
         in_specs=[VMEM] * (6 + len(chunks)),
         out_specs=[VMEM] * towers,
-        out_shape=[shape] * towers,
+        out_shape=[shape] + [pltpu.VMEM(shape.shape, shape.dtype)] * (towers - 1),
         scratch_shapes=[pltpu.VMEM((rows, proj.shape[1]), jnp.bfloat16)],
         compiler_params=pltpu.CompilerParams(vmem_limit_bytes=16 * MIB),
         cost_estimate=pl.CostEstimate(
@@ -293,7 +285,7 @@
     fixed = [ids, lens, tables[0], cross_down[0, 0], cross_up[0, 0], proj_weight[0]]
     ids, lens, rows, *weights = (pltpu.with_memory_space_constraint(w, pltpu.HBM) for w in fixed)
     down, up, proj = (pltpu.with_memory_space_constraint(w, pltpu.VMEM) for w in weights)
-    far, near = list(range(per, members)), list(range(per - 1, 0, -1))
+    far, near = list(range(per, members)), [1] + list(range(per - 1, 1, -1))
     order = far[:1] + near[:1] + far[1:-1] + near[1:-1] + far[-1:] + near[-1:]
     pooled, got = {}, {}
     pooled[far[0]], ids, lens, rows = pool_first(ids, lens, rows, far[0], block, towers)
@@ -310,8 +302,8 @@
         got[k] = swap(pooled[k], "dev", k)
     got[0] = pooled[0]
     low = []
-    for some in [[k] for k in order[: len(far)]] + [[0] + near[1:-1]]:
-        held = (up, proj) if some == near[:1] else ()
+    for i, some in enumerate([far[:1],near[:1],far[1:-1]+[0]+near[1:-1]]):
+        held = (up, proj) if i == 1 else ()
         low = [low_part(down, [got[k] for k in some], some, low, held)]
     ks = [0] + order
     outs = tower_out(low[0], down, up, bias, proj, proj_bias, [got[k] for k in ks], ks, 2, towers)

time: 40.6 us -> 37.9 us (0.933)
  Pallas kernels: 14 us -> 12.2 us
  starting transfers between devices: 15.6 us -> 14.6 us
    ppermute x10, starting transfers between devices: 15.6 us -> 14.6 us  [swap(): return lax.ppermute(x, axis, [(i, i ^ k) for i in range(size)])]
    pallas_call x1, Pallas kernels: 2.57 us -> 1.76 us  [tower_out(): pl.pallas_call(functools.partial(tower_kernel, ks, late, towers), in_spec...]
    pallas_call x1, Pallas kernels: 3.3 us -> 2.66 us  [pool_first(): pl.pallas_call(functools.partial(first_kernel, k, block, towers), in_spec...]
    pallas_call x5 -> x3, Pallas kernels: 1.25 us -> 0.91 us  [low_part(): pl.pallas_call(functools.partial(low_kernel, ks, len(held)), in_specs=[VM...]
  transfers between devices with their start and end apart: 10 -> 10, of which waited for: 3 -> 4; matrix products, arithmetic and copies ran while one was open for 0% -> 0% of each run, Pallas kernels for 18% -> 18%
where the time goes in v3:
time: 37.9 us; the launch traced here: 37.7 us
  starting transfers between devices  14.6 us (39%)
  Pallas kernels  12.2 us (32%)
  waiting for transfers between devices  10.8 us (28%)
    ppermute x10, starting transfers between devices, swap(): return lax.ppermute(x, axis, [(i, i ^ k) for i in range(size)])  14.6 us
    ppermute x10, waiting for transfers between devices, swap(): return lax.ppermute(x, axis, [(i, i ^ k) for i in range(size)])  10.8 us
    pallas_call x2, Pallas kernels, pool_more(): pl.pallas_call(functools.partial(more_kernel, ks, block, towers), in_spec...  5.96 us
    pallas_call x1, Pallas kernels, pool_first(): pl.pallas_call(functools.partial(first_kernel, k, block, towers), in_spec...  2.66 us
    pallas_call x1, Pallas kernels, tower_out(): pl.pallas_call(functools.partial(tower_kernel, ks, late, towers), in_spec...  1.76 us
    pallas_call x3, Pallas kernels, low_part(): pl.pallas_call(functools.partial(low_kernel, ks, len(held)), in_specs=[VM...  0.91 us
    pallas_call x1, Pallas kernels, gram_pairs(): pl.pallas_call(gram_kernel, in_specs=[VMEM] * towers, out_specs=VMEM, out...  0.87 us
  transfers between devices with their start and end apart: 10, of which 4 were waited for; matrix products, arithmetic and copies ran while one was open for 0% of the time, Pallas kernels for 18%

profile of v3, /device:TPU:0, one launch (start us, length us, event | category | flops | bytes accessed | tf_op | source)
XLA Modules:
  0.0 37.7 jit_solution(12772650326735701692)
XLA Ops:
  0.0 0.0 copy-start
  0.0 2.7 %pool_first.1 = (bf16[128,512]{1,0:T(8,128)(2,1)S(1)}, s32[4,4,1024]{2,1,0:T(4,128)S(1)}, s32[4,1024]{1,0:T(4,128)S(1)}, bf16[4,1024,128]{2,1,0:T(8,128)(2,1)S(1)}) custom-call(s32[4,4,1024]{2,1,0:T(4,128)} %bitcast.22, s32[4,1024]{1,0:T(4,128)} %bitcast.23, bf16[4,1024,128]{2,1,0:T(8,128)(2,1)} %bitcast.21), custom_call_target="tpu_custom_call" | custom-call | tf_op jit(solution)/shard_map/pool_first/pallas_call | solution.py:115
  2.7 0.0 copy-start.6
  2.7 4.1 %collective-permute-start.4 = (bf16[128,512]{1,0:T(8,128)(2,1)S(1)}, bf16[128,512]{1,0:T(8,128)(2,1)S(1)}, u32[]{:S(2)}, u32[]{:S(2)}) collective-permute-start(bf16[128,512]{1,0:T(8,128)(2,1)S(1)} %get-tuple-element.23.after_ref), channel_id=1, source_target_pairs={{0,4},{1,5},{2,6},{3,7},{4,0},{5,1},{6,2},{7,3},{8,12},{9,13},{10,... | collective-permute-start | bytes 393224 | tf_op jit(solution)/shard_map/ppermute | solution.py:272
  6.8 0.0 copy-done.6
  6.8 0.0 copy-start.2
  6.8 2.8 %pool_more.2 = (bf16[128,512]{1,0:T(8,128)(2,1)}, bf16[128,512]{1,0:T(8,128)(2,1)}, bf16[128,512]{1,0:T(8,128)(2,1)}) custom-call(s32[4,4,1024]{2,1,0:T(4,128)S(1)} %get-tuple-element.20.ids_ref, s32[4,1024]{1,0:T(4,128)S(1)} %get-tuple-element.21.len_ref, bf16[4,1024,128]{2,1,0:T(8,128)(2,1)S(1)} %get-tuple-element.22.tab_ref, bf16[128,512]{1,0:T(8,128)(2,1)} %copy-done.6), custom_call_target="tpu_custom_call" | custom-call | flops 1000000000 | tf_op jit(solution)/shard_map/pool_more/pallas_call | solution.py:153
  9.6 0.0 copy-start.1
  9.7 1.6 %collective-permute-start.3 = (bf16[128,512]{1,0:T(8,128)(2,1)}, bf16[128,512]{1,0:T(8,128)(2,1)S(1)}, u32[]{:S(2)}, u32[]{:S(2)}) collective-permute-start(bf16[128,512]{1,0:T(8,128)(2,1)} %get-tuple-element.28), channel_id=1, source_target_pairs={{0,1},{1,0},{2,3},{3,2},{4,5},{5,4},{6,7},{7,6},{8,9},{9,8},{10,11... | collective-permute-start | bytes 393224 | tf_op jit(solution)/shard_map/ppermute | solution.py:272
  11.2 1.6 %collective-permute-start.1 = (bf16[128,512]{1,0:T(8,128)(2,1)}, bf16[128,512]{1,0:T(8,128)(2,1)S(1)}, u32[]{:S(2)}, u32[]{:S(2)}) collective-permute-start(bf16[128,512]{1,0:T(8,128)(2,1)} %get-tuple-element.25.after_ref), channel_id=1, source_target_pairs={{0,6},{1,7},{2,4},{3,5},{4,2},{5,3},{6,0},{7,1},{8,14},{9,15},{10,... | collective-permute-start | bytes 393224 | tf_op jit(solution)/shard_map/ppermute | solution.py:272
  12.8 3.1 %pool_more.3 = (bf16[128,512]{1,0:T(8,128)(2,1)}, bf16[128,512]{1,0:T(8,128)(2,1)}, bf16[128,512]{1,0:T(8,128)(2,1)}, bf16[128,512]{1,0:T(8,128)(2,1)}) custom-call(s32[4,4,1024]{2,1,0:T(4,128)S(1)} %get-tuple-element.20.ids_ref, s32[4,1024]{1,0:T(4,128)S(1)} %get-tuple-element.21.len_ref, bf16[4,1024,128]{2,1,0:T(8,128)(2,1)S(1)} %get-tuple-element.22.tab_ref, ...), custom_call_target="tpu_custom_call" | custom-call | flops 1000000000 | tf_op jit(solution)/shard_map/pool_more/pallas_call | solution.py:153
  15.9 0.0 copy-start.7
  15.9 0.1 collective-permute-start.2
  16.0 3.7 %collective-permute-start = (bf16[128,512]{1,0:T(8,128)(2,1)}, bf16[128,512]{1,0:T(8,128)(2,1)S(1)}, u32[]{:S(2)}, u32[]{:S(2)}) collective-permute-start(bf16[128,512]{1,0:T(8,128)(2,1)} %get-tuple-element.24), channel_id=1, source_target_pairs={{0,5},{1,4},{2,7},{3,6},{4,1},{5,0},{6,3},{7,2},{8,13},{9,12},{10,... | collective-permute-start | bytes 393224 | tf_op jit(solution)/shard_map/ppermute | solution.py:272
  19.7 0.0 collective-permute-done.4.rest_0_.rest_1_
  19.7 1.5 %collective-permute-start.5 = (bf16[128,512]{1,0:T(8,128)(2,1)}, bf16[128,512]{1,0:T(8,128)(2,1)S(1)}, u32[]{:S(2)}, u32[]{:S(2)}) collective-permute-start(bf16[128,512]{1,0:T(8,128)(2,1)} %get-tuple-element.29), channel_id=1, source_target_pairs={{0,7},{1,6},{2,5},{3,4},{4,3},{5,2},{6,1},{7,0},{8,15},{9,14},{10,... | collective-permute-start | bytes 393224 | tf_op jit(solution)/shard_map/ppermute | solution.py:272
  21.2 0.0 copy-done
  21.2 0.2 low_part.3.rest_1_
  21.5 0.0 collective-permute-done.3.rest_0_.rest_2_
  21.5 0.0 copy-done.7
  21.5 0.1 collective-permute-start.6
  21.6 0.0 copy-done.2
  21.6 0.0 copy-done.1
  21.6 0.0 copy-start.3
  21.6 0.2 low_part.4.rest_4_
  21.9 0.0 copy-start.4
  21.9 0.0 copy-start.5
  21.9 1.9 %collective-permute-done.2.rest_3_.rest_5_ = bf16[128,512]{1,0:T(8,128)(2,1)S(1)} collective-permute-done((bf16[128,512]{1,0:T(8,128)(2,1)}, bf16[128,512]{1,0:T(8,128)(2,1)S(1)}, u32[]{:S(2)}, u32[]{:S(2)}) %collective-permute-start.2) | collective-permute-done | bytes 131104 | tf_op jit(solution)/shard_map/ppermute | solution.py:272
  23.8 0.0 collective-permute-done.1.rest_1_.rest_4_
  23.8 5.8 %collective-permute-done.rest_0_.rest_3_ = bf16[128,512]{1,0:T(8,128)(2,1)S(1)} collective-permute-done((bf16[128,512]{1,0:T(8,128)(2,1)}, bf16[128,512]{1,0:T(8,128)(2,1)S(1)}, u32[]{:S(2)}, u32[]{:S(2)}) %collective-permute-start) | collective-permute-done | bytes 131104 | tf_op jit(solution)/shard_map/ppermute | solution.py:272
  29.6 0.0 copy-done.3
  29.6 0.4 %low_part.5.low_ref = f32[128,512]{1,0:T(8,128)S(1)} custom-call(bf16[4096,512]{1,0:T(8,128)(2,1)S(1)} %bitcast.14, bf16[128,512]{1,0:T(8,128)(2,1)S(1)} %collective-permute-done.rest_0_.rest_3_, bf16[128,512]{1,0:T(8,128)(2,1)S(1)} %collective-permute-done.1.rest_1_.rest_4_, bf16[128,512]{1,0:T(8,128)(2,1)S(1)} %copy-done.3, ...), custom_call_target="tpu_custom_call" | custom-call | flops 1000000000 | tf_op jit(solution)/shard_map/low_part/pallas_call | solution.py:180
  30.0 0.0 collective-permute-done.5.rest_6_
  30.1 0.0 collective-permute-done.6.rest_7_
  30.1 0.0 copy-done.4
  30.1 0.0 copy-done.5
  30.1 1.8 %tower_out.1 = (bf16[32,512]{1,0:T(8,128)(2,1)S(1)}, bf16[32,512]{1,0:T(8,128)(2,1)S(1)}, bf16[32,512]{1,0:T(8,128)(2,1)S(1)}, bf16[32,512]{1,0:T(8,128)(2,1)S(1)}) custom-call(f32[128,512]{1,0:T(8,128)S(1)} %low_part.5.low_ref, bf16[4096,512]{1,0:T(8,128)(2,1)S(1)} %bitcast.15, bf16[512,4096]{1,0:T(8,128)(2,1)S(1)} %bitcast.17, f32[1,4096]{1,0:T(1,128)S(1)} %bitcast.20, ...), custom_call_target="tpu_custom_call" | custom-call | flops 1073741824 | tf_op jit(solution)/shard_map/tower_out/pallas_call | solution.py:220
  31.9 0.1 collective-permute-start.7
  31.9 1.6 %collective-permute-start.8 = (bf16[32,512]{1,0:T(8,128)(2,1)S(1)}, bf16[32,512]{1,0:T(8,128)(2,1)S(1)}, u32[]{:S(2)}, u32[]{:S(2)}) collective-permute-start(bf16[32,512]{1,0:T(8,128)(2,1)S(1)} %get-tuple-element.33), channel_id=1, source_target_pairs={{0,16},{8,24},{16,0},{24,8},{1,17},{9,25},{17,1},{25,9},{2,18},{10... | collective-permute-start | bytes 98312 | tf_op jit(solution)/shard_map/ppermute | solution.py:272
  33.5 0.3 collective-permute-start.9
  33.8 0.0 collective-permute-done.7.rest_1_
  33.8 2.1 %collective-permute-done.8.rest_2_ = bf16[32,512]{1,0:T(8,128)(2,1)S(1)} collective-permute-done((bf16[32,512]{1,0:T(8,128)(2,1)S(1)}, bf16[32,512]{1,0:T(8,128)(2,1)S(1)}, u32[]{:S(2)}, u32[]{:S(2)}) %collective-permute-start.8) | collective-permute-done | bytes 32800 | tf_op jit(solution)/shard_map/ppermute | solution.py:272
  35.9 1.0 %collective-permute-done.9.rest_3_ = bf16[32,512]{1,0:T(8,128)(2,1)S(1)} collective-permute-done((bf16[32,512]{1,0:T(8,128)(2,1)S(1)}, bf16[32,512]{1,0:T(8,128)(2,1)S(1)}, u32[]{:S(2)}, u32[]{:S(2)}) %collective-permute-start.9) | collective-permute-done | bytes 32800 | tf_op jit(solution)/shard_map/ppermute | solution.py:272
  36.9 0.9 %gram_pairs.1 = f32[6,32]{1,0:T(8,128)} custom-call(bf16[32,512]{1,0:T(8,128)(2,1)S(1)} %get-tuple-element.31.rest_0_, bf16[32,512]{1,0:T(8,128)(2,1)S(1)} %collective-permute-done.7.rest_1_, bf16[32,512]{1,0:T(8,128)(2,1)S(1)} %collective-permute-done.8.rest_2_, bf16[32,512]{1,0:T(8,128)(2,1)S(1)} %collective-permute-done.9.rest_3_), custom_call_target="tpu_custom_call" | custom-call | tf_op jit(solution)/shard_map/gram_pairs/pallas_call | solution.py:259
Async XLA Ops:
  0.0 21.2 %copy-start = (bf16[1,1,4096,512]{3,2,1,0:T(8,128)(2,1)S(1)}, bf16[1,1,4096,512]{3,2,1,0:T(8,128)(2,1)}, u32[]{:S(2)}) copy-start(bf16[1,1,4096,512]{3,2,1,0:T(8,128)(2,1)} %param.11) | copy-start | bytes 12582916
  2.7 4.1 %copy-start.6 = (bf16[128,512]{1,0:T(8,128)(2,1)}, bf16[128,512]{1,0:T(8,128)(2,1)S(1)}, u32[]{:S(2)}) copy-start(bf16[128,512]{1,0:T(8,128)(2,1)S(1)} %get-tuple-element.23.after_ref) | copy-start | bytes 393220
  2.7 17.0 %collective-permute-start.4 = (bf16[128,512]{1,0:T(8,128)(2,1)S(1)}, bf16[128,512]{1,0:T(8,128)(2,1)S(1)}, u32[]{:S(2)}, u32[]{:S(2)}) collective-permute-start(bf16[128,512]{1,0:T(8,128)(2,1)S(1)} %get-tuple-element.23.after_ref), channel_id=1, source_target_pairs={{0,4},{1,5},{2,6},{3,7},{4,0},{5,1},{6,2},{7,3},{8,12},{9,13},{10,... | collective-permute-start | bytes 393224 | tf_op jit(solution)/shard_map/ppermute | solution.py:272
  6.8 14.8 %copy-start.2 = (bf16[1,4096,512]{2,1,0:T(8,128)(2,1)S(1)}, bf16[1,4096,512]{2,1,0:T(8,128)(2,1)}, u32[]{:S(2)}) copy-start(bf16[1,4096,512]{2,1,0:T(8,128)(2,1)} %param.14) | copy-start | bytes 12582916
  9.6 11.9 %copy-start.1 = (bf16[1,1,512,4096]{3,2,1,0:T(8,128)(2,1)S(1)}, bf16[1,1,512,4096]{3,2,1,0:T(8,128)(2,1)}, u32[]{:S(2)}) copy-start(bf16[1,1,512,4096]{3,2,1,0:T(8,128)(2,1)} %param.12) | copy-start | bytes 12582916
  9.7 11.8 %collective-permute-start.3 = (bf16[128,512]{1,0:T(8,128)(2,1)}, bf16[128,512]{1,0:T(8,128)(2,1)S(1)}, u32[]{:S(2)}, u32[]{:S(2)}) collective-permute-start(bf16[128,512]{1,0:T(8,128)(2,1)} %get-tuple-element.28), channel_id=1, source_target_pairs={{0,1},{1,0},{2,3},{3,2},{4,5},{5,4},{6,7},{7,6},{8,9},{9,8},{10,11... | collective-permute-start | bytes 393224 | tf_op jit(solution)/shard_map/ppermute | solution.py:272
  11.2 12.6 %collective-permute-start.1 = (bf16[128,512]{1,0:T(8,128)(2,1)}, bf16[128,512]{1,0:T(8,128)(2,1)S(1)}, u32[]{:S(2)}, u32[]{:S(2)}) collective-permute-start(bf16[128,512]{1,0:T(8,128)(2,1)} %get-tuple-element.25.after_ref), channel_id=1, source_target_pairs={{0,6},{1,7},{2,4},{3,5},{4,2},{5,3},{6,0},{7,1},{8,14},{9,15},{10,... | collective-permute-start | bytes 393224 | tf_op jit(solution)/shard_map/ppermute | solution.py:272
  15.9 5.6 %copy-start.7 = (bf16[128,512]{1,0:T(8,128)(2,1)S(1)}, bf16[128,512]{1,0:T(8,128)(2,1)}, u32[]{:S(2)}) copy-start(bf16[128,512]{1,0:T(8,128)(2,1)} %get-tuple-element.30) | copy-start | bytes 393220
  15.9 7.9 %collective-permute-start.2 = (bf16[128,512]{1,0:T(8,128)(2,1)}, bf16[128,512]{1,0:T(8,128)(2,1)S(1)}, u32[]{:S(2)}, u32[]{:S(2)}) collective-permute-start(bf16[128,512]{1,0:T(8,128)(2,1)} %get-tuple-element.27), channel_id=1, source_target_pairs={{0,3},{1,2},{2,1},{3,0},{4,7},{5,6},{6,5},{7,4},{8,11},{9,10},{10,... | collective-permute-start | bytes 393224 | tf_op jit(solution)/shard_map/ppermute | solution.py:272
  16.0 13.6 %collective-permute-start = (bf16[128,512]{1,0:T(8,128)(2,1)}, bf16[128,512]{1,0:T(8,128)(2,1)S(1)}, u32[]{:S(2)}, u32[]{:S(2)}) collective-permute-start(bf16[128,512]{1,0:T(8,128)(2,1)} %get-tuple-element.24), channel_id=1, source_target_pairs={{0,5},{1,4},{2,7},{3,6},{4,1},{5,0},{6,3},{7,2},{8,13},{9,12},{10,... | collective-permute-start | bytes 393224 | tf_op jit(solution)/shard_map/ppermute | solution.py:272
  19.7 10.4 %collective-permute-start.5 = (bf16[128,512]{1,0:T(8,128)(2,1)}, bf16[128,512]{1,0:T(8,128)(2,1)S(1)}, u32[]{:S(2)}, u32[]{:S(2)}) collective-permute-start(bf16[128,512]{1,0:T(8,128)(2,1)} %get-tuple-element.29), channel_id=1, source_target_pairs={{0,7},{1,6},{2,5},{3,4},{4,3},{5,2},{6,1},{7,0},{8,15},{9,14},{10,... | collective-permute-start | bytes 393224 | tf_op jit(solution)/shard_map/ppermute | solution.py:272
  21.5 8.6 %collective-permute-start.6 = (bf16[128,512]{1,0:T(8,128)(2,1)S(1)}, bf16[128,512]{1,0:T(8,128)(2,1)S(1)}, u32[]{:S(2)}, u32[]{:S(2)}) collective-permute-start(bf16[128,512]{1,0:T(8,128)(2,1)S(1)} %copy-done.7), channel_id=1, source_target_pairs={{0,2},{1,3},{2,0},{3,1},{4,6},{5,7},{6,4},{7,5},{8,10},{9,11},{10,... | collective-permute-start | bytes 393224 | tf_op jit(solution)/shard_map/ppermute | solution.py:272
  21.6 8.0 %copy-start.3 = (bf16[128,512]{1,0:T(8,128)(2,1)S(1)}, bf16[128,512]{1,0:T(8,128)(2,1)}, u32[]{:S(2)}) copy-start(bf16[128,512]{1,0:T(8,128)(2,1)} %get-tuple-element.26.rest_2_.rest_0_) | copy-start | bytes 393220
  21.9 8.2 %copy-start.4 = (f32[1,1,4096]{2,1,0:T(1,128)S(1)}, f32[1,1,4096]{2,1,0:T(1,128)}, u32[]{:S(2)}) copy-start(f32[1,1,4096]{2,1,0:T(1,128)} %param.13) | copy-start | bytes 49156
  21.9 8.2 %copy-start.5 = (f32[1,512]{1,0:T(1,128)S(1)}, f32[1,512]{1,0:T(1,128)}, u32[]{:S(2)}) copy-start(f32[1,512]{1,0:T(1,128)} %pb_ref.1) | copy-start | bytes 6148
  31.9 1.9 %collective-permute-start.7 = (bf16[32,512]{1,0:T(8,128)(2,1)S(1)}, bf16[32,512]{1,0:T(8,128)(2,1)S(1)}, u32[]{:S(2)}, u32[]{:S(2)}) collective-permute-start(bf16[32,512]{1,0:T(8,128)(2,1)S(1)} %get-tuple-element.32), channel_id=1, source_target_pairs={{0,8},{8,0},{16,24},{24,16},{1,9},{9,1},{17,25},{25,17},{2,10},{10... | collective-permute-start | bytes 98312 | tf_op jit(solution)/shard_map/ppermute | solution.py:272
  31.9 4.0 %collective-permute-start.8 = (bf16[32,512]{1,0:T(8,128)(2,1)S(1)}, bf16[32,512]{1,0:T(8,128)(2,1)S(1)}, u32[]{:S(2)}, u32[]{:S(2)}) collective-permute-start(bf16[32,512]{1,0:T(8,128)(2,1)S(1)} %get-tuple-element.33), channel_id=1, source_target_pairs={{0,16},{8,24},{16,0},{24,8},{1,17},{9,25},{17,1},{25,9},{2,18},{10... | collective-permute-start | bytes 98312 | tf_op jit(solution)/shard_map/ppermute | solution.py:272
  33.5 3.3 %collective-permute-start.9 = (bf16[32,512]{1,0:T(8,128)(2,1)S(1)}, bf16[32,512]{1,0:T(8,128)(2,1)S(1)}, u32[]{:S(2)}, u32[]{:S(2)}) collective-permute-start(bf16[32,512]{1,0:T(8,128)(2,1)S(1)} %get-tuple-element.34), channel_id=1, source_target_pairs={{0,24},{8,16},{16,8},{24,0},{1,25},{9,17},{17,9},{25,1},{2,26},{10... | collective-permute-start | bytes 98312 | tf_op jit(solution)/shard_map/ppermute | solution.py:272

commit v4 on v3

--- a/solution.py
+++ b/solution.py
@@ -16,40 +16,32 @@
 VMEM = pl.BlockSpec(memory_space=pltpu.VMEM)
 
 
-def bag_tiles(group, block, towers, ids_ref, len_ref):
+def bag_columns(group, dest, block, towers, ids_ref, len_ref):
     feats, slots, samples = ids_ref.shape
-    groups = samples // (towers * LANES)
-    tiles = []
-    for t in range(towers):
-        at = pl.ds(pl.multiple_of((t * groups + group) * LANES, LANES), LANES)
-        lens = len_ref[:, at]
+    groups, per = samples // (towers * LANES), LANES // block
+    lane = lax.broadcasted_iota(jnp.int32, (feats * slots, LANES), 1) // block
+    columns = []
+    for first in range(0, towers, per):
+        bags = lens = None
+        for q in range(per):
+            start = ((first + q) * groups + group) * LANES
+            at = pl.ds(pl.multiple_of(start, LANES), LANES)
+            shift = lax.rem(q - dest + per, per) * block
+            ids = jnp.concatenate([ids_ref[f, :, at] for f in range(feats)], axis=0)
+            ids, own = pltpu.roll(ids, shift, 1), pltpu.roll(len_ref[:, at], shift, 1)
+            bags = ids if bags is None else jnp.where(lane == q, ids, bags)
+            lens = own if lens is None else jnp.where(lane[:feats] == q, own, lens)
         rows = []
         for f in range(feats):
-            ids = ids_ref[f, :, at]
+            ids = bags[f * slots : (f + 1) * slots]
             slot = lax.broadcasted_iota(jnp.int32, ids.shape, 0)
             ids = jnp.where(slot < lens[f : f + 1], ids, -1)
             times = jnp.zeros(ids.shape, jnp.float32)
             for p in range(slots):
                 times += jnp.where(ids == ids[p : p + 1], 1.0, 0.0)
             rows += [ids.astype(jnp.float32), times]
-        tiles.append(jnp.concatenate(rows, axis=0))
-    return tiles
-
-
-def bag_columns(tiles, dest, block):
-    per = LANES // block
-    lane = lax.broadcasted_iota(jnp.int32, tiles[0].shape, 1) // block
-    columns = []
-    for first in range(0, len(tiles), per):
-        merged = None
-        for q in range(per):
-            shift = lax.rem(q - dest + per, per) * block
-            moved = pltpu.roll(tiles[first + q], shift, 1)
-            merged = moved if merged is None else jnp.where(lane == q, moved, merged)
-        pad = -merged.shape[0] % LANES
-        if pad:
-            merged = jnp.concatenate([merged, jnp.zeros((pad, LANES), jnp.float32)], axis=0)
-        columns.append(merged.T)
+        rows = jnp.concatenate(rows, axis=0)
+        columns.append(rows.T)
     return columns
 
 
@@ -65,30 +57,40 @@
     return jnp.dot(counts, table, preferred_element_type=jnp.float32).astype(jnp.bfloat16)
 
 
-def pool_dests(tiles, dests, block, slots, tables, buf, ready=None):
-    feats, width = tables.shape[0], tables.shape[2]
-    height = buf.shape[1]
+def pool_dests(group, dests, block, towers, ids_ref, len_ref, tables, outs, ready):
+    (feats, slots, _), width = ids_ref.shape, tables.shape[2]
+    height = outs[0].shape[0]
     batch = max(1, BATCH // height)
     for first in range(0, len(dests), batch):
         some = dests[first : first + batch]
-        columns = [c for d in some for c in bag_columns(tiles, d, block)]
+        columns = [
+            c for d in some for c in bag_columns(group, d, block, towers, ids_ref, len_ref)
+        ]
         columns = jnp.concatenate(columns, axis=0) if len(columns) > 1 else columns[0]
         for f in range(feats):
-            if ready is not None:
-                ready(f)
+            if ready is not None and first == 0:
+                ready[f].wait()
             rows = pool_rows(columns, f, slots, tables[f])
             for i in range(len(some)):
-                buf[first + i, :, f * width : (f + 1) * width] = rows[
+                outs[first + i][:, f * width : (f + 1) * width] = rows[
                     i * height : (i + 1) * height
                 ]
 
 
-def first_kernel(
-    k, block, towers, ids_hbm, len_hbm, tab_hbm, out_ref, ids_ref, len_ref, tab_ref, sems
-):
+def pool_groups(ks, block, towers, ids_ref, len_ref, tab_ref, outs, ready=None):
     per = LANES // block
-    feats, slots, _ = ids_ref.shape
-    width = tab_ref.shape[2]
+    me = lax.axis_index("dev")
+    for g in sorted({k // per for k in ks}):
+        some = [i for i, k in enumerate(ks) if k // per == g]
+        dests = [lax.rem(me, per) ^ ks[i] % per for i in some]
+        some = [outs[i] for i in some]
+        pool_dests(me // per ^ g, dests, block, towers, ids_ref, len_ref, tab_ref, some, ready)
+        ready = None
+
+
+def first_kernel(ks, block, towers, ids_hbm, len_hbm, tab_hbm, ids_ref, len_ref, tab_ref, *rest):
+    outs, sems = rest[:-1], rest[-1]
+    feats = ids_ref.shape[0]
     bags = [
         pltpu.make_async_copy(ids_hbm, ids_ref, sems.at[0]),
         pltpu.make_async_copy(len_hbm, len_ref, sems.at[1]),
@@ -100,67 +102,37 @@
         copy.start()
     for copy in bags:
         copy.wait()
-    tiles = bag_tiles(lax.axis_index("dev") // per ^ k // per, block, towers, ids_ref, len_ref)
-    dest = lax.rem(lax.axis_index("dev"), per) ^ k % per
-    columns = bag_columns(tiles, dest, block)
-    columns = jnp.concatenate(columns, axis=0) if len(columns) > 1 else columns[0]
-    for f in range(feats):
-        rows[f].wait()
-        out_ref[:, f * width : (f + 1) * width] = pool_rows(columns, f, slots, tab_ref[f])
-
-
-def pool_first(ids, lens, tables, k, block, towers):
+    pool_groups(ks, block, towers, ids_ref, len_ref, tab_ref, outs, rows)
+
+
+def pool_first(ids, lens, tables, ks, block, towers):
     feats = ids.shape[0]
-    depth = feats * tables.shape[2]
-    return pl.pallas_call(
-        functools.partial(first_kernel, k, block, towers),
-        in_specs=[ANY, ANY, ANY],
-        out_specs=[VMEM, VMEM, VMEM, VMEM],
-        out_shape=[
-            pltpu.VMEM((towers * block, depth), jnp.bfloat16),
-            jax.ShapeDtypeStruct(ids.shape, ids.dtype),
-            jax.ShapeDtypeStruct(lens.shape, lens.dtype),
-            jax.ShapeDtypeStruct(tables.shape, tables.dtype),
-        ],
+    shape = (towers * block, feats * tables.shape[2])
+    return pl.pallas_call(
+        functools.partial(first_kernel, ks, block, towers),
+        in_specs=[ANY] * 3,
+        out_specs=[VMEM] * (3 + len(ks)),
+        out_shape=[jax.ShapeDtypeStruct(x.shape, x.dtype) for x in (ids, lens, tables)]
+        + [pltpu.VMEM(shape, jnp.bfloat16)] * len(ks),
         scratch_shapes=[pltpu.SemaphoreType.DMA((2 + feats,))],
         compiler_params=pltpu.CompilerParams(vmem_limit_bytes=16 * MIB),
         name="pool_first",
     )(ids, lens, tables)
 
 
-def more_kernel(ks, block, towers, ids_ref, len_ref, tab_ref, after_ref, *rest):
-    outs, (buf, sems) = rest[:-2], rest[-2:]
-    per = LANES // block
-    slots = ids_ref.shape[1]
-    low = lax.rem(lax.axis_index("dev"), per)
-    for g in sorted({k // per for k in ks}):
-        some = [i for i, k in enumerate(ks) if k // per == g]
-        tiles = bag_tiles(lax.axis_index("dev") // per ^ g, block, towers, ids_ref, len_ref)
-        dests = [low ^ ks[i] % per for i in some]
-        pool_dests(
-            tiles, dests, block, slots, tab_ref, buf.at[some[0] : some[0] + len(some)]
-        )
-    copies = [pltpu.make_async_copy(buf.at[i], out, sems.at[i]) for i, out in enumerate(outs)]
-    for copy in copies:
-        copy.start()
-    for copy in copies:
-        copy.wait()
+def more_kernel(ks, block, towers, ids_ref, len_ref, tab_ref, after_ref, *outs):
+    pool_groups(ks, block, towers, ids_ref, len_ref, tab_ref, outs)
 
 
 def pool_more(ids, lens, tables, after, ks, block, towers):
-    depth = ids.shape[0] * tables.shape[2]
-    shape = (towers * block, depth)
+    shape = (towers * block, ids.shape[0] * tables.shape[2])
     return pl.pallas_call(
         functools.partial(more_kernel, ks, block, towers),
         in_specs=[VMEM, VMEM, VMEM, ANY],
-        out_specs=[ANY] * len(ks),
-        out_shape=[pltpu.HBM(shape, jnp.bfloat16)] * len(ks),
-        scratch_shapes=[
-            pltpu.VMEM((len(ks),) + shape, jnp.bfloat16),
-            pltpu.SemaphoreType.DMA((len(ks),)),
-        ],
-        compiler_params=pltpu.CompilerParams(vmem_limit_bytes=16 * MIB),
-        cost_estimate=pl.CostEstimate(flops=10**9, bytes_accessed=0, transcendentals=0),
+        out_specs=[VMEM] * len(ks),
+        out_shape=[pltpu.VMEM(shape, jnp.bfloat16)] * len(ks),
+        compiler_params=pltpu.CompilerParams(vmem_limit_bytes=16 * MIB),
+        cost_estimate=pl.CostEstimate(flops=2 * 10**9, bytes_accessed=0, transcendentals=0),
         name="pool_more",
     )(ids, lens, tables, after)
 
@@ -183,7 +155,7 @@
         out_specs=VMEM,
         out_shape=jax.ShapeDtypeStruct((chunks[0].shape[0], down.shape[1]), jnp.float32),
         compiler_params=pltpu.CompilerParams(vmem_limit_bytes=16 * MIB),
-        cost_estimate=pl.CostEstimate(flops=10**9, bytes_accessed=0, transcendentals=0),
+        cost_estimate=pl.CostEstimate(flops=4 * 10**9, bytes_accessed=0, transcendentals=0),
         name="low_part",
     )(down, *chunks, *low, *held)
 
@@ -287,26 +259,30 @@
     down, up, proj = (pltpu.with_memory_space_constraint(w, pltpu.VMEM) for w in weights)
     far, near = list(range(per, members)), [1] + list(range(per - 1, 1, -1))
     order = far[:1] + near[:1] + far[1:-1] + near[1:-1] + far[-1:] + near[-1:]
+    batches = [
+        far[:1],
+        [0] + near[:1] + far[1:2],
+        near[1:-1] + far[2:-1],
+        near[-1:] + far[-1:],
+    ]
+    steps = [far[:1], near[:1], far[1:-1] + [0] + near[1:-1]]
     pooled, got = {}, {}
-    pooled[far[0]], ids, lens, rows = pool_first(ids, lens, rows, far[0], block, towers)
-
-    def pool(ks, after):
-        ks = sorted(ks)
-        done = pltpu.with_memory_space_constraint(pooled[after], pltpu.HBM)
-        parts = pool_more(ids, lens, rows, done, ks, block, towers)
+    ids, lens, rows, *parts = pool_first(ids, lens, rows, batches[0], block, towers)
+    pooled.update(zip(batches[0], parts, strict=True))
+    for ks in batches[1:]:
+        after = pltpu.with_memory_space_constraint(parts[0], pltpu.VMEM)
+        parts = pool_more(ids, lens, rows, after, ks, block, towers)
         pooled.update(zip(ks, parts, strict=True))
-
-    pool(order[1 : len(far)], far[0])
-    pool([0] + order[len(far) :], far[-2])
     for k in order:
         got[k] = swap(pooled[k], "dev", k)
     got[0] = pooled[0]
     low = []
-    for i, some in enumerate([far[:1],near[:1],far[1:-1]+[0]+near[1:-1]]):
+    for i, some in enumerate(steps):
         held = (up, proj) if i == 1 else ()
         low = [low_part(down, [got[k] for k in some], some, low, held)]
-    ks = [0] + order
-    outs = tower_out(low[0], down, up, bias, proj, proj_bias, [got[k] for k in ks], ks, 2, towers)
+    done = [k for some in steps for k in some]
+    ks = done + [k for k in [0] + order if k not in done]
+    outs = tower_out(low[0], down, up, bias, proj, proj_bias, [got[k] for k in ks], ks, len(ks) - len(done), towers)
     met = [outs[0]] + [swap(outs[k], "tower", k) for k in range(1, towers)]
     return gram_pairs(met).T
 

time: 37.9 us -> 37 us (0.976)
  waiting for transfers between devices: 10.8 us -> 8.47 us
  local copies, waits for them, and re-layouts: 0.04 us -> 2.15 us
  Pallas kernels: 12.2 us -> 11.1 us
    ppermute x10, waiting for transfers between devices: 10.8 us -> 8.47 us  [swap(): return lax.ppermute(x, axis, [(i, i ^ k) for i in range(size)])]
    unnamed x16 -> x10, local copies, waits for them, and re-layouts: 0.04 us -> 2.15 us
    pallas_call x2 -> x3, Pallas kernels: 5.96 us -> 5.07 us  [pool_more(): pl.pallas_call(functools.partial(more_kernel, ks, block, towers), in_spec...]
  transfers between devices with their start and end apart: 10 -> 10, of which waited for: 4 -> 3; matrix products, arithmetic and copies ran while one was open for 0% -> 0% of each run, Pallas kernels for 18% -> 16%
where the time goes in v4:
time: 37 us; the launch traced here: 36.6 us
  starting transfers between devices  14.7 us (40%)
  Pallas kernels  11.1 us (30%)
  waiting for transfers between devices  8.47 us (23%)
  local copies, waits for them, and re-layouts  2.15 us (6%)
    ppermute x10, starting transfers between devices, swap(): return lax.ppermute(x, axis, [(i, i ^ k) for i in range(size)])  14.7 us
    ppermute x10, waiting for transfers between devices, swap(): return lax.ppermute(x, axis, [(i, i ^ k) for i in range(size)])  8.47 us
    pallas_call x3, Pallas kernels, pool_more(): pl.pallas_call(functools.partial(more_kernel, ks, block, towers), in_spec...  5.07 us
    pallas_call x1, Pallas kernels, pool_first(): pl.pallas_call(functools.partial(first_kernel, ks, block, towers), in_spe...  2.49 us
    unnamed x10, local copies, waits for them, and re-layouts  2.15 us
    pallas_call x1, Pallas kernels, tower_out(): pl.pallas_call(functools.partial(tower_kernel, ks, late, towers), in_spec...  1.76 us
    pallas_call x3, Pallas kernels, low_part(): pl.pallas_call(functools.partial(low_kernel, ks, len(held)), in_specs=[VM...  0.9 us
    pallas_call x1, Pallas kernels, gram_pairs(): pl.pallas_call(gram_kernel, in_specs=[VMEM] * towers, out_specs=VMEM, out...  0.87 us
  transfers between devices with their start and end apart: 10, of which 3 were waited for; matrix products, arithmetic and copies ran while one was open for 0% of the time, Pallas kernels for 16%

profile of v4, /device:TPU:0, one launch (start us, length us, event | category | flops | bytes accessed | tf_op | source)
XLA Modules:
  0.0 36.6 jit_solution(16476320758778611939)
XLA Ops:
  0.0 2.5 %pool_first.1 = (s32[4,4,1024]{2,1,0:T(4,128)S(1)}, s32[4,1024]{1,0:T(4,128)S(1)}, bf16[4,1024,128]{2,1,0:T(8,128)(2,1)S(1)}, bf16[128,512]{1,0:T(8,128)(2,1)S(1)}) custom-call(s32[4,4,1024]{2,1,0:T(4,128)} %bitcast.22, s32[4,1024]{1,0:T(4,128)} %bitcast.23, bf16[4,1024,128]{2,1,0:T(8,128)(2,1)} %bitcast.21), custom_call_target="tpu_custom_call" | custom-call | tf_op jit(solution)/shard_map/pool_first/pallas_call | solution.py:111
  2.5 4.1 %collective-permute-start.4 = (bf16[128,512]{1,0:T(8,128)(2,1)S(1)}, bf16[128,512]{1,0:T(8,128)(2,1)S(1)}, u32[]{:S(2)}, u32[]{:S(2)}) collective-permute-start(bf16[128,512]{1,0:T(8,128)(2,1)S(1)} %get-tuple-element.23.after_ref), channel_id=1, source_target_pairs={{0,4},{1,5},{2,6},{3,7},{4,0},{5,1},{6,2},{7,3},{8,12},{9,13},{10,... | collective-permute-start | bytes 393224 | tf_op jit(solution)/shard_map/ppermute | solution.py:244
  6.6 1.9 %pool_more.3 = (bf16[128,512]{1,0:T(8,128)(2,1)S(1)}, bf16[128,512]{1,0:T(8,128)(2,1)S(1)}, bf16[128,512]{1,0:T(8,128)(2,1)S(1)}) custom-call(s32[4,4,1024]{2,1,0:T(4,128)S(1)} %get-tuple-element.20.ids_ref, s32[4,1024]{1,0:T(4,128)S(1)} %get-tuple-element.21.len_ref, bf16[4,1024,128]{2,1,0:T(8,128)(2,1)S(1)} %get-tuple-element.22.tab_ref, ...), custom_call_target="tpu_custom_call" | custom-call | flops 2000000000 | tf_op jit(solution)/shard_map/pool_more/pallas_call | solution.py:129
  8.5 1.3 %collective-permute-start = (bf16[128,512]{1,0:T(8,128)(2,1)S(1)}, bf16[128,512]{1,0:T(8,128)(2,1)S(1)}, u32[]{:S(2)}, u32[]{:S(2)}) collective-permute-start(bf16[128,512]{1,0:T(8,128)(2,1)S(1)} %get-tuple-element.24), channel_id=1, source_target_pairs={{0,5},{1,4},{2,7},{3,6},{4,1},{5,0},{6,3},{7,2},{8,13},{9,12},{10,... | collective-permute-start | bytes 393224 | tf_op jit(solution)/shard_map/ppermute | solution.py:244
  9.8 0.3 collective-permute-start.3
  10.1 1.6 %pool_more.4 = (bf16[128,512]{1,0:T(8,128)(2,1)S(1)}, bf16[128,512]{1,0:T(8,128)(2,1)S(1)}) custom-call(s32[4,4,1024]{2,1,0:T(4,128)S(1)} %get-tuple-element.20.ids_ref, s32[4,1024]{1,0:T(4,128)S(1)} %get-tuple-element.21.len_ref, bf16[4,1024,128]{2,1,0:T(8,128)(2,1)S(1)} %get-tuple-element.22.tab_ref, ...), custom_call_target="tpu_custom_call" | custom-call | flops 2000000000 | tf_op jit(solution)/shard_map/pool_more/pallas_call | solution.py:129
  11.7 0.0 copy-start
  11.7 2.8 %collective-permute-start.2 = (bf16[128,512]{1,0:T(8,128)(2,1)S(1)}, bf16[128,512]{1,0:T(8,128)(2,1)S(1)}, u32[]{:S(2)}, u32[]{:S(2)}) collective-permute-start(bf16[128,512]{1,0:T(8,128)(2,1)S(1)} %get-tuple-element.27.after_ref), channel_id=1, source_target_pairs={{0,3},{1,2},{2,1},{3,0},{4,7},{5,6},{6,5},{7,4},{8,11},{9,10},{10,... | collective-permute-start | bytes 393224 | tf_op jit(solution)/shard_map/ppermute | solution.py:244
  14.5 1.6 %pool_more.5 = (bf16[128,512]{1,0:T(8,128)(2,1)S(1)}, bf16[128,512]{1,0:T(8,128)(2,1)S(1)}) custom-call(s32[4,4,1024]{2,1,0:T(4,128)S(1)} %get-tuple-element.20.ids_ref, s32[4,1024]{1,0:T(4,128)S(1)} %get-tuple-element.21.len_ref, bf16[4,1024,128]{2,1,0:T(8,128)(2,1)S(1)} %get-tuple-element.22.tab_ref, bf16[128,512]{1,0:T(8,128)(2,1)S(1)} %get-tuple-element.27.after_ref), custom_call_target="tpu_custom_call" | custom-call | flops 2000000000 | tf_op jit(solution)/shard_map/pool_more/pallas_call | solution.py:129
  16.1 2.5 %collective-permute-start.5 = (bf16[128,512]{1,0:T(8,128)(2,1)S(1)}, bf16[128,512]{1,0:T(8,128)(2,1)S(1)}, u32[]{:S(2)}, u32[]{:S(2)}) collective-permute-start(bf16[128,512]{1,0:T(8,128)(2,1)S(1)} %get-tuple-element.29), channel_id=1, source_target_pairs={{0,7},{1,6},{2,5},{3,4},{4,3},{5,2},{6,1},{7,0},{8,15},{9,14},{10,... | collective-permute-start | bytes 393224 | tf_op jit(solution)/shard_map/ppermute | solution.py:244
  18.6 0.0 collective-permute-done.4.rest_0_
  18.6 0.7 %collective-permute-start.6 = (bf16[128,512]{1,0:T(8,128)(2,1)S(1)}, bf16[128,512]{1,0:T(8,128)(2,1)S(1)}, u32[]{:S(2)}, u32[]{:S(2)}) collective-permute-start(bf16[128,512]{1,0:T(8,128)(2,1)S(1)} %get-tuple-element.30), channel_id=1, source_target_pairs={{0,2},{1,3},{2,0},{3,1},{4,6},{5,7},{6,4},{7,5},{8,10},{9,11},{10,... | collective-permute-start | bytes 393224 | tf_op jit(solution)/shard_map/ppermute | solution.py:244
  19.3 0.0 copy-done
  19.3 0.0 copy-start.1
  19.3 0.0 copy-start.2
  19.3 0.2 low_part.3.rest_1_
  19.6 0.0 collective-permute-done.3.rest_0_.rest_1_
  19.6 1.1 %collective-permute-start.1 = (bf16[128,512]{1,0:T(8,128)(2,1)S(1)}, bf16[128,512]{1,0:T(8,128)(2,1)S(1)}, u32[]{:S(2)}, u32[]{:S(2)}) collective-permute-start(bf16[128,512]{1,0:T(8,128)(2,1)S(1)} %get-tuple-element.26), channel_id=1, source_target_pairs={{0,6},{1,7},{2,4},{3,5},{4,2},{5,3},{6,0},{7,1},{8,14},{9,15},{10,... | collective-permute-start | bytes 393224 | tf_op jit(solution)/shard_map/ppermute | solution.py:244
  20.7 0.9 %copy-done.1 = bf16[1,1,512,4096]{3,2,1,0:T(8,128)(2,1)S(1)} copy-done((bf16[1,1,512,4096]{3,2,1,0:T(8,128)(2,1)S(1)}, bf16[1,1,512,4096]{3,2,1,0:T(8,128)(2,1)}, u32[]{:S(2)}) %copy-start.1) | copy-done | bytes 4194328
  21.5 1.3 %copy-done.2 = bf16[1,4096,512]{2,1,0:T(8,128)(2,1)S(1)} copy-done((bf16[1,4096,512]{2,1,0:T(8,128)(2,1)S(1)}, bf16[1,4096,512]{2,1,0:T(8,128)(2,1)}, u32[]{:S(2)}) %copy-start.2) | copy-done | bytes 4194328
  22.8 0.2 low_part.4.rest_4_
  23.0 0.0 copy-start.3
  23.0 0.0 copy-start.4
  23.1 0.0 collective-permute-done.rest_0_.rest_2_
  23.1 5.4 %collective-permute-done.1.rest_1_.rest_3_ = bf16[128,512]{1,0:T(8,128)(2,1)S(1)} collective-permute-done((bf16[128,512]{1,0:T(8,128)(2,1)S(1)}, bf16[128,512]{1,0:T(8,128)(2,1)S(1)}, u32[]{:S(2)}, u32[]{:S(2)}) %collective-permute-start.1) | collective-permute-done | bytes 131104 | tf_op jit(solution)/shard_map/ppermute | solution.py:244
  28.4 0.0 collective-permute-done.2.rest_3_.rest_5_
  28.4 0.4 %low_part.5.low_ref = f32[128,512]{1,0:T(8,128)S(1)} custom-call(bf16[4096,512]{1,0:T(8,128)(2,1)S(1)} %bitcast.14, bf16[128,512]{1,0:T(8,128)(2,1)S(1)} %collective-permute-done.rest_0_.rest_2_, bf16[128,512]{1,0:T(8,128)(2,1)S(1)} %collective-permute-done.1.rest_1_.rest_3_, bf16[128,512]{1,0:T(8,128)(2,1)S(1)} %get-tuple-element.25.after_ref.rest_2_.rest_4_, ...), custom_call_target="tpu_custom_call" | custom-call | flops 4000000000 | tf_op jit(solution)/shard_map/low_part/pallas_call | solution.py:152
  28.9 0.0 collective-permute-done.5.rest_6_
  28.9 0.0 collective-permute-done.6.rest_7_
  28.9 0.0 copy-done.3
  28.9 0.0 copy-done.4
  28.9 1.8 %tower_out.1 = (bf16[32,512]{1,0:T(8,128)(2,1)S(1)}, bf16[32,512]{1,0:T(8,128)(2,1)S(1)}, bf16[32,512]{1,0:T(8,128)(2,1)S(1)}, bf16[32,512]{1,0:T(8,128)(2,1)S(1)}) custom-call(f32[128,512]{1,0:T(8,128)S(1)} %low_part.5.low_ref, bf16[4096,512]{1,0:T(8,128)(2,1)S(1)} %bitcast.15, bf16[512,4096]{1,0:T(8,128)(2,1)S(1)} %bitcast.17, f32[1,4096]{1,0:T(1,128)S(1)} %bitcast.20, ...), custom_call_target="tpu_custom_call" | custom-call | flops 1073741824 | tf_op jit(solution)/shard_map/tower_out/pallas_call | solution.py:192
  30.7 0.1 collective-permute-start.7
  30.8 1.6 %collective-permute-start.8 = (bf16[32,512]{1,0:T(8,128)(2,1)S(1)}, bf16[32,512]{1,0:T(8,128)(2,1)S(1)}, u32[]{:S(2)}, u32[]{:S(2)}) collective-permute-start(bf16[32,512]{1,0:T(8,128)(2,1)S(1)} %get-tuple-element.33), channel_id=1, source_target_pairs={{0,16},{8,24},{16,0},{24,8},{1,17},{9,25},{17,1},{25,9},{2,18},{10... | collective-permute-start | bytes 98312 | tf_op jit(solution)/shard_map/ppermute | solution.py:244
  32.4 0.3 collective-permute-start.9
  32.6 0.0 collective-permute-done.7.rest_1_
  32.6 2.1 %collective-permute-done.8.rest_2_ = bf16[32,512]{1,0:T(8,128)(2,1)S(1)} collective-permute-done((bf16[32,512]{1,0:T(8,128)(2,1)S(1)}, bf16[32,512]{1,0:T(8,128)(2,1)S(1)}, u32[]{:S(2)}, u32[]{:S(2)}) %collective-permute-start.8) | collective-permute-done | bytes 32800 | tf_op jit(solution)/shard_map/ppermute | solution.py:244
  34.8 1.0 %collective-permute-done.9.rest_3_ = bf16[32,512]{1,0:T(8,128)(2,1)S(1)} collective-permute-done((bf16[32,512]{1,0:T(8,128)(2,1)S(1)}, bf16[32,512]{1,0:T(8,128)(2,1)S(1)}, u32[]{:S(2)}, u32[]{:S(2)}) %collective-permute-start.9) | collective-permute-done | bytes 32800 | tf_op jit(solution)/shard_map/ppermute | solution.py:244
  35.7 0.9 %gram_pairs.1 = f32[6,32]{1,0:T(8,128)} custom-call(bf16[32,512]{1,0:T(8,128)(2,1)S(1)} %get-tuple-element.31.rest_0_, bf16[32,512]{1,0:T(8,128)(2,1)S(1)} %collective-permute-done.7.rest_1_, bf16[32,512]{1,0:T(8,128)(2,1)S(1)} %collective-permute-done.8.rest_2_, bf16[32,512]{1,0:T(8,128)(2,1)S(1)} %collective-permute-done.9.rest_3_), custom_call_target="tpu_custom_call" | custom-call | tf_op jit(solution)/shard_map/gram_pairs/pallas_call | solution.py:231
Async XLA Ops:
  2.5 16.1 %collective-permute-start.4 = (bf16[128,512]{1,0:T(8,128)(2,1)S(1)}, bf16[128,512]{1,0:T(8,128)(2,1)S(1)}, u32[]{:S(2)}, u32[]{:S(2)}) collective-permute-start(bf16[128,512]{1,0:T(8,128)(2,1)S(1)} %get-tuple-element.23.after_ref), channel_id=1, source_target_pairs={{0,4},{1,5},{2,6},{3,7},{4,0},{5,1},{6,2},{7,3},{8,12},{9,13},{10,... | collective-permute-start | bytes 393224 | tf_op jit(solution)/shard_map/ppermute | solution.py:244
  8.5 14.5 %collective-permute-start = (bf16[128,512]{1,0:T(8,128)(2,1)S(1)}, bf16[128,512]{1,0:T(8,128)(2,1)S(1)}, u32[]{:S(2)}, u32[]{:S(2)}) collective-permute-start(bf16[128,512]{1,0:T(8,128)(2,1)S(1)} %get-tuple-element.24), channel_id=1, source_target_pairs={{0,5},{1,4},{2,7},{3,6},{4,1},{5,0},{6,3},{7,2},{8,13},{9,12},{10,... | collective-permute-start | bytes 393224 | tf_op jit(solution)/shard_map/ppermute | solution.py:244
  9.8 9.7 %collective-permute-start.3 = (bf16[128,512]{1,0:T(8,128)(2,1)S(1)}, bf16[128,512]{1,0:T(8,128)(2,1)S(1)}, u32[]{:S(2)}, u32[]{:S(2)}) collective-permute-start(bf16[128,512]{1,0:T(8,128)(2,1)S(1)} %get-tuple-element.28), channel_id=1, source_target_pairs={{0,1},{1,0},{2,3},{3,2},{4,5},{5,4},{6,7},{7,6},{8,9},{9,8},{10,11... | collective-permute-start | bytes 393224 | tf_op jit(solution)/shard_map/ppermute | solution.py:244
  11.7 7.6 %copy-start = (bf16[1,1,4096,512]{3,2,1,0:T(8,128)(2,1)S(1)}, bf16[1,1,4096,512]{3,2,1,0:T(8,128)(2,1)}, u32[]{:S(2)}) copy-start(bf16[1,1,4096,512]{3,2,1,0:T(8,128)(2,1)} %param.11) | copy-start | bytes 12582916
  11.7 16.7 %collective-permute-start.2 = (bf16[128,512]{1,0:T(8,128)(2,1)S(1)}, bf16[128,512]{1,0:T(8,128)(2,1)S(1)}, u32[]{:S(2)}, u32[]{:S(2)}) collective-permute-start(bf16[128,512]{1,0:T(8,128)(2,1)S(1)} %get-tuple-element.27.after_ref), channel_id=1, source_target_pairs={{0,3},{1,2},{2,1},{3,0},{4,7},{5,6},{6,5},{7,4},{8,11},{9,10},{10,... | collective-permute-start | bytes 393224 | tf_op jit(solution)/shard_map/ppermute | solution.py:244
  16.1 12.8 %collective-permute-start.5 = (bf16[128,512]{1,0:T(8,128)(2,1)S(1)}, bf16[128,512]{1,0:T(8,128)(2,1)S(1)}, u32[]{:S(2)}, u32[]{:S(2)}) collective-permute-start(bf16[128,512]{1,0:T(8,128)(2,1)S(1)} %get-tuple-element.29), channel_id=1, source_target_pairs={{0,7},{1,6},{2,5},{3,4},{4,3},{5,2},{6,1},{7,0},{8,15},{9,14},{10,... | collective-permute-start | bytes 393224 | tf_op jit(solution)/shard_map/ppermute | solution.py:244
  18.6 10.3 %collective-permute-start.6 = (bf16[128,512]{1,0:T(8,128)(2,1)S(1)}, bf16[128,512]{1,0:T(8,128)(2,1)S(1)}, u32[]{:S(2)}, u32[]{:S(2)}) collective-permute-start(bf16[128,512]{1,0:T(8,128)(2,1)S(1)} %get-tuple-element.30), channel_id=1, source_target_pairs={{0,2},{1,3},{2,0},{3,1},{4,6},{5,7},{6,4},{7,5},{8,10},{9,11},{10,... | collective-permute-start | bytes 393224 | tf_op jit(solution)/shard_map/ppermute | solution.py:244
  19.3 2.2 %copy-start.1 = (bf16[1,1,512,4096]{3,2,1,0:T(8,128)(2,1)S(1)}, bf16[1,1,512,4096]{3,2,1,0:T(8,128)(2,1)}, u32[]{:S(2)}) copy-start(bf16[1,1,512,4096]{3,2,1,0:T(8,128)(2,1)} %param.12) | copy-start | bytes 12582916
  19.3 3.5 %copy-start.2 = (bf16[1,4096,512]{2,1,0:T(8,128)(2,1)S(1)}, bf16[1,4096,512]{2,1,0:T(8,128)(2,1)}, u32[]{:S(2)}) copy-start(bf16[1,4096,512]{2,1,0:T(8,128)(2,1)} %param.14) | copy-start | bytes 12582916
  19.6 8.9 %collective-permute-start.1 = (bf16[128,512]{1,0:T(8,128)(2,1)S(1)}, bf16[128,512]{1,0:T(8,128)(2,1)S(1)}, u32[]{:S(2)}, u32[]{:S(2)}) collective-permute-start(bf16[128,512]{1,0:T(8,128)(2,1)S(1)} %get-tuple-element.26), channel_id=1, source_target_pairs={{0,6},{1,7},{2,4},{3,5},{4,2},{5,3},{6,0},{7,1},{8,14},{9,15},{10,... | collective-permute-start | bytes 393224 | tf_op jit(solution)/shard_map/ppermute | solution.py:244
  23.0 5.9 %copy-start.3 = (f32[1,1,4096]{2,1,0:T(1,128)S(1)}, f32[1,1,4096]{2,1,0:T(1,128)}, u32[]{:S(2)}) copy-start(f32[1,1,4096]{2,1,0:T(1,128)} %param.13) | copy-start | bytes 49156
  23.0 5.9 %copy-start.4 = (f32[1,512]{1,0:T(1,128)S(1)}, f32[1,512]{1,0:T(1,128)}, u32[]{:S(2)}) copy-start(f32[1,512]{1,0:T(1,128)} %pb_ref.1) | copy-start | bytes 6148
  30.7 1.9 %collective-permute-start.7 = (bf16[32,512]{1,0:T(8,128)(2,1)S(1)}, bf16[32,512]{1,0:T(8,128)(2,1)S(1)}, u32[]{:S(2)}, u32[]{:S(2)}) collective-permute-start(bf16[32,512]{1,0:T(8,128)(2,1)S(1)} %get-tuple-element.32), channel_id=1, source_target_pairs={{0,8},{8,0},{16,24},{24,16},{1,9},{9,1},{17,25},{25,17},{2,10},{10... | collective-permute-start | bytes 98312 | tf_op jit(solution)/shard_map/ppermute | solution.py:244
  30.8 4.0 %collective-permute-start.8 = (bf16[32,512]{1,0:T(8,128)(2,1)S(1)}, bf16[32,512]{1,0:T(8,128)(2,1)S(1)}, u32[]{:S(2)}, u32[]{:S(2)}) collective-permute-start(bf16[32,512]{1,0:T(8,128)(2,1)S(1)} %get-tuple-element.33), channel_id=1, source_target_pairs={{0,16},{8,24},{16,0},{24,8},{1,17},{9,25},{17,1},{25,9},{2,18},{10... | collective-permute-start | bytes 98312 | tf_op jit(solution)/shard_map/ppermute | solution.py:244
  32.4 3.3 %collective-permute-start.9 = (bf16[32,512]{1,0:T(8,128)(2,1)S(1)}, bf16[32,512]{1,0:T(8,128)(2,1)S(1)}, u32[]{:S(2)}, u32[]{:S(2)}) collective-permute-start(bf16[32,512]{1,0:T(8,128)(2,1)S(1)} %get-tuple-element.34), channel_id=1, source_target_pairs={{0,24},{8,16},{16,8},{24,0},{1,25},{9,17},{17,9},{25,1},{2,26},{10... | collective-permute-start | bytes 98312 | tf_op jit(solution)/shard_map/ppermute | solution.py:244

commit v5 on v4

--- a/solution.py
+++ b/solution.py
@@ -206,8 +206,8 @@
 def gram_kernel(*rest):
     chunks, out_ref, rows_ref = rest[:-2], rest[-2], rest[-1]
     towers, (block, width) = len(chunks), chunks[0].shape
-    for k, chunk in enumerate(chunks):
-        rows_ref[lax.axis_index("tower") ^ k] = chunk[...]
+    for i, chunk in enumerate(chunks):
+        rows_ref[lax.axis_index("tower") ^ towers - 1 - i] = chunk[...]
     rows = rows_ref[...].reshape(towers * block, width)
     gram = lax.dot_general(
         rows, rows, (((1,), (1,)), ((), ())), preferred_element_type=jnp.float32
@@ -258,14 +258,9 @@
     ids, lens, rows, *weights = (pltpu.with_memory_space_constraint(w, pltpu.HBM) for w in fixed)
     down, up, proj = (pltpu.with_memory_space_constraint(w, pltpu.VMEM) for w in weights)
     far, near = list(range(per, members)), [1] + list(range(per - 1, 1, -1))
-    order = far[:1] + near[:1] + far[1:-1] + near[1:-1] + far[-1:] + near[-1:]
-    batches = [
-        far[:1],
-        [0] + near[:1] + far[1:2],
-        near[1:-1] + far[2:-1],
-        near[-1:] + far[-1:],
-    ]
-    steps = [far[:1], near[:1], far[1:-1] + [0] + near[1:-1]]
+    order = far[:1] + near[:1] + far[1:2] + near[:0:-1] + far[:1:-1]
+    batches = [far[:1], [0] + near[:1] + far[1:2], near[1:], far[2:]]
+    steps = [far[:1], near[:1], far[1:2] + near[-1:] + [0] + near[1:-1]]
     pooled, got = {}, {}
     ids, lens, rows, *parts = pool_first(ids, lens, rows, batches[0], block, towers)
     pooled.update(zip(batches[0], parts, strict=True))
@@ -283,7 +278,7 @@
     done = [k for some in steps for k in some]
     ks = done + [k for k in [0] + order if k not in done]
     outs = tower_out(low[0], down, up, bias, proj, proj_bias, [got[k] for k in ks], ks, len(ks) - len(done), towers)
-    met = [outs[0]] + [swap(outs[k], "tower", k) for k in range(1, towers)]
+    met = [swap(outs[k], "tower", k) for k in range(towers - 1, 0, -1)] + [outs[0]]
     return gram_pairs(met).T
 
 

time: 37 us -> 36.7 us (level)
  starting transfers between devices: 14.7 us -> 17.4 us
  local copies, waits for them, and re-layouts: 2.15 us -> 0.17 us
  Pallas kernels: 11.1 us -> 10.6 us
    ppermute x10, starting transfers between devices: 14.7 us -> 17.4 us  [swap(): return lax.ppermute(x, axis, [(i, i ^ k) for i in range(size)])]
    unnamed x10, local copies, waits for them, and re-layouts: 2.15 us -> 0.17 us
    pallas_call x3, Pallas kernels: 5.07 us -> 4.53 us  [pool_more(): pl.pallas_call(functools.partial(more_kernel, ks, block, towers), in_spec...]
  transfers between devices with their start and end apart: 10 -> 10, of which waited for: 3 -> 4; matrix products, arithmetic and copies ran while one was open for 0% -> 0% of each run, Pallas kernels for 16% -> 15%
where the time goes in v5:
time: 36.7 us; the launch traced here: 36.4 us
  starting transfers between devices  17.4 us (47%)
  Pallas kernels  10.6 us (29%)
  waiting for transfers between devices  8.19 us (22%)
    ppermute x10, starting transfers between devices, swap(): return lax.ppermute(x, axis, [(i, i ^ k) for i in range(size)])  17.4 us
    ppermute x10, waiting for transfers between devices, swap(): return lax.ppermute(x, axis, [(i, i ^ k) for i in range(size)])  8.19 us
    pallas_call x3, Pallas kernels, pool_more(): pl.pallas_call(functools.partial(more_kernel, ks, block, towers), in_spec...  4.53 us
    pallas_call x1, Pallas kernels, pool_first(): pl.pallas_call(functools.partial(first_kernel, ks, block, towers), in_spe...  2.49 us
    pallas_call x1, Pallas kernels, tower_out(): pl.pallas_call(functools.partial(tower_kernel, ks, late, towers), in_spec...  1.76 us
    pallas_call x3, Pallas kernels, low_part(): pl.pallas_call(functools.partial(low_kernel, ks, len(held)), in_specs=[VM...  0.91 us
    pallas_call x1, Pallas kernels, gram_pairs(): pl.pallas_call(gram_kernel, in_specs=[VMEM] * towers, out_specs=VMEM, out...  0.87 us
  transfers between devices with their start and end apart: 10, of which 4 were waited for; matrix products, arithmetic and copies ran while one was open for 0% of the time, Pallas kernels for 15%

profile of v5, /device:TPU:0, one launch (start us, length us, event | category | flops | bytes accessed | tf_op | source)
XLA Modules:
  0.0 36.4 jit_solution(4535955169298579322)
XLA Ops:
  0.0 2.5 %pool_first.1 = (s32[4,4,1024]{2,1,0:T(4,128)S(1)}, s32[4,1024]{1,0:T(4,128)S(1)}, bf16[4,1024,128]{2,1,0:T(8,128)(2,1)S(1)}, bf16[128,512]{1,0:T(8,128)(2,1)S(1)}) custom-call(s32[4,4,1024]{2,1,0:T(4,128)} %bitcast.22, s32[4,1024]{1,0:T(4,128)} %bitcast.23, bf16[4,1024,128]{2,1,0:T(8,128)(2,1)} %bitcast.21), custom_call_target="tpu_custom_call" | custom-call | tf_op jit(solution)/shard_map/pool_first/pallas_call | solution.py:111
  2.5 4.1 %collective-permute-start.4 = (bf16[128,512]{1,0:T(8,128)(2,1)S(1)}, bf16[128,512]{1,0:T(8,128)(2,1)S(1)}, u32[]{:S(2)}, u32[]{:S(2)}) collective-permute-start(bf16[128,512]{1,0:T(8,128)(2,1)S(1)} %get-tuple-element.23.after_ref), channel_id=1, source_target_pairs={{0,4},{1,5},{2,6},{3,7},{4,0},{5,1},{6,2},{7,3},{8,12},{9,13},{10,... | collective-permute-start | bytes 393224 | tf_op jit(solution)/shard_map/ppermute | solution.py:244
  6.6 1.9 %pool_more.3 = (bf16[128,512]{1,0:T(8,128)(2,1)S(1)}, bf16[128,512]{1,0:T(8,128)(2,1)S(1)}, bf16[128,512]{1,0:T(8,128)(2,1)S(1)}) custom-call(s32[4,4,1024]{2,1,0:T(4,128)S(1)} %get-tuple-element.20.ids_ref, s32[4,1024]{1,0:T(4,128)S(1)} %get-tuple-element.21.len_ref, bf16[4,1024,128]{2,1,0:T(8,128)(2,1)S(1)} %get-tuple-element.22.tab_ref, ...), custom_call_target="tpu_custom_call" | custom-call | flops 2000000000 | tf_op jit(solution)/shard_map/pool_more/pallas_call | solution.py:129
  8.5 1.3 %collective-permute-start = (bf16[128,512]{1,0:T(8,128)(2,1)S(1)}, bf16[128,512]{1,0:T(8,128)(2,1)S(1)}, u32[]{:S(2)}, u32[]{:S(2)}) collective-permute-start(bf16[128,512]{1,0:T(8,128)(2,1)S(1)} %get-tuple-element.24), channel_id=1, source_target_pairs={{0,5},{1,4},{2,7},{3,6},{4,1},{5,0},{6,3},{7,2},{8,13},{9,12},{10,... | collective-permute-start | bytes 393224 | tf_op jit(solution)/shard_map/ppermute | solution.py:244
  9.8 0.3 collective-permute-start.3
  10.1 1.3 %pool_more.4 = (bf16[128,512]{1,0:T(8,128)(2,1)S(1)}, bf16[128,512]{1,0:T(8,128)(2,1)S(1)}) custom-call(s32[4,4,1024]{2,1,0:T(4,128)S(1)} %get-tuple-element.20.ids_ref, s32[4,1024]{1,0:T(4,128)S(1)} %get-tuple-element.21.len_ref, bf16[4,1024,128]{2,1,0:T(8,128)(2,1)S(1)} %get-tuple-element.22.tab_ref, ...), custom_call_target="tpu_custom_call" | custom-call | flops 2000000000 | tf_op jit(solution)/shard_map/pool_more/pallas_call | solution.py:129
  11.5 0.0 copy-start
  11.5 2.8 %collective-permute-start.2 = (bf16[128,512]{1,0:T(8,128)(2,1)S(1)}, bf16[128,512]{1,0:T(8,128)(2,1)S(1)}, u32[]{:S(2)}, u32[]{:S(2)}) collective-permute-start(bf16[128,512]{1,0:T(8,128)(2,1)S(1)} %get-tuple-element.27.after_ref), channel_id=1, source_target_pairs={{0,3},{1,2},{2,1},{3,0},{4,7},{5,6},{6,5},{7,4},{8,11},{9,10},{10,... | collective-permute-start | bytes 393224 | tf_op jit(solution)/shard_map/ppermute | solution.py:244
  14.3 1.3 %pool_more.5 = (bf16[128,512]{1,0:T(8,128)(2,1)S(1)}, bf16[128,512]{1,0:T(8,128)(2,1)S(1)}) custom-call(s32[4,4,1024]{2,1,0:T(4,128)S(1)} %get-tuple-element.20.ids_ref, s32[4,1024]{1,0:T(4,128)S(1)} %get-tuple-element.21.len_ref, bf16[4,1024,128]{2,1,0:T(8,128)(2,1)S(1)} %get-tuple-element.22.tab_ref, bf16[128,512]{1,0:T(8,128)(2,1)S(1)} %get-tuple-element.27.after_ref), custom_call_target="tpu_custom_call" | custom-call | flops 2000000000 | tf_op jit(solution)/shard_map/pool_more/pallas_call | solution.py:129
  15.6 2.5 %collective-permute-start.5 = (bf16[128,512]{1,0:T(8,128)(2,1)S(1)}, bf16[128,512]{1,0:T(8,128)(2,1)S(1)}, u32[]{:S(2)}, u32[]{:S(2)}) collective-permute-start(bf16[128,512]{1,0:T(8,128)(2,1)S(1)} %get-tuple-element.29), channel_id=1, source_target_pairs={{0,7},{1,6},{2,5},{3,4},{4,3},{5,2},{6,1},{7,0},{8,15},{9,14},{10,... | collective-permute-start | bytes 393224 | tf_op jit(solution)/shard_map/ppermute | solution.py:244
  18.1 0.0 collective-permute-done.4.rest_0_
  18.1 1.4 %collective-permute-start.6 = (bf16[128,512]{1,0:T(8,128)(2,1)S(1)}, bf16[128,512]{1,0:T(8,128)(2,1)S(1)}, u32[]{:S(2)}, u32[]{:S(2)}) collective-permute-start(bf16[128,512]{1,0:T(8,128)(2,1)S(1)} %get-tuple-element.30), channel_id=1, source_target_pairs={{0,6},{1,7},{2,4},{3,5},{4,2},{5,3},{6,0},{7,1},{8,14},{9,15},{10,... | collective-permute-start | bytes 393224 | tf_op jit(solution)/shard_map/ppermute | solution.py:244
  19.5 0.0 copy-done
  19.5 0.0 copy-start.1
  19.5 0.0 copy-start.2
  19.5 0.2 low_part.3.rest_1_
  19.7 0.0 collective-permute-done.3.rest_0_.rest_1_
  19.7 3.1 %collective-permute-start.1 = (bf16[128,512]{1,0:T(8,128)(2,1)S(1)}, bf16[128,512]{1,0:T(8,128)(2,1)S(1)}, u32[]{:S(2)}, u32[]{:S(2)}) collective-permute-start(bf16[128,512]{1,0:T(8,128)(2,1)S(1)} %get-tuple-element.26), channel_id=1, source_target_pairs={{0,2},{1,3},{2,0},{3,1},{4,6},{5,7},{6,4},{7,5},{8,10},{9,11},{10,... | collective-permute-start | bytes 393224 | tf_op jit(solution)/shard_map/ppermute | solution.py:244
  22.8 0.0 copy-done.1
  22.8 0.1 copy-done.2
  22.9 0.2 low_part.4.rest_4_
  23.2 0.0 copy-start.3
  23.2 0.0 copy-start.4
  23.2 1.8 %collective-permute-done.rest_0_.rest_2_ = bf16[128,512]{1,0:T(8,128)(2,1)S(1)} collective-permute-done((bf16[128,512]{1,0:T(8,128)(2,1)S(1)}, bf16[128,512]{1,0:T(8,128)(2,1)S(1)}, u32[]{:S(2)}, u32[]{:S(2)}) %collective-permute-start) | collective-permute-done | bytes 131104 | tf_op jit(solution)/shard_map/ppermute | solution.py:244
  25.0 3.1 %collective-permute-done.1.rest_1_.rest_3_ = bf16[128,512]{1,0:T(8,128)(2,1)S(1)} collective-permute-done((bf16[128,512]{1,0:T(8,128)(2,1)S(1)}, bf16[128,512]{1,0:T(8,128)(2,1)S(1)}, u32[]{:S(2)}, u32[]{:S(2)}) %collective-permute-start.1) | collective-permute-done | bytes 131104 | tf_op jit(solution)/shard_map/ppermute | solution.py:244
  28.1 0.0 collective-permute-done.2.rest_3_.rest_5_
  28.1 0.4 %low_part.5.low_ref = f32[128,512]{1,0:T(8,128)S(1)} custom-call(bf16[4096,512]{1,0:T(8,128)(2,1)S(1)} %bitcast.14, bf16[128,512]{1,0:T(8,128)(2,1)S(1)} %collective-permute-done.rest_0_.rest_2_, bf16[128,512]{1,0:T(8,128)(2,1)S(1)} %collective-permute-done.1.rest_1_.rest_3_, bf16[128,512]{1,0:T(8,128)(2,1)S(1)} %get-tuple-element.25.after_ref.rest_2_.rest_4_, ...), custom_call_target="tpu_custom_call" | custom-call | flops 4000000000 | tf_op jit(solution)/shard_map/low_part/pallas_call | solution.py:152
  28.6 0.0 collective-permute-done.5.rest_6_
  28.6 0.0 collective-permute-done.6.rest_7_
  28.6 0.0 copy-done.3
  28.6 0.0 copy-done.4
  28.6 1.8 %tower_out.1 = (bf16[32,512]{1,0:T(8,128)(2,1)S(1)}, bf16[32,512]{1,0:T(8,128)(2,1)S(1)}, bf16[32,512]{1,0:T(8,128)(2,1)S(1)}, bf16[32,512]{1,0:T(8,128)(2,1)S(1)}) custom-call(f32[128,512]{1,0:T(8,128)S(1)} %low_part.5.low_ref, bf16[4096,512]{1,0:T(8,128)(2,1)S(1)} %bitcast.15, bf16[512,4096]{1,0:T(8,128)(2,1)S(1)} %bitcast.17, f32[1,4096]{1,0:T(1,128)S(1)} %bitcast.20, ...), custom_call_target="tpu_custom_call" | custom-call | flops 1073741824 | tf_op jit(solution)/shard_map/tower_out/pallas_call | solution.py:192
  30.4 1.3 %collective-permute-start.7 = (bf16[32,512]{1,0:T(8,128)(2,1)S(1)}, bf16[32,512]{1,0:T(8,128)(2,1)S(1)}, u32[]{:S(2)}, u32[]{:S(2)}) collective-permute-start(bf16[32,512]{1,0:T(8,128)(2,1)S(1)} %get-tuple-element.31), channel_id=1, source_target_pairs={{0,24},{8,16},{16,8},{24,0},{1,25},{9,17},{17,9},{25,1},{2,26},{10... | collective-permute-start | bytes 98312 | tf_op jit(solution)/shard_map/ppermute | solution.py:244
  31.7 0.5 %collective-permute-start.8 = (bf16[32,512]{1,0:T(8,128)(2,1)S(1)}, bf16[32,512]{1,0:T(8,128)(2,1)S(1)}, u32[]{:S(2)}, u32[]{:S(2)}) collective-permute-start(bf16[32,512]{1,0:T(8,128)(2,1)S(1)} %get-tuple-element.32), channel_id=1, source_target_pairs={{0,16},{8,24},{16,0},{24,8},{1,17},{9,25},{17,1},{25,9},{2,18},{10... | collective-permute-start | bytes 98312 | tf_op jit(solution)/shard_map/ppermute | solution.py:244
  32.1 0.2 collective-permute-start.9
  32.3 1.7 %collective-permute-done.7.rest_0_ = bf16[32,512]{1,0:T(8,128)(2,1)S(1)} collective-permute-done((bf16[32,512]{1,0:T(8,128)(2,1)S(1)}, bf16[32,512]{1,0:T(8,128)(2,1)S(1)}, u32[]{:S(2)}, u32[]{:S(2)}) %collective-permute-start.7) | collective-permute-done | bytes 32800 | tf_op jit(solution)/shard_map/ppermute | solution.py:244
  34.0 1.6 %collective-permute-done.8.rest_1_ = bf16[32,512]{1,0:T(8,128)(2,1)S(1)} collective-permute-done((bf16[32,512]{1,0:T(8,128)(2,1)S(1)}, bf16[32,512]{1,0:T(8,128)(2,1)S(1)}, u32[]{:S(2)}, u32[]{:S(2)}) %collective-permute-start.8) | collective-permute-done | bytes 32800 | tf_op jit(solution)/shard_map/ppermute | solution.py:244
  35.6 0.0 collective-permute-done.9.rest_2_
  35.6 0.9 %gram_pairs.1 = f32[6,32]{1,0:T(8,128)} custom-call(bf16[32,512]{1,0:T(8,128)(2,1)S(1)} %collective-permute-done.7.rest_0_, bf16[32,512]{1,0:T(8,128)(2,1)S(1)} %collective-permute-done.8.rest_1_, bf16[32,512]{1,0:T(8,128)(2,1)S(1)} %collective-permute-done.9.rest_2_, bf16[32,512]{1,0:T(8,128)(2,1)S(1)} %get-tuple-element.34.rest_3_), custom_call_target="tpu_custom_call" | custom-call | tf_op jit(solution)/shard_map/gram_pairs/pallas_call | solution.py:231
Async XLA Ops:
  2.5 15.6 %collective-permute-start.4 = (bf16[128,512]{1,0:T(8,128)(2,1)S(1)}, bf16[128,512]{1,0:T(8,128)(2,1)S(1)}, u32[]{:S(2)}, u32[]{:S(2)}) collective-permute-start(bf16[128,512]{1,0:T(8,128)(2,1)S(1)} %get-tuple-element.23.after_ref), channel_id=1, source_target_pairs={{0,4},{1,5},{2,6},{3,7},{4,0},{5,1},{6,2},{7,3},{8,12},{9,13},{10,... | collective-permute-start | bytes 393224 | tf_op jit(solution)/shard_map/ppermute | solution.py:244
  8.5 16.5 %collective-permute-start = (bf16[128,512]{1,0:T(8,128)(2,1)S(1)}, bf16[128,512]{1,0:T(8,128)(2,1)S(1)}, u32[]{:S(2)}, u32[]{:S(2)}) collective-permute-start(bf16[128,512]{1,0:T(8,128)(2,1)S(1)} %get-tuple-element.24), channel_id=1, source_target_pairs={{0,5},{1,4},{2,7},{3,6},{4,1},{5,0},{6,3},{7,2},{8,13},{9,12},{10,... | collective-permute-start | bytes 393224 | tf_op jit(solution)/shard_map/ppermute | solution.py:244
  9.8 9.9 %collective-permute-start.3 = (bf16[128,512]{1,0:T(8,128)(2,1)S(1)}, bf16[128,512]{1,0:T(8,128)(2,1)S(1)}, u32[]{:S(2)}, u32[]{:S(2)}) collective-permute-start(bf16[128,512]{1,0:T(8,128)(2,1)S(1)} %get-tuple-element.28), channel_id=1, source_target_pairs={{0,1},{1,0},{2,3},{3,2},{4,5},{5,4},{6,7},{7,6},{8,9},{9,8},{10,11... | collective-permute-start | bytes 393224 | tf_op jit(solution)/shard_map/ppermute | solution.py:244
  11.5 8.0 %copy-start = (bf16[1,1,4096,512]{3,2,1,0:T(8,128)(2,1)S(1)}, bf16[1,1,4096,512]{3,2,1,0:T(8,128)(2,1)}, u32[]{:S(2)}) copy-start(bf16[1,1,4096,512]{3,2,1,0:T(8,128)(2,1)} %param.11) | copy-start | bytes 12582916
  11.5 16.7 %collective-permute-start.2 = (bf16[128,512]{1,0:T(8,128)(2,1)S(1)}, bf16[128,512]{1,0:T(8,128)(2,1)S(1)}, u32[]{:S(2)}, u32[]{:S(2)}) collective-permute-start(bf16[128,512]{1,0:T(8,128)(2,1)S(1)} %get-tuple-element.27.after_ref), channel_id=1, source_target_pairs={{0,3},{1,2},{2,1},{3,0},{4,7},{5,6},{6,5},{7,4},{8,11},{9,10},{10,... | collective-permute-start | bytes 393224 | tf_op jit(solution)/shard_map/ppermute | solution.py:244
  15.6 13.0 %collective-permute-start.5 = (bf16[128,512]{1,0:T(8,128)(2,1)S(1)}, bf16[128,512]{1,0:T(8,128)(2,1)S(1)}, u32[]{:S(2)}, u32[]{:S(2)}) collective-permute-start(bf16[128,512]{1,0:T(8,128)(2,1)S(1)} %get-tuple-element.29), channel_id=1, source_target_pairs={{0,7},{1,6},{2,5},{3,4},{4,3},{5,2},{6,1},{7,0},{8,15},{9,14},{10,... | collective-permute-start | bytes 393224 | tf_op jit(solution)/shard_map/ppermute | solution.py:244
  18.1 10.5 %collective-permute-start.6 = (bf16[128,512]{1,0:T(8,128)(2,1)S(1)}, bf16[128,512]{1,0:T(8,128)(2,1)S(1)}, u32[]{:S(2)}, u32[]{:S(2)}) collective-permute-start(bf16[128,512]{1,0:T(8,128)(2,1)S(1)} %get-tuple-element.30), channel_id=1, source_target_pairs={{0,6},{1,7},{2,4},{3,5},{4,2},{5,3},{6,0},{7,1},{8,14},{9,15},{10,... | collective-permute-start | bytes 393224 | tf_op jit(solution)/shard_map/ppermute | solution.py:244
  19.5 3.3 %copy-start.1 = (bf16[1,1,512,4096]{3,2,1,0:T(8,128)(2,1)S(1)}, bf16[1,1,512,4096]{3,2,1,0:T(8,128)(2,1)}, u32[]{:S(2)}) copy-start(bf16[1,1,512,4096]{3,2,1,0:T(8,128)(2,1)} %param.12) | copy-start | bytes 12582916
  19.5 3.5 %copy-start.2 = (bf16[1,4096,512]{2,1,0:T(8,128)(2,1)S(1)}, bf16[1,4096,512]{2,1,0:T(8,128)(2,1)}, u32[]{:S(2)}) copy-start(bf16[1,4096,512]{2,1,0:T(8,128)(2,1)} %param.14) | copy-start | bytes 12582916
  19.7 8.4 %collective-permute-start.1 = (bf16[128,512]{1,0:T(8,128)(2,1)S(1)}, bf16[128,512]{1,0:T(8,128)(2,1)S(1)}, u32[]{:S(2)}, u32[]{:S(2)}) collective-permute-start(bf16[128,512]{1,0:T(8,128)(2,1)S(1)} %get-tuple-element.26), channel_id=1, source_target_pairs={{0,2},{1,3},{2,0},{3,1},{4,6},{5,7},{6,4},{7,5},{8,10},{9,11},{10,... | collective-permute-start | bytes 393224 | tf_op jit(solution)/shard_map/ppermute | solution.py:244
  23.2 5.4 %copy-start.3 = (f32[1,1,4096]{2,1,0:T(1,128)S(1)}, f32[1,1,4096]{2,1,0:T(1,128)}, u32[]{:S(2)}) copy-start(f32[1,1,4096]{2,1,0:T(1,128)} %param.13) | copy-start | bytes 49156
  23.2 5.4 %copy-start.4 = (f32[1,512]{1,0:T(1,128)S(1)}, f32[1,512]{1,0:T(1,128)}, u32[]{:S(2)}) copy-start(f32[1,512]{1,0:T(1,128)} %pb_ref.1) | copy-start | bytes 6148
  30.4 3.6 %collective-permute-start.7 = (bf16[32,512]{1,0:T(8,128)(2,1)S(1)}, bf16[32,512]{1,0:T(8,128)(2,1)S(1)}, u32[]{:S(2)}, u32[]{:S(2)}) collective-permute-start(bf16[32,512]{1,0:T(8,128)(2,1)S(1)} %get-tuple-element.31), channel_id=1, source_target_pairs={{0,24},{8,16},{16,8},{24,0},{1,25},{9,17},{17,9},{25,1},{2,26},{10... | collective-permute-start | bytes 98312 | tf_op jit(solution)/shard_map/ppermute | solution.py:244
  31.7 3.9 %collective-permute-start.8 = (bf16[32,512]{1,0:T(8,128)(2,1)S(1)}, bf16[32,512]{1,0:T(8,128)(2,1)S(1)}, u32[]{:S(2)}, u32[]{:S(2)}) collective-permute-start(bf16[32,512]{1,0:T(8,128)(2,1)S(1)} %get-tuple-element.32), channel_id=1, source_target_pairs={{0,16},{8,24},{16,0},{24,8},{1,17},{9,25},{17,1},{25,9},{2,18},{10... | collective-permute-start | bytes 98312 | tf_op jit(solution)/shard_map/ppermute | solution.py:244
  32.1 3.4 %collective-permute-start.9 = (bf16[32,512]{1,0:T(8,128)(2,1)S(1)}, bf16[32,512]{1,0:T(8,128)(2,1)S(1)}, u32[]{:S(2)}, u32[]{:S(2)}) collective-permute-start(bf16[32,512]{1,0:T(8,128)(2,1)S(1)} %get-tuple-element.33), channel_id=1, source_target_pairs={{0,8},{8,0},{16,24},{24,16},{1,9},{9,1},{17,25},{25,17},{2,10},{10... | collective-permute-start | bytes 98312 | tf_op jit(solution)/shard_map/ppermute | solution.py:244

commit v6 on v5

--- a/solution.py
+++ b/solution.py
@@ -260,7 +260,7 @@
     far, near = list(range(per, members)), [1] + list(range(per - 1, 1, -1))
     order = far[:1] + near[:1] + far[1:2] + near[:0:-1] + far[:1:-1]
     batches = [far[:1], [0] + near[:1] + far[1:2], near[1:], far[2:]]
-    steps = [far[:1], near[:1], far[1:2] + near[-1:] + [0] + near[1:-1]]
+    steps = [far[:1], near[:1], far[1:2] + [0] + near[1:-1]]
     pooled, got = {}, {}
     ids, lens, rows, *parts = pool_first(ids, lens, rows, batches[0], block, towers)
     pooled.update(zip(batches[0], parts, strict=True))

time: 36.7 us -> 36.4 us (level)
  waiting for transfers between devices: 8.19 us -> 7.78 us
    ppermute x10, waiting for transfers between devices: 8.19 us -> 7.78 us  [swap(): return lax.ppermute(x, axis, [(i, i ^ k) for i in range(size)])]
  transfers between devices with their start and end apart: 10 -> 10, of which waited for: 4 -> 5; matrix products, arithmetic and copies ran while one was open for 0% -> 0% of each run, Pallas kernels for 15% -> 15%
where the time goes in v6:
time: 36.4 us; the launch traced here: 36 us
  starting transfers between devices  17.4 us (48%)
  Pallas kernels  10.6 us (29%)
  waiting for transfers between devices  7.78 us (21%)
    ppermute x10, starting transfers between devices, swap(): return lax.ppermute(x, axis, [(i, i ^ k) for i in range(size)])  17.4 us
    ppermute x10, waiting for transfers between devices, swap(): return lax.ppermute(x, axis, [(i, i ^ k) for i in range(size)])  7.78 us
    pallas_call x3, Pallas kernels, pool_more(): pl.pallas_call(functools.partial(more_kernel, ks, block, towers), in_spec...  4.53 us
    pallas_call x1, Pallas kernels, pool_first(): pl.pallas_call(functools.partial(first_kernel, ks, block, towers), in_spe...  2.49 us
    pallas_call x1, Pallas kernels, tower_out(): pl.pallas_call(functools.partial(tower_kernel, ks, late, towers), in_spec...  1.83 us
    pallas_call x1, Pallas kernels, gram_pairs(): pl.pallas_call(gram_kernel, in_specs=[VMEM] * towers, out_specs=VMEM, out...  0.87 us
    pallas_call x3, Pallas kernels, low_part(): pl.pallas_call(functools.partial(low_kernel, ks, len(held)), in_specs=[VM...  0.85 us
  transfers between devices with their start and end apart: 10, of which 5 were waited for; matrix products, arithmetic and copies ran while one was open for 0% of the time, Pallas kernels for 15%

profile of v6, /device:TPU:0, one launch (start us, length us, event | category | flops | bytes accessed | tf_op | source)
XLA Modules:
  0.0 36.0 jit_solution(6407608878839746706)
XLA Ops:
  0.0 2.5 %pool_first.1 = (s32[4,4,1024]{2,1,0:T(4,128)S(1)}, s32[4,1024]{1,0:T(4,128)S(1)}, bf16[4,1024,128]{2,1,0:T(8,128)(2,1)S(1)}, bf16[128,512]{1,0:T(8,128)(2,1)S(1)}) custom-call(s32[4,4,1024]{2,1,0:T(4,128)} %bitcast.22, s32[4,1024]{1,0:T(4,128)} %bitcast.23, bf16[4,1024,128]{2,1,0:T(8,128)(2,1)} %bitcast.21), custom_call_target="tpu_custom_call" | custom-call | tf_op jit(solution)/shard_map/pool_first/pallas_call | solution.py:111
  2.5 4.1 %collective-permute-start.3 = (bf16[128,512]{1,0:T(8,128)(2,1)S(1)}, bf16[128,512]{1,0:T(8,128)(2,1)S(1)}, u32[]{:S(2)}, u32[]{:S(2)}) collective-permute-start(bf16[128,512]{1,0:T(8,128)(2,1)S(1)} %get-tuple-element.23.after_ref), channel_id=1, source_target_pairs={{0,4},{1,5},{2,6},{3,7},{4,0},{5,1},{6,2},{7,3},{8,12},{9,13},{10,... | collective-permute-start | bytes 393224 | tf_op jit(solution)/shard_map/ppermute | solution.py:244
  6.6 1.9 %pool_more.3 = (bf16[128,512]{1,0:T(8,128)(2,1)S(1)}, bf16[128,512]{1,0:T(8,128)(2,1)S(1)}, bf16[128,512]{1,0:T(8,128)(2,1)S(1)}) custom-call(s32[4,4,1024]{2,1,0:T(4,128)S(1)} %get-tuple-element.20.ids_ref, s32[4,1024]{1,0:T(4,128)S(1)} %get-tuple-element.21.len_ref, bf16[4,1024,128]{2,1,0:T(8,128)(2,1)S(1)} %get-tuple-element.22.tab_ref, ...), custom_call_target="tpu_custom_call" | custom-call | flops 2000000000 | tf_op jit(solution)/shard_map/pool_more/pallas_call | solution.py:129
  8.5 1.3 %collective-permute-start = (bf16[128,512]{1,0:T(8,128)(2,1)S(1)}, bf16[128,512]{1,0:T(8,128)(2,1)S(1)}, u32[]{:S(2)}, u32[]{:S(2)}) collective-permute-start(bf16[128,512]{1,0:T(8,128)(2,1)S(1)} %get-tuple-element.24), channel_id=1, source_target_pairs={{0,5},{1,4},{2,7},{3,6},{4,1},{5,0},{6,3},{7,2},{8,13},{9,12},{10,... | collective-permute-start | bytes 393224 | tf_op jit(solution)/shard_map/ppermute | solution.py:244
  9.8 0.3 collective-permute-start.2
  10.1 1.3 %pool_more.4 = (bf16[128,512]{1,0:T(8,128)(2,1)S(1)}, bf16[128,512]{1,0:T(8,128)(2,1)S(1)}) custom-call(s32[4,4,1024]{2,1,0:T(4,128)S(1)} %get-tuple-element.20.ids_ref, s32[4,1024]{1,0:T(4,128)S(1)} %get-tuple-element.21.len_ref, bf16[4,1024,128]{2,1,0:T(8,128)(2,1)S(1)} %get-tuple-element.22.tab_ref, ...), custom_call_target="tpu_custom_call" | custom-call | flops 2000000000 | tf_op jit(solution)/shard_map/pool_more/pallas_call | solution.py:129
  11.5 0.0 copy-start
  11.5 2.8 %collective-permute-start.1 = (bf16[128,512]{1,0:T(8,128)(2,1)S(1)}, bf16[128,512]{1,0:T(8,128)(2,1)S(1)}, u32[]{:S(2)}, u32[]{:S(2)}) collective-permute-start(bf16[128,512]{1,0:T(8,128)(2,1)S(1)} %get-tuple-element.26.after_ref), channel_id=1, source_target_pairs={{0,3},{1,2},{2,1},{3,0},{4,7},{5,6},{6,5},{7,4},{8,11},{9,10},{10,... | collective-permute-start | bytes 393224 | tf_op jit(solution)/shard_map/ppermute | solution.py:244
  14.3 1.3 %pool_more.5 = (bf16[128,512]{1,0:T(8,128)(2,1)S(1)}, bf16[128,512]{1,0:T(8,128)(2,1)S(1)}) custom-call(s32[4,4,1024]{2,1,0:T(4,128)S(1)} %get-tuple-element.20.ids_ref, s32[4,1024]{1,0:T(4,128)S(1)} %get-tuple-element.21.len_ref, bf16[4,1024,128]{2,1,0:T(8,128)(2,1)S(1)} %get-tuple-element.22.tab_ref, bf16[128,512]{1,0:T(8,128)(2,1)S(1)} %get-tuple-element.26.after_ref), custom_call_target="tpu_custom_call" | custom-call | flops 2000000000 | tf_op jit(solution)/shard_map/pool_more/pallas_call | solution.py:129
  15.6 2.5 %collective-permute-start.5 = (bf16[128,512]{1,0:T(8,128)(2,1)S(1)}, bf16[128,512]{1,0:T(8,128)(2,1)S(1)}, u32[]{:S(2)}, u32[]{:S(2)}) collective-permute-start(bf16[128,512]{1,0:T(8,128)(2,1)S(1)} %get-tuple-element.29), channel_id=1, source_target_pairs={{0,7},{1,6},{2,5},{3,4},{4,3},{5,2},{6,1},{7,0},{8,15},{9,14},{10,... | collective-permute-start | bytes 393224 | tf_op jit(solution)/shard_map/ppermute | solution.py:244
  18.1 0.0 collective-permute-done.3.rest_0_
  18.1 1.4 %collective-permute-start.6 = (bf16[128,512]{1,0:T(8,128)(2,1)S(1)}, bf16[128,512]{1,0:T(8,128)(2,1)S(1)}, u32[]{:S(2)}, u32[]{:S(2)}) collective-permute-start(bf16[128,512]{1,0:T(8,128)(2,1)S(1)} %get-tuple-element.30), channel_id=1, source_target_pairs={{0,6},{1,7},{2,4},{3,5},{4,2},{5,3},{6,0},{7,1},{8,14},{9,15},{10,... | collective-permute-start | bytes 393224 | tf_op jit(solution)/shard_map/ppermute | solution.py:244
  19.5 0.0 copy-done
  19.5 0.0 copy-start.1
  19.5 0.0 copy-start.2
  19.5 0.2 low_part.3.rest_1_
  19.7 0.0 collective-permute-done.2.rest_0_.rest_1_
  19.7 3.1 %collective-permute-start.4 = (bf16[128,512]{1,0:T(8,128)(2,1)S(1)}, bf16[128,512]{1,0:T(8,128)(2,1)S(1)}, u32[]{:S(2)}, u32[]{:S(2)}) collective-permute-start(bf16[128,512]{1,0:T(8,128)(2,1)S(1)} %get-tuple-element.28), channel_id=1, source_target_pairs={{0,2},{1,3},{2,0},{3,1},{4,6},{5,7},{6,4},{7,5},{8,10},{9,11},{10,... | collective-permute-start | bytes 393224 | tf_op jit(solution)/shard_map/ppermute | solution.py:244
  22.8 0.0 copy-done.1
  22.8 0.1 copy-done.2
  22.9 0.2 low_part.4.rest_3_
  23.2 0.0 copy-start.3
  23.2 0.0 copy-start.4
  23.2 1.8 %collective-permute-done.rest_0_.rest_2_ = bf16[128,512]{1,0:T(8,128)(2,1)S(1)} collective-permute-done((bf16[128,512]{1,0:T(8,128)(2,1)S(1)}, bf16[128,512]{1,0:T(8,128)(2,1)S(1)}, u32[]{:S(2)}, u32[]{:S(2)}) %collective-permute-start) | collective-permute-done | bytes 131104 | tf_op jit(solution)/shard_map/ppermute | solution.py:244
  25.0 0.0 collective-permute-done.1.rest_2_.rest_4_
  25.0 0.4 %low_part.5.low_ref = f32[128,512]{1,0:T(8,128)S(1)} custom-call(bf16[4096,512]{1,0:T(8,128)(2,1)S(1)} %bitcast.14, bf16[128,512]{1,0:T(8,128)(2,1)S(1)} %collective-permute-done.rest_0_.rest_2_, bf16[128,512]{1,0:T(8,128)(2,1)S(1)} %get-tuple-element.25.after_ref.rest_1_.rest_3_, bf16[128,512]{1,0:T(8,128)(2,1)S(1)} %collective-permute-done.1.rest_2_.rest_4_, ...), custom_call_target="tpu_custom_call" | custom-call | flops 4000000000 | tf_op jit(solution)/shard_map/low_part/pallas_call | solution.py:152
  25.4 0.0 collective-permute-done.5.rest_6_
  25.4 1.3 %collective-permute-done.6.rest_7_ = bf16[128,512]{1,0:T(8,128)(2,1)S(1)} collective-permute-done((bf16[128,512]{1,0:T(8,128)(2,1)S(1)}, bf16[128,512]{1,0:T(8,128)(2,1)S(1)}, u32[]{:S(2)}, u32[]{:S(2)}) %collective-permute-start.6) | collective-permute-done | bytes 131104 | tf_op jit(solution)/shard_map/ppermute | solution.py:244
  26.7 1.4 %collective-permute-done.4.rest_5_ = bf16[128,512]{1,0:T(8,128)(2,1)S(1)} collective-permute-done((bf16[128,512]{1,0:T(8,128)(2,1)S(1)}, bf16[128,512]{1,0:T(8,128)(2,1)S(1)}, u32[]{:S(2)}, u32[]{:S(2)}) %collective-permute-start.4) | collective-permute-done | bytes 131104 | tf_op jit(solution)/shard_map/ppermute | solution.py:244
  28.1 0.0 copy-done.3
  28.1 0.0 copy-done.4
  28.1 1.8 %tower_out.1 = (bf16[32,512]{1,0:T(8,128)(2,1)S(1)}, bf16[32,512]{1,0:T(8,128)(2,1)S(1)}, bf16[32,512]{1,0:T(8,128)(2,1)S(1)}, bf16[32,512]{1,0:T(8,128)(2,1)S(1)}) custom-call(f32[128,512]{1,0:T(8,128)S(1)} %low_part.5.low_ref, bf16[4096,512]{1,0:T(8,128)(2,1)S(1)} %bitcast.15, bf16[512,4096]{1,0:T(8,128)(2,1)S(1)} %bitcast.17, f32[1,4096]{1,0:T(1,128)S(1)} %bitcast.20, ...), custom_call_target="tpu_custom_call" | custom-call | flops 1073741824 | tf_op jit(solution)/shard_map/tower_out/pallas_call | solution.py:192
  30.0 1.3 %collective-permute-start.7 = (bf16[32,512]{1,0:T(8,128)(2,1)S(1)}, bf16[32,512]{1,0:T(8,128)(2,1)S(1)}, u32[]{:S(2)}, u32[]{:S(2)}) collective-permute-start(bf16[32,512]{1,0:T(8,128)(2,1)S(1)} %get-tuple-element.31), channel_id=1, source_target_pairs={{0,24},{8,16},{16,8},{24,0},{1,25},{9,17},{17,9},{25,1},{2,26},{10... | collective-permute-start | bytes 98312 | tf_op jit(solution)/shard_map/ppermute | solution.py:244
  31.2 0.5 %collective-permute-start.8 = (bf16[32,512]{1,0:T(8,128)(2,1)S(1)}, bf16[32,512]{1,0:T(8,128)(2,1)S(1)}, u32[]{:S(2)}, u32[]{:S(2)}) collective-permute-start(bf16[32,512]{1,0:T(8,128)(2,1)S(1)} %get-tuple-element.32), channel_id=1, source_target_pairs={{0,16},{8,24},{16,0},{24,8},{1,17},{9,25},{17,1},{25,9},{2,18},{10... | collective-permute-start | bytes 98312 | tf_op jit(solution)/shard_map/ppermute | solution.py:244
  31.7 0.2 collective-permute-start.9
  31.9 1.7 %collective-permute-done.7.rest_0_ = bf16[32,512]{1,0:T(8,128)(2,1)S(1)} collective-permute-done((bf16[32,512]{1,0:T(8,128)(2,1)S(1)}, bf16[32,512]{1,0:T(8,128)(2,1)S(1)}, u32[]{:S(2)}, u32[]{:S(2)}) %collective-permute-start.7) | collective-permute-done | bytes 32800 | tf_op jit(solution)/shard_map/ppermute | solution.py:244
  33.6 1.6 %collective-permute-done.8.rest_1_ = bf16[32,512]{1,0:T(8,128)(2,1)S(1)} collective-permute-done((bf16[32,512]{1,0:T(8,128)(2,1)S(1)}, bf16[32,512]{1,0:T(8,128)(2,1)S(1)}, u32[]{:S(2)}, u32[]{:S(2)}) %collective-permute-start.8) | collective-permute-done | bytes 32800 | tf_op jit(solution)/shard_map/ppermute | solution.py:244
  35.1 0.0 collective-permute-done.9.rest_2_
  35.1 0.9 %gram_pairs.1 = f32[6,32]{1,0:T(8,128)} custom-call(bf16[32,512]{1,0:T(8,128)(2,1)S(1)} %collective-permute-done.7.rest_0_, bf16[32,512]{1,0:T(8,128)(2,1)S(1)} %collective-permute-done.8.rest_1_, bf16[32,512]{1,0:T(8,128)(2,1)S(1)} %collective-permute-done.9.rest_2_, bf16[32,512]{1,0:T(8,128)(2,1)S(1)} %get-tuple-element.34.rest_3_), custom_call_target="tpu_custom_call" | custom-call | tf_op jit(solution)/shard_map/gram_pairs/pallas_call | solution.py:231
Async XLA Ops:
  2.5 15.6 %collective-permute-start.3 = (bf16[128,512]{1,0:T(8,128)(2,1)S(1)}, bf16[128,512]{1,0:T(8,128)(2,1)S(1)}, u32[]{:S(2)}, u32[]{:S(2)}) collective-permute-start(bf16[128,512]{1,0:T(8,128)(2,1)S(1)} %get-tuple-element.23.after_ref), channel_id=1, source_target_pairs={{0,4},{1,5},{2,6},{3,7},{4,0},{5,1},{6,2},{7,3},{8,12},{9,13},{10,... | collective-permute-start | bytes 393224 | tf_op jit(solution)/shard_map/ppermute | solution.py:244
  8.5 16.5 %collective-permute-start = (bf16[128,512]{1,0:T(8,128)(2,1)S(1)}, bf16[128,512]{1,0:T(8,128)(2,1)S(1)}, u32[]{:S(2)}, u32[]{:S(2)}) collective-permute-start(bf16[128,512]{1,0:T(8,128)(2,1)S(1)} %get-tuple-element.24), channel_id=1, source_target_pairs={{0,5},{1,4},{2,7},{3,6},{4,1},{5,0},{6,3},{7,2},{8,13},{9,12},{10,... | collective-permute-start | bytes 393224 | tf_op jit(solution)/shard_map/ppermute | solution.py:244
  9.8 9.9 %collective-permute-start.2 = (bf16[128,512]{1,0:T(8,128)(2,1)S(1)}, bf16[128,512]{1,0:T(8,128)(2,1)S(1)}, u32[]{:S(2)}, u32[]{:S(2)}) collective-permute-start(bf16[128,512]{1,0:T(8,128)(2,1)S(1)} %get-tuple-element.27), channel_id=1, source_target_pairs={{0,1},{1,0},{2,3},{3,2},{4,5},{5,4},{6,7},{7,6},{8,9},{9,8},{10,11... | collective-permute-start | bytes 393224 | tf_op jit(solution)/shard_map/ppermute | solution.py:244
  11.5 8.0 %copy-start = (bf16[1,1,4096,512]{3,2,1,0:T(8,128)(2,1)S(1)}, bf16[1,1,4096,512]{3,2,1,0:T(8,128)(2,1)}, u32[]{:S(2)}) copy-start(bf16[1,1,4096,512]{3,2,1,0:T(8,128)(2,1)} %param.11) | copy-start | bytes 12582916
  11.5 13.6 %collective-permute-start.1 = (bf16[128,512]{1,0:T(8,128)(2,1)S(1)}, bf16[128,512]{1,0:T(8,128)(2,1)S(1)}, u32[]{:S(2)}, u32[]{:S(2)}) collective-permute-start(bf16[128,512]{1,0:T(8,128)(2,1)S(1)} %get-tuple-element.26.after_ref), channel_id=1, source_target_pairs={{0,3},{1,2},{2,1},{3,0},{4,7},{5,6},{6,5},{7,4},{8,11},{9,10},{10,... | collective-permute-start | bytes 393224 | tf_op jit(solution)/shard_map/ppermute | solution.py:244
  15.6 9.8 %collective-permute-start.5 = (bf16[128,512]{1,0:T(8,128)(2,1)S(1)}, bf16[128,512]{1,0:T(8,128)(2,1)S(1)}, u32[]{:S(2)}, u32[]{:S(2)}) collective-permute-start(bf16[128,512]{1,0:T(8,128)(2,1)S(1)} %get-tuple-element.29), channel_id=1, source_target_pairs={{0,7},{1,6},{2,5},{3,4},{4,3},{5,2},{6,1},{7,0},{8,15},{9,14},{10,... | collective-permute-start | bytes 393224 | tf_op jit(solution)/shard_map/ppermute | solution.py:244
  18.1 8.6 %collective-permute-start.6 = (bf16[128,512]{1,0:T(8,128)(2,1)S(1)}, bf16[128,512]{1,0:T(8,128)(2,1)S(1)}, u32[]{:S(2)}, u32[]{:S(2)}) collective-permute-start(bf16[128,512]{1,0:T(8,128)(2,1)S(1)} %get-tuple-element.30), channel_id=1, source_target_pairs={{0,6},{1,7},{2,4},{3,5},{4,2},{5,3},{6,0},{7,1},{8,14},{9,15},{10,... | collective-permute-start | bytes 393224 | tf_op jit(solution)/shard_map/ppermute | solution.py:244
  19.5 3.3 %copy-start.1 = (bf16[1,1,512,4096]{3,2,1,0:T(8,128)(2,1)S(1)}, bf16[1,1,512,4096]{3,2,1,0:T(8,128)(2,1)}, u32[]{:S(2)}) copy-start(bf16[1,1,512,4096]{3,2,1,0:T(8,128)(2,1)} %param.12) | copy-start | bytes 12582916
  19.5 3.5 %copy-start.2 = (bf16[1,4096,512]{2,1,0:T(8,128)(2,1)S(1)}, bf16[1,4096,512]{2,1,0:T(8,128)(2,1)}, u32[]{:S(2)}) copy-start(bf16[1,4096,512]{2,1,0:T(8,128)(2,1)} %param.14) | copy-start | bytes 12582916
  19.7 8.4 %collective-permute-start.4 = (bf16[128,512]{1,0:T(8,128)(2,1)S(1)}, bf16[128,512]{1,0:T(8,128)(2,1)S(1)}, u32[]{:S(2)}, u32[]{:S(2)}) collective-permute-start(bf16[128,512]{1,0:T(8,128)(2,1)S(1)} %get-tuple-element.28), channel_id=1, source_target_pairs={{0,2},{1,3},{2,0},{3,1},{4,6},{5,7},{6,4},{7,5},{8,10},{9,11},{10,... | collective-permute-start | bytes 393224 | tf_op jit(solution)/shard_map/ppermute | solution.py:244
  23.2 5.0 %copy-start.3 = (f32[1,1,4096]{2,1,0:T(1,128)S(1)}, f32[1,1,4096]{2,1,0:T(1,128)}, u32[]{:S(2)}) copy-start(f32[1,1,4096]{2,1,0:T(1,128)} %param.13) | copy-start | bytes 49156
  23.2 4.9 %copy-start.4 = (f32[1,512]{1,0:T(1,128)S(1)}, f32[1,512]{1,0:T(1,128)}, u32[]{:S(2)}) copy-start(f32[1,512]{1,0:T(1,128)} %pb_ref.1) | copy-start | bytes 6148
  30.0 3.6 %collective-permute-start.7 = (bf16[32,512]{1,0:T(8,128)(2,1)S(1)}, bf16[32,512]{1,0:T(8,128)(2,1)S(1)}, u32[]{:S(2)}, u32[]{:S(2)}) collective-permute-start(bf16[32,512]{1,0:T(8,128)(2,1)S(1)} %get-tuple-element.31), channel_id=1, source_target_pairs={{0,24},{8,16},{16,8},{24,0},{1,25},{9,17},{17,9},{25,1},{2,26},{10... | collective-permute-start | bytes 98312 | tf_op jit(solution)/shard_map/ppermute | solution.py:244
  31.2 3.9 %collective-permute-start.8 = (bf16[32,512]{1,0:T(8,128)(2,1)S(1)}, bf16[32,512]{1,0:T(8,128)(2,1)S(1)}, u32[]{:S(2)}, u32[]{:S(2)}) collective-permute-start(bf16[32,512]{1,0:T(8,128)(2,1)S(1)} %get-tuple-element.32), channel_id=1, source_target_pairs={{0,16},{8,24},{16,0},{24,8},{1,17},{9,25},{17,1},{25,9},{2,18},{10... | collective-permute-start | bytes 98312 | tf_op jit(solution)/shard_map/ppermute | solution.py:244
  31.7 3.4 %collective-permute-start.9 = (bf16[32,512]{1,0:T(8,128)(2,1)S(1)}, bf16[32,512]{1,0:T(8,128)(2,1)S(1)}, u32[]{:S(2)}, u32[]{:S(2)}) collective-permute-start(bf16[32,512]{1,0:T(8,128)(2,1)S(1)} %get-tuple-element.33), channel_id=1, source_target_pairs={{0,8},{8,0},{16,24},{24,16},{1,9},{9,1},{17,25},{25,17},{2,10},{10... | collective-permute-start | bytes 98312 | tf_op jit(solution)/shard_map/ppermute | solution.py:244

commit v7 on v6

--- a/solution.py
+++ b/solution.py
@@ -260,7 +260,7 @@
     far, near = list(range(per, members)), [1] + list(range(per - 1, 1, -1))
     order = far[:1] + near[:1] + far[1:2] + near[:0:-1] + far[:1:-1]
     batches = [far[:1], [0] + near[:1] + far[1:2], near[1:], far[2:]]
-    steps = [far[:1], near[:1], far[1:2] + [0] + near[1:-1]]
+    steps = [far[:1], near[:1], [0] + near[1:-1], far[1:2]]
     pooled, got = {}, {}
     ids, lens, rows, *parts = pool_first(ids, lens, rows, batches[0], block, towers)
     pooled.update(zip(batches[0], parts, strict=True))

time: 36.4 us -> 36.4 us (level)
    pallas_call x3 -> x4, Pallas kernels: 0.85 us -> 1.01 us  [low_part(): pl.pallas_call(functools.partial(low_kernel, ks, len(held)), in_specs=[VM...]
where the time goes in v7:
time: 36.4 us; the launch traced here: 36 us
  starting transfers between devices  17.4 us (48%)
  Pallas kernels  10.7 us (29%)
  waiting for transfers between devices  7.6 us (21%)
    ppermute x10, starting transfers between devices, swap(): return lax.ppermute(x, axis, [(i, i ^ k) for i in range(size)])  17.4 us
    ppermute x10, waiting for transfers between devices, swap(): return lax.ppermute(x, axis, [(i, i ^ k) for i in range(size)])  7.6 us
    pallas_call x3, Pallas kernels, pool_more(): pl.pallas_call(functools.partial(more_kernel, ks, block, towers), in_spec...  4.53 us
    pallas_call x1, Pallas kernels, pool_first(): pl.pallas_call(functools.partial(first_kernel, ks, block, towers), in_spe...  2.49 us
    pallas_call x1, Pallas kernels, tower_out(): pl.pallas_call(functools.partial(tower_kernel, ks, late, towers), in_spec...  1.83 us
    pallas_call x4, Pallas kernels, low_part(): pl.pallas_call(functools.partial(low_kernel, ks, len(held)), in_specs=[VM...  1.01 us
    pallas_call x1, Pallas kernels, gram_pairs(): pl.pallas_call(gram_kernel, in_specs=[VMEM] * towers, out_specs=VMEM, out...  0.87 us
  transfers between devices with their start and end apart: 10, of which 5 were waited for; matrix products, arithmetic and copies ran while one was open for 0% of the time, Pallas kernels for 15%

profile of v7, /device:TPU:0, one launch (start us, length us, event | category | flops | bytes accessed | tf_op | source)
XLA Modules:
  0.0 36.0 jit_solution(725011583495158956)
XLA Ops:
  0.0 2.5 %pool_first.1 = (s32[4,4,1024]{2,1,0:T(4,128)S(1)}, s32[4,1024]{1,0:T(4,128)S(1)}, bf16[4,1024,128]{2,1,0:T(8,128)(2,1)S(1)}, bf16[128,512]{1,0:T(8,128)(2,1)S(1)}) custom-call(s32[4,4,1024]{2,1,0:T(4,128)} %bitcast.23, s32[4,1024]{1,0:T(4,128)} %bitcast.24, bf16[4,1024,128]{2,1,0:T(8,128)(2,1)} %bitcast.22), custom_call_target="tpu_custom_call" | custom-call | tf_op jit(solution)/shard_map/pool_first/pallas_call | solution.py:111
  2.5 4.1 %collective-permute-start.3 = (bf16[128,512]{1,0:T(8,128)(2,1)S(1)}, bf16[128,512]{1,0:T(8,128)(2,1)S(1)}, u32[]{:S(2)}, u32[]{:S(2)}) collective-permute-start(bf16[128,512]{1,0:T(8,128)(2,1)S(1)} %get-tuple-element.23.after_ref), channel_id=1, source_target_pairs={{0,4},{1,5},{2,6},{3,7},{4,0},{5,1},{6,2},{7,3},{8,12},{9,13},{10,... | collective-permute-start | bytes 393224 | tf_op jit(solution)/shard_map/ppermute | solution.py:244
  6.6 1.9 %pool_more.3 = (bf16[128,512]{1,0:T(8,128)(2,1)S(1)}, bf16[128,512]{1,0:T(8,128)(2,1)S(1)}, bf16[128,512]{1,0:T(8,128)(2,1)S(1)}) custom-call(s32[4,4,1024]{2,1,0:T(4,128)S(1)} %get-tuple-element.20.ids_ref, s32[4,1024]{1,0:T(4,128)S(1)} %get-tuple-element.21.len_ref, bf16[4,1024,128]{2,1,0:T(8,128)(2,1)S(1)} %get-tuple-element.22.tab_ref, ...), custom_call_target="tpu_custom_call" | custom-call | flops 2000000000 | tf_op jit(solution)/shard_map/pool_more/pallas_call | solution.py:129
  8.5 1.3 %collective-permute-start = (bf16[128,512]{1,0:T(8,128)(2,1)S(1)}, bf16[128,512]{1,0:T(8,128)(2,1)S(1)}, u32[]{:S(2)}, u32[]{:S(2)}) collective-permute-start(bf16[128,512]{1,0:T(8,128)(2,1)S(1)} %get-tuple-element.24), channel_id=1, source_target_pairs={{0,5},{1,4},{2,7},{3,6},{4,1},{5,0},{6,3},{7,2},{8,13},{9,12},{10,... | collective-permute-start | bytes 393224 | tf_op jit(solution)/shard_map/ppermute | solution.py:244
  9.8 0.3 collective-permute-start.2
  10.1 1.3 %pool_more.4 = (bf16[128,512]{1,0:T(8,128)(2,1)S(1)}, bf16[128,512]{1,0:T(8,128)(2,1)S(1)}) custom-call(s32[4,4,1024]{2,1,0:T(4,128)S(1)} %get-tuple-element.20.ids_ref, s32[4,1024]{1,0:T(4,128)S(1)} %get-tuple-element.21.len_ref, bf16[4,1024,128]{2,1,0:T(8,128)(2,1)S(1)} %get-tuple-element.22.tab_ref, ...), custom_call_target="tpu_custom_call" | custom-call | flops 2000000000 | tf_op jit(solution)/shard_map/pool_more/pallas_call | solution.py:129
  11.5 0.0 copy-start
  11.5 2.8 %collective-permute-start.1 = (bf16[128,512]{1,0:T(8,128)(2,1)S(1)}, bf16[128,512]{1,0:T(8,128)(2,1)S(1)}, u32[]{:S(2)}, u32[]{:S(2)}) collective-permute-start(bf16[128,512]{1,0:T(8,128)(2,1)S(1)} %get-tuple-element.26.after_ref), channel_id=1, source_target_pairs={{0,3},{1,2},{2,1},{3,0},{4,7},{5,6},{6,5},{7,4},{8,11},{9,10},{10,... | collective-permute-start | bytes 393224 | tf_op jit(solution)/shard_map/ppermute | solution.py:244
  14.3 1.3 %pool_more.5 = (bf16[128,512]{1,0:T(8,128)(2,1)S(1)}, bf16[128,512]{1,0:T(8,128)(2,1)S(1)}) custom-call(s32[4,4,1024]{2,1,0:T(4,128)S(1)} %get-tuple-element.20.ids_ref, s32[4,1024]{1,0:T(4,128)S(1)} %get-tuple-element.21.len_ref, bf16[4,1024,128]{2,1,0:T(8,128)(2,1)S(1)} %get-tuple-element.22.tab_ref, bf16[128,512]{1,0:T(8,128)(2,1)S(1)} %get-tuple-element.26.after_ref), custom_call_target="tpu_custom_call" | custom-call | flops 2000000000 | tf_op jit(solution)/shard_map/pool_more/pallas_call | solution.py:129
  15.6 2.5 %collective-permute-start.5 = (bf16[128,512]{1,0:T(8,128)(2,1)S(1)}, bf16[128,512]{1,0:T(8,128)(2,1)S(1)}, u32[]{:S(2)}, u32[]{:S(2)}) collective-permute-start(bf16[128,512]{1,0:T(8,128)(2,1)S(1)} %get-tuple-element.29), channel_id=1, source_target_pairs={{0,7},{1,6},{2,5},{3,4},{4,3},{5,2},{6,1},{7,0},{8,15},{9,14},{10,... | collective-permute-start | bytes 393224 | tf_op jit(solution)/shard_map/ppermute | solution.py:244
  18.1 0.0 collective-permute-done.3.rest_0_
  18.1 1.4 %collective-permute-start.6 = (bf16[128,512]{1,0:T(8,128)(2,1)S(1)}, bf16[128,512]{1,0:T(8,128)(2,1)S(1)}, u32[]{:S(2)}, u32[]{:S(2)}) collective-permute-start(bf16[128,512]{1,0:T(8,128)(2,1)S(1)} %get-tuple-element.30), channel_id=1, source_target_pairs={{0,6},{1,7},{2,4},{3,5},{4,2},{5,3},{6,0},{7,1},{8,14},{9,15},{10,... | collective-permute-start | bytes 393224 | tf_op jit(solution)/shard_map/ppermute | solution.py:244
  19.5 0.0 copy-done
  19.5 0.0 copy-start.1
  19.5 0.0 copy-start.2
  19.5 0.2 low_part.4.rest_1_
  19.7 0.0 collective-permute-done.2.rest_0_.rest_1_
  19.7 3.1 %collective-permute-start.4 = (bf16[128,512]{1,0:T(8,128)(2,1)S(1)}, bf16[128,512]{1,0:T(8,128)(2,1)S(1)}, u32[]{:S(2)}, u32[]{:S(2)}) collective-permute-start(bf16[128,512]{1,0:T(8,128)(2,1)S(1)} %get-tuple-element.28), channel_id=1, source_target_pairs={{0,2},{1,3},{2,0},{3,1},{4,6},{5,7},{6,4},{7,5},{8,10},{9,11},{10,... | collective-permute-start | bytes 393224 | tf_op jit(solution)/shard_map/ppermute | solution.py:244
  22.8 0.0 copy-done.1
  22.8 0.1 copy-done.2
  22.9 0.2 low_part.5.rest_2_
  23.2 0.0 collective-permute-done.1.rest_1_.rest_3_
  23.2 0.3 low_part.6.rest_1_
  23.5 0.0 copy-start.3
  23.5 0.0 copy-start.4
  23.5 1.5 %collective-permute-done.rest_0_.rest_4_ = bf16[128,512]{1,0:T(8,128)(2,1)S(1)} collective-permute-done((bf16[128,512]{1,0:T(8,128)(2,1)S(1)}, bf16[128,512]{1,0:T(8,128)(2,1)S(1)}, u32[]{:S(2)}, u32[]{:S(2)}) %collective-permute-start) | collective-permute-done | bytes 131104 | tf_op jit(solution)/shard_map/ppermute | solution.py:244
  25.0 0.2 low_part.7.low_ref
  25.3 0.0 collective-permute-done.5.rest_6_
  25.3 1.4 %collective-permute-done.6.rest_7_ = bf16[128,512]{1,0:T(8,128)(2,1)S(1)} collective-permute-done((bf16[128,512]{1,0:T(8,128)(2,1)S(1)}, bf16[128,512]{1,0:T(8,128)(2,1)S(1)}, u32[]{:S(2)}, u32[]{:S(2)}) %collective-permute-start.6) | collective-permute-done | bytes 131104 | tf_op jit(solution)/shard_map/ppermute | solution.py:244
  26.7 1.4 %collective-permute-done.4.rest_5_ = bf16[128,512]{1,0:T(8,128)(2,1)S(1)} collective-permute-done((bf16[128,512]{1,0:T(8,128)(2,1)S(1)}, bf16[128,512]{1,0:T(8,128)(2,1)S(1)}, u32[]{:S(2)}, u32[]{:S(2)}) %collective-permute-start.4) | collective-permute-done | bytes 131104 | tf_op jit(solution)/shard_map/ppermute | solution.py:244
  28.1 0.0 copy-done.3
  28.1 0.0 copy-done.4
  28.1 1.8 %tower_out.1 = (bf16[32,512]{1,0:T(8,128)(2,1)S(1)}, bf16[32,512]{1,0:T(8,128)(2,1)S(1)}, bf16[32,512]{1,0:T(8,128)(2,1)S(1)}, bf16[32,512]{1,0:T(8,128)(2,1)S(1)}) custom-call(f32[128,512]{1,0:T(8,128)S(1)} %low_part.7.low_ref, bf16[4096,512]{1,0:T(8,128)(2,1)S(1)} %bitcast.16, bf16[512,4096]{1,0:T(8,128)(2,1)S(1)} %bitcast.18, f32[1,4096]{1,0:T(1,128)S(1)} %bitcast.21, ...), custom_call_target="tpu_custom_call" | custom-call | flops 1073741824 | tf_op jit(solution)/shard_map/tower_out/pallas_call | solution.py:192
  30.0 1.3 %collective-permute-start.7 = (bf16[32,512]{1,0:T(8,128)(2,1)S(1)}, bf16[32,512]{1,0:T(8,128)(2,1)S(1)}, u32[]{:S(2)}, u32[]{:S(2)}) collective-permute-start(bf16[32,512]{1,0:T(8,128)(2,1)S(1)} %get-tuple-element.31), channel_id=1, source_target_pairs={{0,24},{8,16},{16,8},{24,0},{1,25},{9,17},{17,9},{25,1},{2,26},{10... | collective-permute-start | bytes 98312 | tf_op jit(solution)/shard_map/ppermute | solution.py:244
  31.2 0.5 %collective-permute-start.8 = (bf16[32,512]{1,0:T(8,128)(2,1)S(1)}, bf16[32,512]{1,0:T(8,128)(2,1)S(1)}, u32[]{:S(2)}, u32[]{:S(2)}) collective-permute-start(bf16[32,512]{1,0:T(8,128)(2,1)S(1)} %get-tuple-element.32), channel_id=1, source_target_pairs={{0,16},{8,24},{16,0},{24,8},{1,17},{9,25},{17,1},{25,9},{2,18},{10... | collective-permute-start | bytes 98312 | tf_op jit(solution)/shard_map/ppermute | solution.py:244
  31.7 0.2 collective-permute-start.9
  31.9 1.7 %collective-permute-done.7.rest_0_ = bf16[32,512]{1,0:T(8,128)(2,1)S(1)} collective-permute-done((bf16[32,512]{1,0:T(8,128)(2,1)S(1)}, bf16[32,512]{1,0:T(8,128)(2,1)S(1)}, u32[]{:S(2)}, u32[]{:S(2)}) %collective-permute-start.7) | collective-permute-done | bytes 32800 | tf_op jit(solution)/shard_map/ppermute | solution.py:244
  33.6 1.6 %collective-permute-done.8.rest_1_ = bf16[32,512]{1,0:T(8,128)(2,1)S(1)} collective-permute-done((bf16[32,512]{1,0:T(8,128)(2,1)S(1)}, bf16[32,512]{1,0:T(8,128)(2,1)S(1)}, u32[]{:S(2)}, u32[]{:S(2)}) %collective-permute-start.8) | collective-permute-done | bytes 32800 | tf_op jit(solution)/shard_map/ppermute | solution.py:244
  35.1 0.0 collective-permute-done.9.rest_2_
  35.1 0.9 %gram_pairs.1 = f32[6,32]{1,0:T(8,128)} custom-call(bf16[32,512]{1,0:T(8,128)(2,1)S(1)} %collective-permute-done.7.rest_0_, bf16[32,512]{1,0:T(8,128)(2,1)S(1)} %collective-permute-done.8.rest_1_, bf16[32,512]{1,0:T(8,128)(2,1)S(1)} %collective-permute-done.9.rest_2_, bf16[32,512]{1,0:T(8,128)(2,1)S(1)} %get-tuple-element.34.rest_3_), custom_call_target="tpu_custom_call" | custom-call | tf_op jit(solution)/shard_map/gram_pairs/pallas_call | solution.py:231
Async XLA Ops:
  2.5 15.6 %collective-permute-start.3 = (bf16[128,512]{1,0:T(8,128)(2,1)S(1)}, bf16[128,512]{1,0:T(8,128)(2,1)S(1)}, u32[]{:S(2)}, u32[]{:S(2)}) collective-permute-start(bf16[128,512]{1,0:T(8,128)(2,1)S(1)} %get-tuple-element.23.after_ref), channel_id=1, source_target_pairs={{0,4},{1,5},{2,6},{3,7},{4,0},{5,1},{6,2},{7,3},{8,12},{9,13},{10,... | collective-permute-start | bytes 393224 | tf_op jit(solution)/shard_map/ppermute | solution.py:244
  8.5 16.5 %collective-permute-start = (bf16[128,512]{1,0:T(8,128)(2,1)S(1)}, bf16[128,512]{1,0:T(8,128)(2,1)S(1)}, u32[]{:S(2)}, u32[]{:S(2)}) collective-permute-start(bf16[128,512]{1,0:T(8,128)(2,1)S(1)} %get-tuple-element.24), channel_id=1, source_target_pairs={{0,5},{1,4},{2,7},{3,6},{4,1},{5,0},{6,3},{7,2},{8,13},{9,12},{10,... | collective-permute-start | bytes 393224 | tf_op jit(solution)/shard_map/ppermute | solution.py:244
  9.8 9.9 %collective-permute-start.2 = (bf16[128,512]{1,0:T(8,128)(2,1)S(1)}, bf16[128,512]{1,0:T(8,128)(2,1)S(1)}, u32[]{:S(2)}, u32[]{:S(2)}) collective-permute-start(bf16[128,512]{1,0:T(8,128)(2,1)S(1)} %get-tuple-element.27), channel_id=1, source_target_pairs={{0,1},{1,0},{2,3},{3,2},{4,5},{5,4},{6,7},{7,6},{8,9},{9,8},{10,11... | collective-permute-start | bytes 393224 | tf_op jit(solution)/shard_map/ppermute | solution.py:244
  11.5 8.0 %copy-start = (bf16[1,1,4096,512]{3,2,1,0:T(8,128)(2,1)S(1)}, bf16[1,1,4096,512]{3,2,1,0:T(8,128)(2,1)}, u32[]{:S(2)}) copy-start(bf16[1,1,4096,512]{3,2,1,0:T(8,128)(2,1)} %param.11) | copy-start | bytes 12582916
  11.5 11.7 %collective-permute-start.1 = (bf16[128,512]{1,0:T(8,128)(2,1)S(1)}, bf16[128,512]{1,0:T(8,128)(2,1)S(1)}, u32[]{:S(2)}, u32[]{:S(2)}) collective-permute-start(bf16[128,512]{1,0:T(8,128)(2,1)S(1)} %get-tuple-element.26.after_ref), channel_id=1, source_target_pairs={{0,3},{1,2},{2,1},{3,0},{4,7},{5,6},{6,5},{7,4},{8,11},{9,10},{10,... | collective-permute-start | bytes 393224 | tf_op jit(solution)/shard_map/ppermute | solution.py:244
  15.6 9.7 %collective-permute-start.5 = (bf16[128,512]{1,0:T(8,128)(2,1)S(1)}, bf16[128,512]{1,0:T(8,128)(2,1)S(1)}, u32[]{:S(2)}, u32[]{:S(2)}) collective-permute-start(bf16[128,512]{1,0:T(8,128)(2,1)S(1)} %get-tuple-element.29), channel_id=1, source_target_pairs={{0,7},{1,6},{2,5},{3,4},{4,3},{5,2},{6,1},{7,0},{8,15},{9,14},{10,... | collective-permute-start | bytes 393224 | tf_op jit(solution)/shard_map/ppermute | solution.py:244
  18.1 8.6 %collective-permute-start.6 = (bf16[128,512]{1,0:T(8,128)(2,1)S(1)}, bf16[128,512]{1,0:T(8,128)(2,1)S(1)}, u32[]{:S(2)}, u32[]{:S(2)}) collective-permute-start(bf16[128,512]{1,0:T(8,128)(2,1)S(1)} %get-tuple-element.30), channel_id=1, source_target_pairs={{0,6},{1,7},{2,4},{3,5},{4,2},{5,3},{6,0},{7,1},{8,14},{9,15},{10,... | collective-permute-start | bytes 393224 | tf_op jit(solution)/shard_map/ppermute | solution.py:244
  19.5 3.3 %copy-start.1 = (bf16[1,1,512,4096]{3,2,1,0:T(8,128)(2,1)S(1)}, bf16[1,1,512,4096]{3,2,1,0:T(8,128)(2,1)}, u32[]{:S(2)}) copy-start(bf16[1,1,512,4096]{3,2,1,0:T(8,128)(2,1)} %param.12) | copy-start | bytes 12582916
  19.5 3.5 %copy-start.2 = (bf16[1,4096,512]{2,1,0:T(8,128)(2,1)S(1)}, bf16[1,4096,512]{2,1,0:T(8,128)(2,1)}, u32[]{:S(2)}) copy-start(bf16[1,4096,512]{2,1,0:T(8,128)(2,1)} %param.14) | copy-start | bytes 12582916
  19.7 8.4 %collective-permute-start.4 = (bf16[128,512]{1,0:T(8,128)(2,1)S(1)}, bf16[128,512]{1,0:T(8,128)(2,1)S(1)}, u32[]{:S(2)}, u32[]{:S(2)}) collective-permute-start(bf16[128,512]{1,0:T(8,128)(2,1)S(1)} %get-tuple-element.28), channel_id=1, source_target_pairs={{0,2},{1,3},{2,0},{3,1},{4,6},{5,7},{6,4},{7,5},{8,10},{9,11},{10,... | collective-permute-start | bytes 393224 | tf_op jit(solution)/shard_map/ppermute | solution.py:244
  23.5 4.6 %copy-start.3 = (f32[1,1,4096]{2,1,0:T(1,128)S(1)}, f32[1,1,4096]{2,1,0:T(1,128)}, u32[]{:S(2)}) copy-start(f32[1,1,4096]{2,1,0:T(1,128)} %param.13) | copy-start | bytes 49156
  23.5 4.6 %copy-start.4 = (f32[1,512]{1,0:T(1,128)S(1)}, f32[1,512]{1,0:T(1,128)}, u32[]{:S(2)}) copy-start(f32[1,512]{1,0:T(1,128)} %pb_ref.1) | copy-start | bytes 6148
  30.0 3.6 %collective-permute-start.7 = (bf16[32,512]{1,0:T(8,128)(2,1)S(1)}, bf16[32,512]{1,0:T(8,128)(2,1)S(1)}, u32[]{:S(2)}, u32[]{:S(2)}) collective-permute-start(bf16[32,512]{1,0:T(8,128)(2,1)S(1)} %get-tuple-element.31), channel_id=1, source_target_pairs={{0,24},{8,16},{16,8},{24,0},{1,25},{9,17},{17,9},{25,1},{2,26},{10... | collective-permute-start | bytes 98312 | tf_op jit(solution)/shard_map/ppermute | solution.py:244
  31.2 3.9 %collective-permute-start.8 = (bf16[32,512]{1,0:T(8,128)(2,1)S(1)}, bf16[32,512]{1,0:T(8,128)(2,1)S(1)}, u32[]{:S(2)}, u32[]{:S(2)}) collective-permute-start(bf16[32,512]{1,0:T(8,128)(2,1)S(1)} %get-tuple-element.32), channel_id=1, source_target_pairs={{0,16},{8,24},{16,0},{24,8},{1,17},{9,25},{17,1},{25,9},{2,18},{10... | collective-permute-start | bytes 98312 | tf_op jit(solution)/shard_map/ppermute | solution.py:244
  31.7 3.4 %collective-permute-start.9 = (bf16[32,512]{1,0:T(8,128)(2,1)S(1)}, bf16[32,512]{1,0:T(8,128)(2,1)S(1)}, u32[]{:S(2)}, u32[]{:S(2)}) collective-permute-start(bf16[32,512]{1,0:T(8,128)(2,1)S(1)} %get-tuple-element.33), channel_id=1, source_target_pairs={{0,8},{8,0},{16,24},{24,16},{1,9},{9,1},{17,25},{25,17},{2,10},{10... | collective-permute-start | bytes 98312 | tf_op jit(solution)/shard_map/ppermute | solution.py:244

commit v8 on v6

--- a/solution.py
+++ b/solution.py
@@ -46,15 +46,23 @@
 
 
 def pool_rows(columns, f, slots, table):
-    rows, table_rows = columns.shape[0], table.shape[0]
-    place = lax.broadcasted_iota(jnp.int16, (rows, table_rows), 1)
-    counts = jnp.zeros((rows, table_rows), jnp.bfloat16)
-    for p in range(slots):
-        c = 2 * slots * f + p
-        own = columns[:, c : c + 1].astype(jnp.int32).astype(jnp.int16)
-        times = columns[:, c + slots : c + slots + 1].astype(jnp.bfloat16)
-        counts = jnp.where(place == own, times, counts)
-    return jnp.dot(counts, table, preferred_element_type=jnp.float32).astype(jnp.bfloat16)
+    blocks = []
+    for first in range(0, columns.shape[0], LANES):
+        own = columns[first : first + LANES, 2 * slots * f : 2 * slots * (f + 1)]
+        ids = own[:, :slots].astype(jnp.int32).astype(jnp.int16)
+        times = own[:, slots:].astype(jnp.bfloat16)
+        total = None
+        for start in range(0, table.shape[0], SPLIT):
+            place = lax.broadcasted_iota(jnp.int16, (LANES, SPLIT), 1) + jnp.int16(start)
+            counts = jnp.zeros((LANES, SPLIT), jnp.bfloat16)
+            for p in range(slots):
+                counts = jnp.where(place == ids[:, p : p + 1], times[:, p : p + 1], counts)
+            part = jnp.dot(
+                counts, table[start : start + SPLIT], preferred_element_type=jnp.float32
+            )
+            total = part if total is None else total + part
+        blocks.append(total.astype(jnp.bfloat16))
+    return jnp.concatenate(blocks, axis=0) if len(blocks) > 1 else blocks[0]
 
 
 def pool_dests(group, dests, block, towers, ids_ref, len_ref, tables, outs, ready):

time: 36.4 us -> 36.4 us (level)
  no operation moved by 1% of the time
where the time goes in v8:
time: 36.4 us; the launch traced here: 36 us
  starting transfers between devices  17.4 us (48%)
  Pallas kernels  10.5 us (29%)
  waiting for transfers between devices  7.77 us (21%)
    ppermute x10, starting transfers between devices, swap(): return lax.ppermute(x, axis, [(i, i ^ k) for i in range(size)])  17.4 us
    ppermute x10, waiting for transfers between devices, swap(): return lax.ppermute(x, axis, [(i, i ^ k) for i in range(size)])  7.77 us
    pallas_call x3, Pallas kernels, pool_more(): pl.pallas_call(functools.partial(more_kernel, ks, block, towers), in_spec...  4.51 us
    pallas_call x1, Pallas kernels, pool_first(): pl.pallas_call(functools.partial(first_kernel, ks, block, towers), in_spe...  2.49 us
    pallas_call x1, Pallas kernels, tower_out(): pl.pallas_call(functools.partial(tower_kernel, ks, late, towers), in_spec...  1.83 us
    pallas_call x1, Pallas kernels, gram_pairs(): pl.pallas_call(gram_kernel, in_specs=[VMEM] * towers, out_specs=VMEM, out...  0.87 us
    pallas_call x3, Pallas kernels, low_part(): pl.pallas_call(functools.partial(low_kernel, ks, len(held)), in_specs=[VM...  0.84 us
  transfers between devices with their start and end apart: 10, of which 5 were waited for; matrix products, arithmetic and copies ran while one was open for 0% of the time, Pallas kernels for 15%

profile of v8, /device:TPU:0, one launch (start us, length us, event | category | flops | bytes accessed | tf_op | source)
XLA Modules:
  0.0 36.0 jit_solution(15958705577503390418)
XLA Ops:
  0.0 2.5 %pool_first.1 = (s32[4,4,1024]{2,1,0:T(4,128)S(1)}, s32[4,1024]{1,0:T(4,128)S(1)}, bf16[4,1024,128]{2,1,0:T(8,128)(2,1)S(1)}, bf16[128,512]{1,0:T(8,128)(2,1)S(1)}) custom-call(s32[4,4,1024]{2,1,0:T(4,128)} %bitcast.22, s32[4,1024]{1,0:T(4,128)} %bitcast.23, bf16[4,1024,128]{2,1,0:T(8,128)(2,1)} %bitcast.21), custom_call_target="tpu_custom_call" | custom-call | tf_op jit(solution)/shard_map/pool_first/pallas_call | solution.py:119
  2.5 4.1 %collective-permute-start.3 = (bf16[128,512]{1,0:T(8,128)(2,1)S(1)}, bf16[128,512]{1,0:T(8,128)(2,1)S(1)}, u32[]{:S(2)}, u32[]{:S(2)}) collective-permute-start(bf16[128,512]{1,0:T(8,128)(2,1)S(1)} %get-tuple-element.23.after_ref), channel_id=1, source_target_pairs={{0,4},{1,5},{2,6},{3,7},{4,0},{5,1},{6,2},{7,3},{8,12},{9,13},{10,... | collective-permute-start | bytes 393224 | tf_op jit(solution)/shard_map/ppermute | solution.py:252
  6.6 1.9 %pool_more.3 = (bf16[128,512]{1,0:T(8,128)(2,1)S(1)}, bf16[128,512]{1,0:T(8,128)(2,1)S(1)}, bf16[128,512]{1,0:T(8,128)(2,1)S(1)}) custom-call(s32[4,4,1024]{2,1,0:T(4,128)S(1)} %get-tuple-element.20.ids_ref, s32[4,1024]{1,0:T(4,128)S(1)} %get-tuple-element.21.len_ref, bf16[4,1024,128]{2,1,0:T(8,128)(2,1)S(1)} %get-tuple-element.22.tab_ref, ...), custom_call_target="tpu_custom_call" | custom-call | flops 2000000000 | tf_op jit(solution)/shard_map/pool_more/pallas_call | solution.py:137
  8.5 1.3 %collective-permute-start = (bf16[128,512]{1,0:T(8,128)(2,1)S(1)}, bf16[128,512]{1,0:T(8,128)(2,1)S(1)}, u32[]{:S(2)}, u32[]{:S(2)}) collective-permute-start(bf16[128,512]{1,0:T(8,128)(2,1)S(1)} %get-tuple-element.24), channel_id=1, source_target_pairs={{0,5},{1,4},{2,7},{3,6},{4,1},{5,0},{6,3},{7,2},{8,13},{9,12},{10,... | collective-permute-start | bytes 393224 | tf_op jit(solution)/shard_map/ppermute | solution.py:252
  9.8 0.3 collective-permute-start.2
  10.2 1.3 %pool_more.4 = (bf16[128,512]{1,0:T(8,128)(2,1)S(1)}, bf16[128,512]{1,0:T(8,128)(2,1)S(1)}) custom-call(s32[4,4,1024]{2,1,0:T(4,128)S(1)} %get-tuple-element.20.ids_ref, s32[4,1024]{1,0:T(4,128)S(1)} %get-tuple-element.21.len_ref, bf16[4,1024,128]{2,1,0:T(8,128)(2,1)S(1)} %get-tuple-element.22.tab_ref, ...), custom_call_target="tpu_custom_call" | custom-call | flops 2000000000 | tf_op jit(solution)/shard_map/pool_more/pallas_call | solution.py:137
  11.5 0.0 copy-start
  11.5 2.8 %collective-permute-start.1 = (bf16[128,512]{1,0:T(8,128)(2,1)S(1)}, bf16[128,512]{1,0:T(8,128)(2,1)S(1)}, u32[]{:S(2)}, u32[]{:S(2)}) collective-permute-start(bf16[128,512]{1,0:T(8,128)(2,1)S(1)} %get-tuple-element.26.after_ref), channel_id=1, source_target_pairs={{0,3},{1,2},{2,1},{3,0},{4,7},{5,6},{6,5},{7,4},{8,11},{9,10},{10,... | collective-permute-start | bytes 393224 | tf_op jit(solution)/shard_map/ppermute | solution.py:252
  14.3 1.3 %pool_more.5 = (bf16[128,512]{1,0:T(8,128)(2,1)S(1)}, bf16[128,512]{1,0:T(8,128)(2,1)S(1)}) custom-call(s32[4,4,1024]{2,1,0:T(4,128)S(1)} %get-tuple-element.20.ids_ref, s32[4,1024]{1,0:T(4,128)S(1)} %get-tuple-element.21.len_ref, bf16[4,1024,128]{2,1,0:T(8,128)(2,1)S(1)} %get-tuple-element.22.tab_ref, bf16[128,512]{1,0:T(8,128)(2,1)S(1)} %get-tuple-element.26.after_ref), custom_call_target="tpu_custom_call" | custom-call | flops 2000000000 | tf_op jit(solution)/shard_map/pool_more/pallas_call | solution.py:137
  15.6 2.5 %collective-permute-start.5 = (bf16[128,512]{1,0:T(8,128)(2,1)S(1)}, bf16[128,512]{1,0:T(8,128)(2,1)S(1)}, u32[]{:S(2)}, u32[]{:S(2)}) collective-permute-start(bf16[128,512]{1,0:T(8,128)(2,1)S(1)} %get-tuple-element.29), channel_id=1, source_target_pairs={{0,7},{1,6},{2,5},{3,4},{4,3},{5,2},{6,1},{7,0},{8,15},{9,14},{10,... | collective-permute-start | bytes 393224 | tf_op jit(solution)/shard_map/ppermute | solution.py:252
  18.1 0.0 collective-permute-done.3.rest_0_
  18.1 1.4 %collective-permute-start.6 = (bf16[128,512]{1,0:T(8,128)(2,1)S(1)}, bf16[128,512]{1,0:T(8,128)(2,1)S(1)}, u32[]{:S(2)}, u32[]{:S(2)}) collective-permute-start(bf16[128,512]{1,0:T(8,128)(2,1)S(1)} %get-tuple-element.30), channel_id=1, source_target_pairs={{0,6},{1,7},{2,4},{3,5},{4,2},{5,3},{6,0},{7,1},{8,14},{9,15},{10,... | collective-permute-start | bytes 393224 | tf_op jit(solution)/shard_map/ppermute | solution.py:252
  19.5 0.0 copy-done
  19.5 0.0 copy-start.1
  19.5 0.0 copy-start.2
  19.5 0.2 low_part.3.rest_1_
  19.7 0.0 collective-permute-done.2.rest_0_.rest_1_
  19.7 3.1 %collective-permute-start.4 = (bf16[128,512]{1,0:T(8,128)(2,1)S(1)}, bf16[128,512]{1,0:T(8,128)(2,1)S(1)}, u32[]{:S(2)}, u32[]{:S(2)}) collective-permute-start(bf16[128,512]{1,0:T(8,128)(2,1)S(1)} %get-tuple-element.28), channel_id=1, source_target_pairs={{0,2},{1,3},{2,0},{3,1},{4,6},{5,7},{6,4},{7,5},{8,10},{9,11},{10,... | collective-permute-start | bytes 393224 | tf_op jit(solution)/shard_map/ppermute | solution.py:252
  22.8 0.0 copy-done.1
  22.8 0.1 copy-done.2
  22.9 0.2 low_part.4.rest_3_
  23.2 0.0 copy-start.3
  23.2 0.0 copy-start.4
  23.2 1.8 %collective-permute-done.rest_0_.rest_2_ = bf16[128,512]{1,0:T(8,128)(2,1)S(1)} collective-permute-done((bf16[128,512]{1,0:T(8,128)(2,1)S(1)}, bf16[128,512]{1,0:T(8,128)(2,1)S(1)}, u32[]{:S(2)}, u32[]{:S(2)}) %collective-permute-start) | collective-permute-done | bytes 131104 | tf_op jit(solution)/shard_map/ppermute | solution.py:252
  25.0 0.0 collective-permute-done.1.rest_2_.rest_4_
  25.0 0.4 %low_part.5.low_ref = f32[128,512]{1,0:T(8,128)S(1)} custom-call(bf16[4096,512]{1,0:T(8,128)(2,1)S(1)} %bitcast.14, bf16[128,512]{1,0:T(8,128)(2,1)S(1)} %collective-permute-done.rest_0_.rest_2_, bf16[128,512]{1,0:T(8,128)(2,1)S(1)} %get-tuple-element.25.after_ref.rest_1_.rest_3_, bf16[128,512]{1,0:T(8,128)(2,1)S(1)} %collective-permute-done.1.rest_2_.rest_4_, ...), custom_call_target="tpu_custom_call" | custom-call | flops 4000000000 | tf_op jit(solution)/shard_map/low_part/pallas_call | solution.py:160
  25.4 0.0 collective-permute-done.5.rest_6_
  25.4 1.2 %collective-permute-done.6.rest_7_ = bf16[128,512]{1,0:T(8,128)(2,1)S(1)} collective-permute-done((bf16[128,512]{1,0:T(8,128)(2,1)S(1)}, bf16[128,512]{1,0:T(8,128)(2,1)S(1)}, u32[]{:S(2)}, u32[]{:S(2)}) %collective-permute-start.6) | collective-permute-done | bytes 131104 | tf_op jit(solution)/shard_map/ppermute | solution.py:252
  26.7 1.5 %collective-permute-done.4.rest_5_ = bf16[128,512]{1,0:T(8,128)(2,1)S(1)} collective-permute-done((bf16[128,512]{1,0:T(8,128)(2,1)S(1)}, bf16[128,512]{1,0:T(8,128)(2,1)S(1)}, u32[]{:S(2)}, u32[]{:S(2)}) %collective-permute-start.4) | collective-permute-done | bytes 131104 | tf_op jit(solution)/shard_map/ppermute | solution.py:252
  28.1 0.0 copy-done.3
  28.1 0.0 copy-done.4
  28.1 1.8 %tower_out.1 = (bf16[32,512]{1,0:T(8,128)(2,1)S(1)}, bf16[32,512]{1,0:T(8,128)(2,1)S(1)}, bf16[32,512]{1,0:T(8,128)(2,1)S(1)}, bf16[32,512]{1,0:T(8,128)(2,1)S(1)}) custom-call(f32[128,512]{1,0:T(8,128)S(1)} %low_part.5.low_ref, bf16[4096,512]{1,0:T(8,128)(2,1)S(1)} %bitcast.15, bf16[512,4096]{1,0:T(8,128)(2,1)S(1)} %bitcast.17, f32[1,4096]{1,0:T(1,128)S(1)} %bitcast.20, ...), custom_call_target="tpu_custom_call" | custom-call | flops 1073741824 | tf_op jit(solution)/shard_map/tower_out/pallas_call | solution.py:200
  30.0 1.2 %collective-permute-start.7 = (bf16[32,512]{1,0:T(8,128)(2,1)S(1)}, bf16[32,512]{1,0:T(8,128)(2,1)S(1)}, u32[]{:S(2)}, u32[]{:S(2)}) collective-permute-start(bf16[32,512]{1,0:T(8,128)(2,1)S(1)} %get-tuple-element.31), channel_id=1, source_target_pairs={{0,24},{8,16},{16,8},{24,0},{1,25},{9,17},{17,9},{25,1},{2,26},{10... | collective-permute-start | bytes 98312 | tf_op jit(solution)/shard_map/ppermute | solution.py:252
  31.2 0.5 %collective-permute-start.8 = (bf16[32,512]{1,0:T(8,128)(2,1)S(1)}, bf16[32,512]{1,0:T(8,128)(2,1)S(1)}, u32[]{:S(2)}, u32[]{:S(2)}) collective-permute-start(bf16[32,512]{1,0:T(8,128)(2,1)S(1)} %get-tuple-element.32), channel_id=1, source_target_pairs={{0,16},{8,24},{16,0},{24,8},{1,17},{9,25},{17,1},{25,9},{2,18},{10... | collective-permute-start | bytes 98312 | tf_op jit(solution)/shard_map/ppermute | solution.py:252
  31.7 0.2 collective-permute-start.9
  31.9 1.7 %collective-permute-done.7.rest_0_ = bf16[32,512]{1,0:T(8,128)(2,1)S(1)} collective-permute-done((bf16[32,512]{1,0:T(8,128)(2,1)S(1)}, bf16[32,512]{1,0:T(8,128)(2,1)S(1)}, u32[]{:S(2)}, u32[]{:S(2)}) %collective-permute-start.7) | collective-permute-done | bytes 32800 | tf_op jit(solution)/shard_map/ppermute | solution.py:252
  33.6 1.5 %collective-permute-done.8.rest_1_ = bf16[32,512]{1,0:T(8,128)(2,1)S(1)} collective-permute-done((bf16[32,512]{1,0:T(8,128)(2,1)S(1)}, bf16[32,512]{1,0:T(8,128)(2,1)S(1)}, u32[]{:S(2)}, u32[]{:S(2)}) %collective-permute-start.8) | collective-permute-done | bytes 32800 | tf_op jit(solution)/shard_map/ppermute | solution.py:252
  35.1 0.0 collective-permute-done.9.rest_2_
  35.1 0.9 %gram_pairs.1 = f32[6,32]{1,0:T(8,128)} custom-call(bf16[32,512]{1,0:T(8,128)(2,1)S(1)} %collective-permute-done.7.rest_0_, bf16[32,512]{1,0:T(8,128)(2,1)S(1)} %collective-permute-done.8.rest_1_, bf16[32,512]{1,0:T(8,128)(2,1)S(1)} %collective-permute-done.9.rest_2_, bf16[32,512]{1,0:T(8,128)(2,1)S(1)} %get-tuple-element.34.rest_3_), custom_call_target="tpu_custom_call" | custom-call | tf_op jit(solution)/shard_map/gram_pairs/pallas_call | solution.py:239
Async XLA Ops:
  2.5 15.6 %collective-permute-start.3 = (bf16[128,512]{1,0:T(8,128)(2,1)S(1)}, bf16[128,512]{1,0:T(8,128)(2,1)S(1)}, u32[]{:S(2)}, u32[]{:S(2)}) collective-permute-start(bf16[128,512]{1,0:T(8,128)(2,1)S(1)} %get-tuple-element.23.after_ref), channel_id=1, source_target_pairs={{0,4},{1,5},{2,6},{3,7},{4,0},{5,1},{6,2},{7,3},{8,12},{9,13},{10,... | collective-permute-start | bytes 393224 | tf_op jit(solution)/shard_map/ppermute | solution.py:252
  8.5 16.5 %collective-permute-start = (bf16[128,512]{1,0:T(8,128)(2,1)S(1)}, bf16[128,512]{1,0:T(8,128)(2,1)S(1)}, u32[]{:S(2)}, u32[]{:S(2)}) collective-permute-start(bf16[128,512]{1,0:T(8,128)(2,1)S(1)} %get-tuple-element.24), channel_id=1, source_target_pairs={{0,5},{1,4},{2,7},{3,6},{4,1},{5,0},{6,3},{7,2},{8,13},{9,12},{10,... | collective-permute-start | bytes 393224 | tf_op jit(solution)/shard_map/ppermute | solution.py:252
  9.8 9.8 %collective-permute-start.2 = (bf16[128,512]{1,0:T(8,128)(2,1)S(1)}, bf16[128,512]{1,0:T(8,128)(2,1)S(1)}, u32[]{:S(2)}, u32[]{:S(2)}) collective-permute-start(bf16[128,512]{1,0:T(8,128)(2,1)S(1)} %get-tuple-element.27), channel_id=1, source_target_pairs={{0,1},{1,0},{2,3},{3,2},{4,5},{5,4},{6,7},{7,6},{8,9},{9,8},{10,11... | collective-permute-start | bytes 393224 | tf_op jit(solution)/shard_map/ppermute | solution.py:252
  11.5 8.0 %copy-start = (bf16[1,1,4096,512]{3,2,1,0:T(8,128)(2,1)S(1)}, bf16[1,1,4096,512]{3,2,1,0:T(8,128)(2,1)}, u32[]{:S(2)}) copy-start(bf16[1,1,4096,512]{3,2,1,0:T(8,128)(2,1)} %param.11) | copy-start | bytes 12582916
  11.5 13.6 %collective-permute-start.1 = (bf16[128,512]{1,0:T(8,128)(2,1)S(1)}, bf16[128,512]{1,0:T(8,128)(2,1)S(1)}, u32[]{:S(2)}, u32[]{:S(2)}) collective-permute-start(bf16[128,512]{1,0:T(8,128)(2,1)S(1)} %get-tuple-element.26.after_ref), channel_id=1, source_target_pairs={{0,3},{1,2},{2,1},{3,0},{4,7},{5,6},{6,5},{7,4},{8,11},{9,10},{10,... | collective-permute-start | bytes 393224 | tf_op jit(solution)/shard_map/ppermute | solution.py:252
  15.6 9.8 %collective-permute-start.5 = (bf16[128,512]{1,0:T(8,128)(2,1)S(1)}, bf16[128,512]{1,0:T(8,128)(2,1)S(1)}, u32[]{:S(2)}, u32[]{:S(2)}) collective-permute-start(bf16[128,512]{1,0:T(8,128)(2,1)S(1)} %get-tuple-element.29), channel_id=1, source_target_pairs={{0,7},{1,6},{2,5},{3,4},{4,3},{5,2},{6,1},{7,0},{8,15},{9,14},{10,... | collective-permute-start | bytes 393224 | tf_op jit(solution)/shard_map/ppermute | solution.py:252
  18.1 8.6 %collective-permute-start.6 = (bf16[128,512]{1,0:T(8,128)(2,1)S(1)}, bf16[128,512]{1,0:T(8,128)(2,1)S(1)}, u32[]{:S(2)}, u32[]{:S(2)}) collective-permute-start(bf16[128,512]{1,0:T(8,128)(2,1)S(1)} %get-tuple-element.30), channel_id=1, source_target_pairs={{0,6},{1,7},{2,4},{3,5},{4,2},{5,3},{6,0},{7,1},{8,14},{9,15},{10,... | collective-permute-start | bytes 393224 | tf_op jit(solution)/shard_map/ppermute | solution.py:252
  19.5 3.3 %copy-start.1 = (bf16[1,1,512,4096]{3,2,1,0:T(8,128)(2,1)S(1)}, bf16[1,1,512,4096]{3,2,1,0:T(8,128)(2,1)}, u32[]{:S(2)}) copy-start(bf16[1,1,512,4096]{3,2,1,0:T(8,128)(2,1)} %param.12) | copy-start | bytes 12582916
  19.5 3.5 %copy-start.2 = (bf16[1,4096,512]{2,1,0:T(8,128)(2,1)S(1)}, bf16[1,4096,512]{2,1,0:T(8,128)(2,1)}, u32[]{:S(2)}) copy-start(bf16[1,4096,512]{2,1,0:T(8,128)(2,1)} %param.14) | copy-start | bytes 12582916
  19.7 8.4 %collective-permute-start.4 = (bf16[128,512]{1,0:T(8,128)(2,1)S(1)}, bf16[128,512]{1,0:T(8,128)(2,1)S(1)}, u32[]{:S(2)}, u32[]{:S(2)}) collective-permute-start(bf16[128,512]{1,0:T(8,128)(2,1)S(1)} %get-tuple-element.28), channel_id=1, source_target_pairs={{0,2},{1,3},{2,0},{3,1},{4,6},{5,7},{6,4},{7,5},{8,10},{9,11},{10,... | collective-permute-start | bytes 393224 | tf_op jit(solution)/shard_map/ppermute | solution.py:252
  23.2 5.0 %copy-start.3 = (f32[1,1,4096]{2,1,0:T(1,128)S(1)}, f32[1,1,4096]{2,1,0:T(1,128)}, u32[]{:S(2)}) copy-start(f32[1,1,4096]{2,1,0:T(1,128)} %param.13) | copy-start | bytes 49156
  23.2 5.0 %copy-start.4 = (f32[1,512]{1,0:T(1,128)S(1)}, f32[1,512]{1,0:T(1,128)}, u32[]{:S(2)}) copy-start(f32[1,512]{1,0:T(1,128)} %pb_ref.1) | copy-start | bytes 6148
  30.0 3.6 %collective-permute-start.7 = (bf16[32,512]{1,0:T(8,128)(2,1)S(1)}, bf16[32,512]{1,0:T(8,128)(2,1)S(1)}, u32[]{:S(2)}, u32[]{:S(2)}) collective-permute-start(bf16[32,512]{1,0:T(8,128)(2,1)S(1)} %get-tuple-element.31), channel_id=1, source_target_pairs={{0,24},{8,16},{16,8},{24,0},{1,25},{9,17},{17,9},{25,1},{2,26},{10... | collective-permute-start | bytes 98312 | tf_op jit(solution)/shard_map/ppermute | solution.py:252
  31.2 3.9 %collective-permute-start.8 = (bf16[32,512]{1,0:T(8,128)(2,1)S(1)}, bf16[32,512]{1,0:T(8,128)(2,1)S(1)}, u32[]{:S(2)}, u32[]{:S(2)}) collective-permute-start(bf16[32,512]{1,0:T(8,128)(2,1)S(1)} %get-tuple-element.32), channel_id=1, source_target_pairs={{0,16},{8,24},{16,0},{24,8},{1,17},{9,25},{17,1},{25,9},{2,18},{10... | collective-permute-start | bytes 98312 | tf_op jit(solution)/shard_map/ppermute | solution.py:252
  31.7 3.4 %collective-permute-start.9 = (bf16[32,512]{1,0:T(8,128)(2,1)S(1)}, bf16[32,512]{1,0:T(8,128)(2,1)S(1)}, u32[]{:S(2)}, u32[]{:S(2)}) collective-permute-start(bf16[32,512]{1,0:T(8,128)(2,1)S(1)} %get-tuple-element.33), channel_id=1, source_target_pairs={{0,8},{8,0},{16,24},{24,16},{1,9},{9,1},{17,25},{25,17},{2,10},{10... | collective-permute-start | bytes 98312 | tf_op jit(solution)/shard_map/ppermute | solution.py:252
